TPU v7x, 32 devices: a whole 2x2x4 slice. The times are simulated.
32 devices in a mesh: replica: 4 (over z), shard: 8 (over y, x, core).
Axes of the slice: x: 2, y: 2, z: 4, core: 2. Of those that a mesh axis runs over, the one named last changes fastest.
Arguments:
- tokens: bfloat16 [16, 1024, 2048], P('replica', 'shard'), may hold values from -8 to 8
- segments: int32 [16, 1024], P('replica', 'shard'), may hold values from 0 to 6, as said below
- positions: int32 [16, 1024], P('replica', 'shard'), may hold values from 0 to 2047, as said below
- cotangent: bfloat16 [16, 1024, 2048], P('replica', 'shard'), may hold values from -6 to 6
- attention_gain: bfloat16 [2048], P('shard'), may hold values from 0.5 to 1.5
- query_weight: bfloat16 [2048, 2048], P('shard'), may hold values from -6 to 6
- key_weight: bfloat16 [2048, 512], P('shard'), may hold values from -6 to 6
- value_weight: bfloat16 [2048, 512], P('shard'), may hold values from -0.125 to 0.125
- output_weight: bfloat16 [2048, 2048], P('shard'), may hold values from -1.5 to 1.5
- mlp_gain: bfloat16 [2048], P('shard'), may hold values from 0.5 to 1.5
- gate_weight: bfloat16 [2048, 8192], P('shard'), may hold values from -0.125 to 0.125
- up_weight: bfloat16 [2048, 8192], P('shard'), may hold values from -0.125 to 0.125
- down_weight: bfloat16 [8192, 2048], P('shard'), may hold values from -0.0625 to 0.0625
Outputs:
- block_output: bfloat16 [16, 1024, 2048], P('replica', 'shard')
- token_grad: float32 [16, 1024, 2048], P('replica', 'shard')
- attention_gain_grad: float32 [2048], P('shard')
- query_grad: float32 [2048, 2048], P('shard')
- key_grad: float32 [2048, 512], P('shard')
- value_grad: float32 [2048, 512], P('shard')
- output_grad: float32 [2048, 2048], P('shard')
- mlp_gain_grad: float32 [2048], P('shard')
- gate_grad: float32 [2048, 8192], P('shard')
- up_grad: float32 [2048, 8192], P('shard')
- down_grad: float32 [8192, 2048], P('shard')
Inputs may be any that keep to these rules, and one draw needn't show every extreme that they name: `segments`: ids never fall along a sequence, are 0 at its first token and rise by one at each document's first token; a document that begins and ends inside a sequence has 204 tokens or more. `positions`: a token's position within its document: it rises by one from token to token of a document and is 0 at a document's first token; a sequence's first document may have begun before the sequence.
All inputs are finite; a program needn't handle non-finite values.
Results may differ from a plain program's by a relative error of at most 0.023.
The roundings to bfloat16 on the way count: a program that leaves them out, or rounds other values in their place, can miss the bound.
Values may be sent and summed in bfloat16 or wider, within the bound.
A program may use at most 512 MiB of HBM per device.

v0:
```python
import math

import jax
import jax.numpy as jnp
from jax import lax
from jax.sharding import PartitionSpec as P

HEADS = 32
KV_HEADS = 8
HEAD_DIM = 64


epsilon = 1e-05
rope_base = 500000.0
masked_score = -1e30


def rotation(doc_positions):
    freq_index = jnp.arange(HEAD_DIM // 2, dtype=jnp.float32)
    inverse_freq = jnp.exp(freq_index * (-2.0 * math.log(rope_base) / HEAD_DIM))
    angle_all = doc_positions.astype(jnp.float32)[..., None] * inverse_freq
    return (jnp.cos(angle_all)[..., None, :], jnp.sin(angle_all)[..., None, :])


def rotate(values_in, cosine, sine_part):
    half_dim = values_in.shape[-1] // 2
    lower_half = values_in[..., :half_dim]
    upper_half = values_in[..., half_dim:]
    return jnp.concatenate(
        [
            lower_half * cosine - upper_half * sine_part,
            upper_half * cosine + lower_half * sine_part,
        ],
        -1,
    )


def outer_sum(left, right):
    return lax.dot_general(
        left, right, (((0,), (0,)), ((), ())), preferred_element_type=jnp.float32
    )


def visible(seg_rows, doc_rows, local_rows):
    first_index = lax.axis_index("shard") * local_rows
    query_at = first_index + jnp.arange(local_rows, dtype=jnp.int32)
    key_at = jnp.arange(doc_rows.shape[0], dtype=jnp.int32)
    causal = key_at[None, :] <= query_at[:, None]
    same_doc = seg_rows.astype(jnp.float32)[:, None] == doc_rows.astype(jnp.float32)[None, :]
    return (same_doc & causal)[None, None, :, :]


def score_block(grouped, all_keys, allowed):
    raw_scores = jnp.einsum(
        "qhgd,khd->hgqk", grouped, all_keys, preferred_element_type=jnp.float32
    ) * HEAD_DIM ** (-0.5)
    return jnp.where(allowed, raw_scores, masked_score)


def norm_back(grad_normed, unit_rows, scale_rows, gain_rows):
    scaled_grad = grad_normed * gain_rows
    return scale_rows * (
        scaled_grad - unit_rows * jnp.mean(scaled_grad * unit_rows, -1, keepdims=True)
    )


def body(
    tokens,
    segments,
    positions,
    cotangent,
    attention_gain,
    query_weight,
    key_weight,
    value_weight,
    output_weight,
    mlp_gain,
    gate_weight,
    up_weight,
    down_weight,
):
    groups, local_rows, model_width = tokens.shape
    all_rows = groups * local_rows
    group_share = HEADS // KV_HEADS
    ff_width = gate_weight.shape[1]
    norm_first, query_full, key_full, value_full, output_full = (
        lax.all_gather(attention_gain, "shard", axis=0, tiled=True),
        lax.all_gather(query_weight, "shard", axis=0, tiled=True),
        lax.all_gather(key_weight, "shard", axis=0, tiled=True),
        lax.all_gather(value_weight, "shard", axis=0, tiled=True),
        lax.all_gather(output_weight, "shard", axis=0, tiled=True),
    )
    norm_first = norm_first.astype(jnp.float32)
    inputs = tokens.astype(jnp.float32)
    scale_first = lax.rsqrt(jnp.mean(inputs * inputs, -1, keepdims=True) + epsilon)
    unit_first = inputs * scale_first
    normed_first = (unit_first * norm_first).astype(jnp.bfloat16)
    queries = jnp.dot(normed_first, query_full, preferred_element_type=jnp.float32).reshape(
        groups, local_rows, HEADS, HEAD_DIM
    )
    key_plain = jnp.dot(normed_first, key_full, preferred_element_type=jnp.float32).reshape(
        groups, local_rows, KV_HEADS, HEAD_DIM
    )
    value_rows = (
        jnp.dot(normed_first, value_full, preferred_element_type=jnp.float32)
        .astype(jnp.bfloat16)
        .reshape(groups, local_rows, KV_HEADS, HEAD_DIM)
    )
    cosine, sine_part = rotation(positions)
    query_turned = rotate(queries, cosine, sine_part).astype(jnp.bfloat16)
    key_turned = rotate(key_plain, cosine, sine_part).astype(jnp.bfloat16)
    doc_float = segments.astype(jnp.bfloat16)
    all_keys, all_values, all_docs = (
        lax.all_gather(key_turned, "shard", axis=1, tiled=True),
        lax.all_gather(value_rows, "shard", axis=1, tiled=True),
        lax.all_gather(doc_float, "shard", axis=1, tiled=True),
    )
    grouped = query_turned.reshape(groups, local_rows, KV_HEADS, group_share, HEAD_DIM)

    def attend_one(item):
        q_seq, k_seq, v_seq, seg_seq, doc_seq = item
        allowed = visible(seg_seq, doc_seq, local_rows)
        scores = score_block(q_seq, k_seq, allowed)
        row_top = jnp.max(scores, -1, keepdims=True)
        lifted = jnp.exp(scores - row_top)
        row_total = jnp.sum(lifted, -1, keepdims=True)
        softmax_low = (lifted / row_total).astype(jnp.bfloat16)
        attended_seq = (
            jnp.einsum("hgqk,khd->qhgd", softmax_low, v_seq, preferred_element_type=jnp.float32)
            .reshape(local_rows, HEADS * HEAD_DIM)
            .astype(jnp.bfloat16)
        )
        return (attended_seq, row_top + jnp.log(row_total))

    attended, log_norm = lax.map(attend_one, (grouped, all_keys, all_values, segments, all_docs))
    hidden = inputs + jnp.dot(attended, output_full, preferred_element_type=jnp.float32)
    norm_second, gate_full, up_full, down_full = (
        lax.all_gather(mlp_gain, "shard", axis=0, tiled=True),
        lax.all_gather(gate_weight, "shard", axis=0, tiled=True),
        lax.all_gather(up_weight, "shard", axis=0, tiled=True),
        lax.all_gather(down_weight, "shard", axis=0, tiled=True),
    )
    norm_second = norm_second.astype(jnp.float32)
    scale_second = lax.rsqrt(jnp.mean(hidden * hidden, -1, keepdims=True) + epsilon)
    unit_second = hidden * scale_second
    normed_second = (unit_second * norm_second).astype(jnp.bfloat16)
    gate_pre = jnp.dot(normed_second, gate_full, preferred_element_type=jnp.float32)
    up_pre = jnp.dot(normed_second, up_full, preferred_element_type=jnp.float32)
    sigmoid_gate = jax.nn.sigmoid(gate_pre)
    swish = gate_pre * sigmoid_gate
    mixed_low = (swish * up_pre).astype(jnp.bfloat16)
    result = hidden + jnp.dot(mixed_low, down_full, preferred_element_type=jnp.float32)
    block_out = result.astype(jnp.bfloat16)
    second_back, gate_back, up_back, down_back = (
        lax.all_gather(mlp_gain, "shard", axis=0, tiled=True),
        lax.all_gather(gate_weight, "shard", axis=0, tiled=True),
        lax.all_gather(up_weight, "shard", axis=0, tiled=True),
        lax.all_gather(down_weight, "shard", axis=0, tiled=True),
    )
    second_back = second_back.astype(jnp.float32)
    grad_out = cotangent.astype(jnp.float32)
    grad_mixed = jnp.einsum("btd,fd->btf", cotangent, down_back, preferred_element_type=jnp.float32)
    grad_gate = (
        grad_mixed * up_pre * (sigmoid_gate + gate_pre * sigmoid_gate * (1.0 - sigmoid_gate))
    ).astype(jnp.bfloat16)
    grad_up = (grad_mixed * swish).astype(jnp.bfloat16)
    grad_second = jnp.einsum(
        "btf,df->btd", grad_gate, gate_back, preferred_element_type=jnp.float32
    ) + jnp.einsum("btf,df->btd", grad_up, up_back, preferred_element_type=jnp.float32)
    second_flat = normed_second.reshape(all_rows, model_width)
    both_grads = jnp.concatenate([grad_gate, grad_up], -1).reshape(all_rows, 2 * ff_width)
    columns = second_flat
    owned_inner = lax.psum_scatter(
        outer_sum(columns, both_grads).astype(jnp.bfloat16),
        "shard",
        scatter_dimension=0,
        tiled=True,
    ).astype(jnp.float32)
    mixed_flat = mixed_low.reshape(all_rows, ff_width)
    cot_flat = cotangent.reshape(all_rows, model_width)
    columns = mixed_flat
    owned_down = lax.psum_scatter(
        outer_sum(columns, cot_flat).astype(jnp.bfloat16), "shard", scatter_dimension=0, tiled=True
    )
    second_grad = jnp.sum(grad_second * unit_second, axis=(0, 1))
    grad_hidden = grad_out + norm_back(grad_second, unit_second, scale_second, second_back)
    first_back, query_back, key_back, value_back, output_back = (
        lax.all_gather(attention_gain, "shard", axis=0, tiled=True),
        lax.all_gather(query_weight, "shard", axis=0, tiled=True),
        lax.all_gather(key_weight, "shard", axis=0, tiled=True),
        lax.all_gather(value_weight, "shard", axis=0, tiled=True),
        lax.all_gather(output_weight, "shard", axis=0, tiled=True),
    )
    first_back = first_back.astype(jnp.float32)
    grad_branch = grad_hidden.astype(jnp.bfloat16)
    output_outer = outer_sum(
        attended.reshape(all_rows, HEADS * HEAD_DIM), grad_branch.reshape(all_rows, model_width)
    )
    grad_attended = (
        jnp.einsum("btd,ed->bte", grad_branch, output_back, preferred_element_type=jnp.float32)
        .astype(jnp.bfloat16)
        .reshape(groups, local_rows, KV_HEADS, group_share, HEAD_DIM)
    )

    def back_one(item):
        q_seq, k_seq, v_seq, seg_seq, doc_seq, grad_seq, norm_seq = item
        allowed = visible(seg_seq, doc_seq, local_rows)
        recomputed = jnp.exp(score_block(q_seq, k_seq, allowed) - norm_seq)
        recomputed_low = recomputed.astype(jnp.bfloat16)
        grad_probs = jnp.einsum(
            "qhgd,khd->hgqk", grad_seq, v_seq, preferred_element_type=jnp.float32
        )
        grad_scores = (
            recomputed * (grad_probs - jnp.sum(recomputed * grad_probs, -1, keepdims=True))
        ).astype(jnp.bfloat16)
        query_part = jnp.einsum(
            "hgqk,khd->qhgd", grad_scores, k_seq, preferred_element_type=jnp.float32
        ) * HEAD_DIM ** (-0.5)
        key_part = jnp.einsum(
            "hgqk,qhgd->khd", grad_scores, q_seq, preferred_element_type=jnp.float32
        ) * HEAD_DIM ** (-0.5)
        value_part = jnp.einsum(
            "hgqk,qhgd->khd", recomputed_low, grad_seq, preferred_element_type=jnp.float32
        )
        return (query_part, key_part, value_part)

    query_terms, key_terms, value_terms = lax.map(
        back_one, (grouped, all_keys, all_values, segments, all_docs, grad_attended, log_norm)
    )
    key_summed, value_summed = (
        lax.psum_scatter(
            key_terms.astype(jnp.bfloat16), "shard", scatter_dimension=1, tiled=True
        ).astype(jnp.float32),
        lax.psum_scatter(
            value_terms.astype(jnp.bfloat16), "shard", scatter_dimension=1, tiled=True
        ).astype(jnp.float32),
    )
    grad_query = (
        rotate(query_terms.reshape(groups, local_rows, HEADS, HEAD_DIM), cosine, -sine_part)
        .reshape(groups, local_rows, HEADS * HEAD_DIM)
        .astype(jnp.bfloat16)
    )
    grad_key = (
        rotate(key_summed, cosine, -sine_part)
        .reshape(groups, local_rows, KV_HEADS * HEAD_DIM)
        .astype(jnp.bfloat16)
    )
    grad_value = value_summed.reshape(groups, local_rows, KV_HEADS * HEAD_DIM).astype(jnp.bfloat16)
    first_flat = normed_first.reshape(all_rows, model_width)
    query_outer = outer_sum(first_flat, grad_query.reshape(all_rows, HEADS * HEAD_DIM))
    key_outer = outer_sum(first_flat, grad_key.reshape(all_rows, KV_HEADS * HEAD_DIM))
    value_outer = outer_sum(first_flat, grad_value.reshape(all_rows, KV_HEADS * HEAD_DIM))
    grad_first = jnp.einsum(
        "bte,de->btd", grad_query, query_back, preferred_element_type=jnp.float32
    )
    grad_first = grad_first + jnp.einsum(
        "bte,de->btd", grad_key, key_back, preferred_element_type=jnp.float32
    )
    grad_first = grad_first + jnp.einsum(
        "bte,de->btd", grad_value, value_back, preferred_element_type=jnp.float32
    )
    first_grad = jnp.sum(grad_first * unit_first, axis=(0, 1))
    token_grad = grad_hidden + norm_back(grad_first, unit_first, scale_first, first_back)
    owned_gain, owned_query, owned_key, owned_value, owned_output, owned_second = (
        lax.psum_scatter(
            first_grad.astype(jnp.bfloat16), "shard", scatter_dimension=0, tiled=True
        ).astype(jnp.float32),
        lax.psum_scatter(
            query_outer.astype(jnp.bfloat16), "shard", scatter_dimension=0, tiled=True
        ).astype(jnp.float32),
        lax.psum_scatter(
            key_outer.astype(jnp.bfloat16), "shard", scatter_dimension=0, tiled=True
        ).astype(jnp.float32),
        lax.psum_scatter(
            value_outer.astype(jnp.bfloat16), "shard", scatter_dimension=0, tiled=True
        ).astype(jnp.float32),
        lax.psum_scatter(
            output_outer.astype(jnp.bfloat16), "shard", scatter_dimension=0, tiled=True
        ).astype(jnp.float32),
        lax.psum_scatter(
            second_grad.astype(jnp.bfloat16), "shard", scatter_dimension=0, tiled=True
        ).astype(jnp.float32),
    )
    summed = (
        lax.psum(owned_gain.astype(jnp.bfloat16), "replica").astype(jnp.float32),
        lax.psum(owned_query.astype(jnp.bfloat16), "replica").astype(jnp.float32),
        lax.psum(owned_key.astype(jnp.bfloat16), "replica").astype(jnp.float32),
        lax.psum(owned_value.astype(jnp.bfloat16), "replica").astype(jnp.float32),
        lax.psum(owned_output.astype(jnp.bfloat16), "replica").astype(jnp.float32),
        lax.psum(owned_second.astype(jnp.bfloat16), "replica").astype(jnp.float32),
        lax.psum(owned_inner[:, :ff_width].astype(jnp.bfloat16), "replica").astype(jnp.float32),
        lax.psum(owned_inner[:, ff_width:].astype(jnp.bfloat16), "replica").astype(jnp.float32),
        lax.psum(owned_down, "replica").astype(jnp.float32),
    )
    return (
        block_out,
        token_grad,
        summed[0],
        summed[1],
        summed[2],
        summed[3],
        summed[4],
        summed[5],
        summed[6],
        summed[7],
        summed[8],
    )


def solution(mesh):
    in_specs = (
        P("replica", "shard", None),
        P("replica", "shard"),
        P("replica", "shard"),
        P("replica", "shard", None),
        P("shard"),
        P("shard", None),
        P("shard", None),
        P("shard", None),
        P("shard", None),
        P("shard"),
        P("shard", None),
        P("shard", None),
        P("shard", None),
    )
    out_specs = (
        P("replica", "shard", None),
        P("replica", "shard", None),
        P("shard"),
        P("shard", None),
        P("shard", None),
        P("shard", None),
        P("shard", None),
        P("shard"),
        P("shard", None),
        P("shard", None),
        P("shard", None),
    )
    return jax.shard_map(body, mesh=mesh, in_specs=in_specs, out_specs=out_specs, check_vma=False)
```

profile of v0, /device:TPU:0, one launch (start us, length us, event | category | flops | bytes accessed | tf_op | source)
XLA Modules:
  0.0 2586.3 jit_solution(8022474154181171376)
XLA Ops:
  22.6 18.0 all-gather.12.cloned.1.call-done
  46.2 24.1 all-gather.16.cloned.1.call-done
  94.7 31.9 %all-gather.20.cloned.1.call-done = bf16[2048,2048]{1,0:T(8,128)(2,1)} async-done(((bf16[256,2048]{1,0:T(8,128)(2,1)}), bf16[2048,2048]{1,0:T(8,128)(2,1)}) %all-gather.20.cloned.1.call-update) | async-done | bytes 8388624 | tf_op jit(solution)/shard_map/all_gather | solution.py:88
  136.2 30.3 %all-gather.14.cloned.1.call-done = bf16[4,1024,8,64]{1,3,2,0:T(8,128)(2,1)} async-done(((bf16[4,128,8,64]{1,3,2,0:T(8,128)(2,1)}), bf16[4,1024,8,64]{1,3,2,0:T(8,128)(2,1)}) %all-gather.14.cloned.1.call-update) | async-done | bytes 4194320 | tf_op jit(solution)/shard_map/all_gather | solution.py:115
  166.5 39.8 %all-gather.18.cloned.1.call-done = bf16[4,1024,8,64]{1,3,2,0:T(8,128)(2,1)} async-done(((bf16[4,128,8,64]{1,3,2,0:T(8,128)(2,1)}), bf16[4,1024,8,64]{1,3,2,0:T(8,128)(2,1)}) %all-gather.18.cloned.1.call-update) | async-done | bytes 4194320 | tf_op jit(solution)/shard_map/all_gather | solution.py:114
  206.2 120.6 %while.26 = (s32[]{:T(128)}, bf16[4,128,2048]{1,2,0:T(8,128)(2,1)}, f32[4,8,4,128,1]{3,2,1,4,0:T(4,128)}, bf16[4,1024,8,64]{1,3,2,0:T(8,128)(2,1)}, s32[4,128]{1...) while((s32[]{:T(128)}, bf16[4,128,2048]{1,2,0:T(8,128)(2,1)}, ...), condition=%wide.region_4.5_spmd, body=%wide.region_1.4_spmd.sunk | while | flops 1124726016 | bytes 55195308 | solution.py:135
  337.7 87.4 %all-gather.26.cloned.1.call-done = bf16[2048,8192]{1,0:T(8,128)(2,1)} async-done(((bf16[256,8192]{1,0:T(8,128)(2,1)}), bf16[2048,8192]{1,0:T(8,128)(2,1)}) %all-gather.26.cloned.1.call-update) | async-done | bytes 33554448 | tf_op jit(solution)/shard_map/all_gather | solution.py:140
  425.1 26.6 %fusion.58 = f32[4,128,8192]{2,1,0:T(8,128)} fusion(bf16[4,128,2048]{2,1,0:T(8,128)(2,1)S(1)} %multiply_convert_fusion.3, bf16[2048,8192]{1,0:T(8,128)(2,1)} %all-gather.26.cloned.1.call-done), kind=kOutput, calls=%fused_computation.79 | convolution fusion | flops 17179869184 | bytes 52428800 | tf_op jit(solution)/shard_map/dot_general | solution.py:148
  451.7 136.1 %all-gather.24.cloned.1.call-done = bf16[2048,8192]{1,0:T(8,128)(2,1)} async-done(((bf16[256,8192]{1,0:T(8,128)(2,1)}), bf16[2048,8192]{1,0:T(8,128)(2,1)}) %all-gather.24.cloned.1.call-update) | async-done | bytes 33554448 | tf_op jit(solution)/shard_map/all_gather | solution.py:139
  587.8 27.0 %fusion.62 = f32[4,128,8192]{2,1,0:T(8,128)} fusion(bf16[4,128,2048]{2,1,0:T(8,128)(2,1)S(1)} %multiply_convert_fusion.3, bf16[2048,8192]{1,0:T(8,128)(2,1)} %all-gather.24.cloned.1.call-done), kind=kOutput, calls=%fused_computation.83 | convolution fusion | flops 17179869184 | bytes 52428800 | tf_op jit(solution)/shard_map/dot_general | solution.py:147
  614.8 135.7 %all-gather.28.cloned.1.call-done = bf16[8192,2048]{1,0:T(8,128)(2,1)} async-done(((bf16[1024,2048]{1,0:T(8,128)(2,1)}), bf16[8192,2048]{1,0:T(8,128)(2,1)}) %all-gather.28.cloned.1.call-update) | async-done | bytes 33554448 | tf_op jit(solution)/shard_map/all_gather | solution.py:141
  750.5 38.7 %multiply_convert_fusion.1 = (bf16[4,128,8192]{2,1,0:T(8,128)(2,1)}, bf16[4,128,8192]{2,1,0:T(8,128)(2,1)}, bf16[4,128,8192]{2,1,0:T(8,128)(2,1)}) fusion(f32[4,128,8192]{2,1,0:T(8,128)} %fusion.58, f32[4,128,8192]{2,1,0:T(8,128)} %fusion.62, bf16[4,128,2048]{2,1,0:T(8,128)(2,1)} %param.20, bf16[8192,2048]{1,0:T(8,128)(2,1)} %all-gather.28.cloned.1.call-done), kind=kOutput, calls=%fused_computation.91 | convolution fusion | flops 17238589440 | bytes 94371840 | tf_op jit(solution)/shard_map/btd,fd->btf/dot_general | solution.py:162
  789.2 25.2 fusion.56
  814.4 26.6 %multiply_reduce_fusion = (bf16[2048]{0:T(1024)(128)(2,1)}, f32[4,128]{1,0:T(4,128)S(1)}, f32[4,128,2048]{2,1,0:T(8,128)}) fusion(f32[4,128,2048]{2,1,0:T(8,128)S(1)} %copy-done.6, f32[4,128]{1,0:T(4,128)S(1)} %add_rsqrt_fusion, f32[2048]{0:T(1024)S(1)} %bitcast.303, f32[4,128,2048]{2,1,0:T(8,128)} %fusion.56, ...), kind=kOutput, calls=%fused_computation.119 | convolution fusion | flops 17187207168 | bytes 54542336 | tf_op jit(solution)/shard_map/btf,df->btd/dot_general | solution.py:167
  857.7 211.9 %while.27 = (s32[]{:T(128)}, f32[4,128,8,4,64]{1,4,3,2,0:T(8,128)}, bf16[4,1024,8,64]{1,3,2,0:T(8,128)(2,1)}, bf16[4,1024,8,64]{1,3,2,0:T(8,128)(2,1)}, bf16[4,1...) while((s32[]{:T(128)}, f32[4,128,8,4,64]{1,4,3,2,0:T(8,128)}, ...), condition=%wide.region_9.10_spmd, body=%wide.region_7.9_spmd.sunk | while | flops 2723280128 | bytes 287672128 | solution.py:227
  869.1 14.8 fusion.177
  922.0 14.8 fusion.177
  974.9 14.8 fusion.177
  1027.8 14.8 fusion.177
  1094.9 13.5 copy.114
  1122.6 44.4 %bitcast_convert_fusion = bf16[2048,16384]{1,0:T(8,128)(2,1)} fusion(bf16[4,128,2048]{2,1,0:T(8,128)(2,1)S(1)} %copy-done.14, bf16[4,128,8192]{2,1,0:T(8,128)(2,1)} %get-tuple-element.188, bf16[4,128,8192]{2,1,0:T(8,128)(2,1)} %get-tuple-element.186), kind=kOutput, calls=%fused_computation.71 | convolution fusion | flops 34426847232 | bytes 85983232 | tf_op jit(solution)/shard_map/dot_general | solution.py:39
  1176.3 25.1 reduce-scatter.27.cloned.1.call-done
  1232.7 28.1 %bitcast_convert_fusion.1 = bf16[8192,2048]{1,0:T(8,128)(2,1)} fusion(bf16[4,128,8192]{2,1,0:T(8,128)(2,1)} %get-tuple-element.187, bf16[4,128,2048]{2,1,0:T(8,128)(2,1)} %param.20), kind=kOutput, calls=%fused_computation.72 | convolution fusion | flops 17196646400 | bytes 44040192 | tf_op jit(solution)/shard_map/dot_general | solution.py:39
  1260.9 327.8 %reduce-scatter.21.cloned.1.call-done = bf16[256,16384]{1,0:T(8,128)(2,1)} async-done(((bf16[2048,16384]{1,0:T(8,128)(2,1)}), bf16[256,16384]{1,0:T(8,128)(2,1)}) %reduce-scatter.21.cloned.1.call-update) | async-done | bytes 8388624 | tf_op jit(solution)/shard_map/reduce_scatter | solution.py:173
  1594.8 39.3 %reduce-scatter.15.cloned.1.call-done = bf16[256,512]{1,0:T(8,128)(2,1)} async-done(((bf16[2048,512]{1,0:T(8,128)(2,1)}), bf16[256,512]{1,0:T(8,128)(2,1)}) %reduce-scatter.15.cloned.1.call-update) | async-done | bytes 262160 | tf_op jit(solution)/shard_map/reduce_scatter | solution.py:271
  1634.1 44.4 %reduce-scatter.17.cloned.1.call-done = bf16[256,512]{1,0:T(8,128)(2,1)} async-done(((bf16[2048,512]{1,0:T(8,128)(2,1)}), bf16[256,512]{1,0:T(8,128)(2,1)}) %reduce-scatter.17.cloned.1.call-update) | async-done | bytes 262160 | tf_op jit(solution)/shard_map/reduce_scatter | solution.py:274
  1678.5 75.6 %reduce-scatter.13.cloned.1.call-done = bf16[256,2048]{1,0:T(8,128)(2,1)} async-done(((bf16[2048,2048]{1,0:T(8,128)(2,1)}), bf16[256,2048]{1,0:T(8,128)(2,1)}) %reduce-scatter.13.cloned.1.call-update) | async-done | bytes 1048592 | tf_op jit(solution)/shard_map/reduce_scatter | solution.py:268
  1754.1 75.2 %reduce-scatter.19.cloned.1.call-done = bf16[256,2048]{1,0:T(8,128)(2,1)} async-done(((bf16[2048,2048]{1,0:T(8,128)(2,1)}), bf16[256,2048]{1,0:T(8,128)(2,1)}) %reduce-scatter.19.cloned.1.call-update) | async-done | bytes 1048592 | tf_op jit(solution)/shard_map/reduce_scatter | solution.py:277
  1829.3 209.1 %reduce-scatter.23.cloned.1.call-done = bf16[1024,2048]{1,0:T(8,128)(2,1)} async-done(((bf16[8192,2048]{1,0:T(8,128)(2,1)}), bf16[1024,2048]{1,0:T(8,128)(2,1)}) %reduce-scatter.23.cloned.1.call-update) | async-done | bytes 4194320 | tf_op jit(solution)/shard_map/reduce_scatter | solution.py:182
  2048.2 25.0 add_convert_fusion
  2079.4 14.6 all-reduce.2
  2114.6 442.1 %all-reduce.7.cloned.1.call-done = (bf16[256,2048]{1,0:T(8,128)(2,1)}, bf16[256,512]{1,0:T(8,128)(2,1)}, bf16[256,512]{1,0:T(8,128)(2,1)}, bf16[256,2048]{1,0:T(...) async-done(((bf16[256,2048]{1,0:T(8,128)(2,1)}, bf16[256,512]{1,0:T(8,128)(2,1)}, bf16[256,512]{1,0:T(8,128)(2,1)}, ...) | async-done | bytes 15204368 | tf_op jit(solution)/shard_map/psum | solution.py:286
  (300 shorter events, 499.3 us)
Async XLA Ops:
  7.2 33.4 %all-gather.12.cloned.1.call-start = ((), (), s32[]{:S(2)}) async-start(), calls=%async_computation.8 | async-start | bytes 2359296 | tf_op jit(solution)/shard_map/all_gather | solution.py:90
  7.9 62.4 %all-gather.16.cloned.1.call-start = ((), (), s32[]{:S(2)}) async-start(), calls=%async_computation.10 | async-start | bytes 2359296 | tf_op jit(solution)/shard_map/all_gather | solution.py:89
  8.7 118.0 %all-gather.20.cloned.1.call-start = ((), (), s32[]{:S(2)}) async-start(), calls=%async_computation.12 | async-start | bytes 9437184 | tf_op jit(solution)/shard_map/all_gather | solution.py:88
  9.4 157.1 %all-gather.14.cloned.1.call-start = ((), (), s32[]{:S(2)}) async-start(), calls=%async_computation.9 | async-start | bytes 4718592 | tf_op jit(solution)/shard_map/all_gather | solution.py:115
  20.4 106.2 %copy-start.25 = (f32[8,1,256]{2,1,0:T(1,128)}, f32[8,1,256]{2,1,0:T(1,128)S(1)}, u32[]{:S(2)}) copy-start(f32[8,1,256]{2,1,0:T(1,128)S(1)} %convert_element_type.235) | copy-start | bytes 24580
  22.5 104.1 %copy-start.28 = (f32[4,128]{1,0:T(4,128)}, f32[4,128]{1,0:T(4,128)S(1)}, u32[]{:S(2)}) copy-start(f32[4,128]{1,0:T(4,128)S(1)} %add_rsqrt_fusion.1) | copy-start | bytes 6148
  40.5 29.8 %copy-start.2 = (bf16[4,128,2048]{2,1,0:T(8,128)(2,1)S(1)}, bf16[4,128,2048]{2,1,0:T(8,128)(2,1)}, u32[]{:S(2)}) copy-start(bf16[4,128,2048]{2,1,0:T(8,128)(2,1)} %param.17) | copy-start | bytes 6291460
  45.2 161.0 %all-gather.18.cloned.1.call-start = ((), (), s32[]{:S(2)}) async-start(), calls=%async_computation.11 | async-start | bytes 4718592 | tf_op jit(solution)/shard_map/all_gather | solution.py:114
  46.2 87.8 %copy-start.20 = (f32[4,128,32]{1,2,0:T(8,128)}, f32[4,128,32]{1,2,0:T(8,128)S(1)}, u32[]{:S(2)}) copy-start(f32[4,128,32]{1,2,0:T(8,128)S(1)} %get-tuple-element.201) | copy-start | bytes 196612
  74.4 252.5 %all-gather.22.cloned.1.call-start = ((), (), s32[]{:S(2)}) async-start(), calls=%async_computation.13 | async-start | bytes 9437184 | tf_op jit(solution)/shard_map/all_gather | solution.py:91
  74.9 350.2 %all-gather.26.cloned.1.call-start = ((), (), s32[]{:S(2)}) async-start(), calls=%async_computation.15 | async-start | bytes 37748736 | tf_op jit(solution)/shard_map/all_gather | solution.py:140
  75.7 512.1 %all-gather.24.cloned.1.call-start = ((), (), s32[]{:S(2)}) async-start(), calls=%async_computation.14 | async-start | bytes 37748736 | tf_op jit(solution)/shard_map/all_gather | solution.py:139
  76.5 674.1 %all-gather.28.cloned.1.call-start = ((), (), s32[]{:S(2)}) async-start(), calls=%async_computation.16 | async-start | bytes 37748736 | tf_op jit(solution)/shard_map/all_gather | solution.py:141
  77.2 1089.9 %reduce-scatter.25.cloned.1.call-start = ((), (), s32[]{:S(2)}) async-start(), calls=%async_computation.23 | async-start | bytes 4718592
  206.2 120.6 %copy-start.3 = (bf16[4,128,2048]{2,1,0:T(8,128)(2,1)S(1)}, bf16[4,128,2048]{2,1,0:T(8,128)(2,1)}, u32[]{:S(2)}) copy-start(bf16[4,128,2048]{2,1,0:T(8,128)(2,1)} %param.17) | copy-start | bytes 6291460
  337.6 250.2 %copy-start.13 = (bf16[4,128,2048]{2,1,0:T(8,128)(2,1)}, bf16[4,128,2048]{2,1,0:T(8,128)(2,1)S(1)}, u32[]{:S(2)}) copy-start(bf16[4,128,2048]{2,1,0:T(8,128)(2,1)S(1)} %multiply_convert_fusion.3) | copy-start | bytes 6291460
  789.2 25.2 copy-start.6
  869.1 16.7 slice-start.3
  921.7 15.0 slice-start
  922.0 16.7 slice-start.3
  974.9 16.7 slice-start.3
  1027.8 16.7 slice-start.3
  1094.9 106.6 %reduce-scatter.27.cloned.1.call-start = ((), (), s32[]{:S(2)}) async-start(), calls=%async_computation.24 | async-start | bytes 4718592
  1121.0 467.7 %reduce-scatter.21.cloned.1.call-start = ((), (), s32[]{:S(2)}) async-start(), calls=%async_computation.21 | async-start | bytes 75497472 | tf_op jit(solution)/shard_map/reduce_scatter | solution.py:173
  1167.1 467.1 %reduce-scatter.15.cloned.1.call-start = ((), (), s32[]{:S(2)}) async-start(), calls=%async_computation.18 | async-start | bytes 2359296 | tf_op jit(solution)/shard_map/reduce_scatter | solution.py:271
  1176.3 502.2 %reduce-scatter.17.cloned.1.call-start = ((), (), s32[]{:S(2)}) async-start(), calls=%async_computation.19 | async-start | bytes 2359296 | tf_op jit(solution)/shard_map/reduce_scatter | solution.py:274
  1209.4 544.7 %reduce-scatter.13.cloned.1.call-start = ((), (), s32[]{:S(2)}) async-start(), calls=%async_computation.17 | async-start | bytes 9437184 | tf_op jit(solution)/shard_map/reduce_scatter | solution.py:268
  1222.0 607.3 %reduce-scatter.19.cloned.1.call-start = ((), (), s32[]{:S(2)}) async-start(), calls=%async_computation.20 | async-start | bytes 9437184 | tf_op jit(solution)/shard_map/reduce_scatter | solution.py:277
  1232.6 805.8 %reduce-scatter.23.cloned.1.call-start = ((), (), s32[]{:S(2)}) async-start(), calls=%async_computation.22 | async-start | bytes 37748736 | tf_op jit(solution)/shard_map/reduce_scatter | solution.py:182
  1260.8 1295.9 %all-reduce.7.cloned.1.call-start = ((), (), s32[]{:S(2)}) async-start(), calls=%async_computation.25 | async-start | bytes 30408704 | tf_op jit(solution)/shard_map/psum | solution.py:286
  2048.1 25.1 copy-start.16
  2048.1 25.1 copy-start.19
  (43 other events, 317.5 us)
Sparse Core Ops, SparseCore 0:
  9.9 30.5 all-gather.11
  42.4 27.8 all-gather.15
  72.2 54.3 all-gather.19
  129.0 37.4 all-gather.13
  168.8 37.4 all-gather.17
  208.0 54.3 all-gather.21
  264.3 160.7 all-gather.25
  427.0 160.7 all-gather.23
  589.7 160.7 all-gather.27
  1095.0 51.3 reduce-scatter.24
  1150.1 51.2 reduce-scatter.26
  1204.9 383.7 reduce-scatter.20
  1592.9 41.2 reduce-scatter.14
  1637.3 41.1 reduce-scatter.16
  1682.8 71.2 reduce-scatter.12
  1758.0 71.2 reduce-scatter.18
  1833.1 205.2 reduce-scatter.22
  2041.7 514.8 all-reduce.6
where the time goes:
time: 2590 us
  waiting for transfers between devices  1750 us (68%)
  matrix products  549 us (21%)
  other arithmetic  121 us (5%)
  local copies, waits for them, and re-layouts  98.8 us (4%)
  blocking collectives  54.3 us (2%)
    psum x1, waiting for transfers between devices, body(): lax.psum(owned_query.astype(jnp.bfloat16), 'replica').astype(jnp.float32)  442 us
    reduce_scatter x1, waiting for transfers between devices, body(): lax.psum_scatter(outer_sum(columns, both_grads).astype(jnp.bfloat16), 'sh...  328 us
    reduce_scatter x1, waiting for transfers between devices, body(): lax.psum_scatter(outer_sum(columns, cot_flat).astype(jnp.bfloat16), 'shar...  209 us
    all_gather x1, waiting for transfers between devices, body(): lax.all_gather(gate_weight, 'shard', axis=0, tiled=True)  136 us
    all_gather x1, waiting for transfers between devices, body(): lax.all_gather(down_weight, 'shard', axis=0, tiled=True)  136 us
    dot_general x8, matrix products, score_block(): jnp.einsum('qhgd,khd->hgqk', grouped, all_keys, preferred_element_type=jn...  101 us
    dot_general x6, matrix products, outer_sum(): lax.dot_general(left, right, (((0,), (0,)), ((), ())), preferred_element_...  97.2 us
    all_gather x1, waiting for transfers between devices, body(): lax.all_gather(up_weight, 'shard', axis=0, tiled=True)  87.4 us
  transfers between devices with their start and end apart: 18, of which 16 were waited for; matrix products, arithmetic and copies ran while one was open for 15% of the time, Pallas kernels for 0%

commit v1 on v0

v1 whole, which is shorter than its diff:
```python
import functools
import math

import jax
import jax.numpy as jnp
from jax import lax
from jax.experimental import pallas as pl
from jax.experimental.pallas import tpu as pltpu
from jax.sharding import PartitionSpec as P

HEADS = 32
KV_HEADS = 8
HEAD_DIM = 64

epsilon = 1e-05
rope_base = 500000.0
masked_score = -1e30
f32 = jnp.float32
bf16 = jnp.bfloat16


def angles(doc_positions):
    freq_index = jnp.arange(HEAD_DIM // 2, dtype=f32)
    inverse_freq = jnp.exp(freq_index * (-2.0 * math.log(rope_base) / HEAD_DIM))
    return doc_positions.astype(f32)[..., None] * inverse_freq


def outer_sum(left, right):
    return lax.dot_general(left, right, (((0,), (0,)), ((), ())), preferred_element_type=f32)


def dot_nt(left, right):
    return lax.dot_general(left, right, (((1,), (1,)), ((), ())), preferred_element_type=f32)


def dot_nn(left, right):
    return lax.dot_general(left, right, (((1,), (0,)), ((), ())), preferred_element_type=f32)


def score_bias(seg_col, seg_row, first, rows):
    last = first + rows
    key_at = lax.broadcasted_iota(jnp.int32, (last, rows), 0)
    query_at = lax.broadcasted_iota(jnp.int32, (last, rows), 1) + first
    allowed = (seg_col[:last] == seg_row[:, first:last]) & (key_at <= query_at)
    return jnp.where(allowed, 0.0, masked_score)


def forward_kernel(heads, rows, qkv_ref, seg_col_ref, seg_row_ref, out_ref, norm_ref):
    shards, _, span, _ = qkv_ref.shape
    length = shards * span
    wide = heads * HEAD_DIM
    seg_col, seg_row = seg_col_ref[0], seg_row_ref[0]
    keys = qkv_ref[:, 0, :, wide : wide + HEAD_DIM].reshape(length, HEAD_DIM)
    values = qkv_ref[:, 0, :, wide + HEAD_DIM :].reshape(length, HEAD_DIM)
    values_t = values.astype(f32).T.astype(bf16)
    for first in range(0, length, rows):
        last = first + rows
        bias = score_bias(seg_col, seg_row, first, rows)
        queries = (
            qkv_ref[first // span : last // span, 0, :, :wide].reshape(rows, wide)
            * HEAD_DIM ** (-0.5)
        )
        parts = []
        for head in range(heads):
            one = queries[:, head * HEAD_DIM : (head + 1) * HEAD_DIM]
            scores = dot_nt(keys[:last], one) + bias
            top = jnp.max(scores, 0, keepdims=True)
            lifted = jnp.exp(scores - top)
            total = jnp.sum(lifted, 0, keepdims=True)
            probs = (lifted * (1.0 / total)).astype(bf16)
            parts.append(dot_nn(values_t[:, :last], probs))
            norm_ref[0, head : head + 1, first:last] = top + jnp.log(total)
        out = jnp.concatenate(parts, 0).T.astype(bf16)
        out_ref[first // span : last // span, 0] = out.reshape(rows // span, span, wide)


def turn_back(part, cosine, sine):
    half = HEAD_DIM // 2
    lower, upper = part[:half], part[half:]
    return [lower * cosine + upper * sine, upper * cosine - lower * sine]


def backward_kernel(
    heads, rows, qkv_ref, grad_ref, norm_ref, seg_col_ref, seg_row_ref, cos_ref, sin_ref,
    out_ref, key_sum, value_sum,
):
    shards, _, span, _ = qkv_ref.shape
    length = shards * span
    wide = heads * HEAD_DIM
    seg_col, seg_row = seg_col_ref[0], seg_row_ref[0]
    keys = qkv_ref[:, 0, :, wide : wide + HEAD_DIM].reshape(length, HEAD_DIM)
    values = qkv_ref[:, 0, :, wide + HEAD_DIM :].reshape(length, HEAD_DIM)
    keys_t = keys.astype(f32).T.astype(bf16)
    key_sum[...] = jnp.zeros_like(key_sum)
    value_sum[...] = jnp.zeros_like(value_sum)
    for first in range(0, length, rows):
        last = first + rows
        at = slice(first // span, last // span)
        bias = score_bias(seg_col, seg_row, first, rows)
        queries = qkv_ref[at, 0, :, :wide].reshape(rows, wide) * HEAD_DIM ** (-0.5)
        grads = grad_ref[at, 0].reshape(rows, wide)
        cosine, sine = cos_ref[0, :, first:last], sin_ref[0, :, first:last]
        parts = []
        for head in range(heads):
            lanes = slice(head * HEAD_DIM, (head + 1) * HEAD_DIM)
            one, grad = queries[:, lanes], grads[:, lanes]
            scores = dot_nt(keys[:last], one) + bias
            probs = jnp.exp(scores - norm_ref[0, head : head + 1, first:last])
            grad_probs = dot_nt(values[:last], grad)
            level = jnp.sum(probs * grad_probs, 0, keepdims=True)
            grad_scores = (probs * (grad_probs - level)).astype(bf16)
            value_sum[:last] += dot_nn(probs.astype(bf16), grad)
            key_sum[:last] += dot_nn(grad_scores, one)
            turned = dot_nn(keys_t[:, :last], grad_scores) * HEAD_DIM ** (-0.5)
            parts.extend(turn_back(turned, cosine, sine))
        out = jnp.concatenate(parts, 0).T.astype(bf16)
        out_ref[at, 0, :, :wide] = out.reshape(rows // span, span, wide)
    key_parts = turn_back(key_sum[...].T, cos_ref[0], sin_ref[0])
    both = jnp.concatenate([jnp.concatenate(key_parts, 0).T, value_sum[...]], -1)
    out_ref[:, 0, :, wide:] = both.astype(bf16).reshape(shards, span, 2 * HEAD_DIM)


def by_sequence(shape, axis):
    block = tuple(1 if at == axis else size for at, size in enumerate(shape))
    return pl.BlockSpec(block, lambda i: tuple(i if at == axis else 0 for at in range(len(shape))))


def attention_forward(heads, qkv, seg_col, seg_row):
    shards, seqs, span, _ = qkv.shape
    length = shards * span
    out_shape = (
        jax.ShapeDtypeStruct((shards, seqs, span, heads * HEAD_DIM), bf16),
        jax.ShapeDtypeStruct((seqs, heads, length), f32),
    )
    return pl.pallas_call(
        functools.partial(forward_kernel, heads, 256),
        grid=(seqs,),
        in_specs=[
            by_sequence(qkv.shape, 1),
            by_sequence(seg_col.shape, 0),
            by_sequence(seg_row.shape, 0),
        ],
        out_specs=(by_sequence(out_shape[0].shape, 1), by_sequence(out_shape[1].shape, 0)),
        out_shape=out_shape,
        compiler_params=pltpu.CompilerParams(vmem_limit_bytes=48 * 2**20),
        cost_estimate=pl.CostEstimate(
            flops=4 * seqs * heads * length * length * HEAD_DIM,
            bytes_accessed=2 * qkv.size * 2,
            transcendentals=seqs * heads * length * length,
        ),
    )(qkv, seg_col, seg_row)


def attention_backward(heads, qkv, grads, norms, seg_col, seg_row, cosine, sine):
    shards, seqs, span, _ = qkv.shape
    length = shards * span
    args = (qkv, grads, norms, seg_col, seg_row, cosine, sine)
    return pl.pallas_call(
        functools.partial(backward_kernel, heads, 256),
        grid=(seqs,),
        in_specs=[by_sequence(a.shape, 1 if i < 2 else 0) for i, a in enumerate(args)],
        out_specs=by_sequence(qkv.shape, 1),
        out_shape=jax.ShapeDtypeStruct(qkv.shape, bf16),
        scratch_shapes=[pltpu.VMEM((length, HEAD_DIM), f32), pltpu.VMEM((length, HEAD_DIM), f32)],
        compiler_params=pltpu.CompilerParams(vmem_limit_bytes=48 * 2**20),
        cost_estimate=pl.CostEstimate(
            flops=10 * seqs * heads * length * length * HEAD_DIM,
            bytes_accessed=3 * qkv.size * 2,
            transcendentals=seqs * heads * length * length,
        ),
    )(*args)


def exchange(blocks):
    return lax.all_to_all(blocks, "shard", 0, 0, tiled=True)


def exchange_async(blocks):
    count = blocks.shape[0]
    me = lax.axis_index("shard")
    result = blocks
    for step in range(1, count):
        pairs = [(i, i ^ step) for i in range(count)]
        partner = me ^ step
        sent = lax.dynamic_index_in_dim(blocks, partner, 0, keepdims=True)
        got = lax.ppermute(sent, "shard", pairs)
        result = lax.dynamic_update_slice_in_dim(result, got, partner, 0)
    return result


def replica_sum(part):
    count = lax.axis_size("replica")
    if count != 4:
        return lax.psum(part.astype(bf16), "replica").astype(f32)
    me = lax.axis_index("replica")
    inner = (me == 1) | (me == 2)
    low = part.astype(bf16)
    inward = lax.ppermute(low, "replica", [(0, 1), (3, 2)])
    half = (part.astype(f32) + inward.astype(f32)).astype(bf16)
    other = lax.ppermute(half, "replica", [(1, 2), (2, 1)])
    whole = (half.astype(f32) + other.astype(f32)).astype(bf16)
    outward = lax.ppermute(whole, "replica", [(1, 0), (2, 3)])
    return jnp.where(inner, whole, outward).astype(f32)


def norm_back(grad_normed, unit_rows, scale_rows, gain_rows):
    scaled_grad = grad_normed * gain_rows
    return scale_rows * (
        scaled_grad - unit_rows * jnp.mean(scaled_grad * unit_rows, -1, keepdims=True)
    )


def gather(block):
    return lax.all_gather(block, "shard", axis=0, tiled=True)


def scatter(partial):
    return lax.psum_scatter(partial.astype(bf16), "shard", scatter_dimension=0, tiled=True).astype(
        f32
    )


def body(
    tokens,
    segments,
    positions,
    cotangent,
    attention_gain,
    query_weight,
    key_weight,
    value_weight,
    output_weight,
    mlp_gain,
    gate_weight,
    up_weight,
    down_weight,
):
    seqs, span, width = tokens.shape
    shards = lax.axis_size("shard")
    me = lax.axis_index("shard")
    rows = seqs * span
    length = shards * span
    owned = query_weight.shape[0]
    heads = HEADS // shards
    copies = max(1, shards // KV_HEADS)
    wide = heads * HEAD_DIM
    part = wide + 2 * HEAD_DIM
    hidden_share = down_weight.shape[0]

    def per_head(weight):
        return jnp.repeat(weight.reshape(owned, KV_HEADS, HEAD_DIM), copies, axis=1)

    qkv_owned = jnp.concatenate(
        [query_weight.reshape(owned, shards, wide), per_head(key_weight), per_head(value_weight)],
        -1,
    ).reshape(owned, shards * part)
    qkv_full = gather(qkv_owned)
    gains = lax.all_gather(jnp.stack([attention_gain, mlp_gain]), "shard", axis=1, tiled=True)
    gain_one, gain_two = gains[0].astype(f32), gains[1].astype(f32)
    places = lax.all_gather(jnp.stack([segments, positions]), "shard", axis=2, tiled=True)
    seg_row, seg_col = places[0][:, None, :], places[0][:, :, None]
    angle_all = jnp.swapaxes(angles(places[1]), 1, 2)
    cos_all, sin_all = jnp.cos(angle_all), jnp.sin(angle_all)
    output_full = gather(output_weight)

    x = tokens.reshape(rows, width).astype(f32)
    scale_one = lax.rsqrt(jnp.mean(x * x, -1, keepdims=True) + epsilon)
    unit_one = x * scale_one
    normed_one = (unit_one * gain_one).astype(bf16)
    projected = dot_nn(normed_one, qkv_full).reshape(rows, shards, part)
    angle = angles(positions).reshape(rows, 1, 1, HEAD_DIM // 2)
    cosine, sine = jnp.cos(angle), jnp.sin(angle)
    turning = projected[:, :, : wide + HEAD_DIM].reshape(rows, shards, heads + 1, HEAD_DIM)
    lower, upper = turning[..., : HEAD_DIM // 2], turning[..., HEAD_DIM // 2 :]
    turned = jnp.concatenate(
        [lower * cosine - upper * sine, upper * cosine + lower * sine], -1
    ).reshape(rows, shards, wide + HEAD_DIM)
    qkv_rows = jnp.concatenate([turned, projected[:, :, wide + HEAD_DIM :]], -1).astype(bf16)
    qkv = exchange(jnp.swapaxes(qkv_rows, 0, 1)).reshape(shards, seqs, span, part)

    attn_heads, norms = attention_forward(heads, qkv, seg_col, seg_row)
    attn = exchange(attn_heads.reshape(shards, rows, wide))
    attn = jnp.swapaxes(attn, 0, 1).reshape(rows, HEADS * HEAD_DIM)
    hidden = x + dot_nn(attn, output_full)
    scale_two = lax.rsqrt(jnp.mean(hidden * hidden, -1, keepdims=True) + epsilon)
    unit_two = hidden * scale_two
    normed_two = (unit_two * gain_two).astype(bf16)

    def to_columns(weight):
        blocks = jnp.swapaxes(weight.reshape(owned, shards, hidden_share), 0, 1)
        return exchange_async(blocks).reshape(shards * owned, hidden_share)

    gate_columns, up_columns = to_columns(gate_weight), to_columns(up_weight)
    cot_rows = cotangent.reshape(rows, width)
    cot_all = gather(cot_rows)
    normed_all = gather(normed_two)
    gate = dot_nn(normed_all, gate_columns)
    up = dot_nn(normed_all, up_columns)
    grad_mixed = dot_nt(cot_all, down_weight)
    sigmoid = jax.nn.sigmoid(gate)
    swish = gate * sigmoid
    mixed = (swish * up).astype(bf16)
    grad_gate = (grad_mixed * up * (sigmoid + swish * (1.0 - sigmoid))).astype(bf16)
    grad_up = (grad_mixed * swish).astype(bf16)
    grad_two = scatter(dot_nt(grad_gate, gate_columns) + dot_nt(grad_up, up_columns))
    down_grad = replica_sum(outer_sum(mixed, cot_all))

    def to_rows(grad):
        blocks = exchange_async(grad.astype(bf16).reshape(shards, owned, hidden_share))
        summed = replica_sum(blocks)
        return jnp.swapaxes(summed, 0, 1).reshape(owned, shards * hidden_share)

    gate_grad = to_rows(outer_sum(normed_all, grad_gate))
    up_grad = to_rows(outer_sum(normed_all, grad_up))
    block_out = (hidden + scatter(dot_nn(mixed, down_weight))).astype(bf16)

    second_grad = jnp.sum(grad_two * unit_two, 0)
    grad_hidden = cot_rows.astype(f32) + norm_back(grad_two, unit_two, scale_two, gain_two)
    branch = grad_hidden.astype(bf16)
    grad_attn = dot_nt(branch, output_full).astype(bf16).reshape(rows, shards, wide)
    grad_heads = exchange(jnp.swapaxes(grad_attn, 0, 1)).reshape(shards, seqs, span, wide)
    output_grad = replica_sum(scatter(outer_sum(attn, branch)))
    grad_qkv = attention_backward(
        heads, qkv, grad_heads, norms, seg_col, seg_row, cos_all, sin_all
    )
    grad_qkv = exchange(grad_qkv.reshape(shards, rows, part))
    grad_qkv = jnp.swapaxes(grad_qkv, 0, 1).reshape(rows, shards * part)
    grad_one = dot_nt(grad_qkv, qkv_full)
    qkv_grad = replica_sum(scatter(outer_sum(normed_one, grad_qkv)))
    qkv_grad = qkv_grad.reshape(owned, shards, part)

    def kv_grad(columns):
        return jnp.sum(columns.reshape(owned, KV_HEADS, copies, HEAD_DIM), 2).reshape(
            owned, KV_HEADS * HEAD_DIM
        )

    query_grad = qkv_grad[:, :, :wide].reshape(owned, HEADS * HEAD_DIM)
    key_grad = kv_grad(qkv_grad[:, :, wide : wide + HEAD_DIM])
    value_grad = kv_grad(qkv_grad[:, :, wide + HEAD_DIM :])
    first_grad = jnp.sum(grad_one * unit_one, 0)
    token_grad = grad_hidden + norm_back(grad_one, unit_one, scale_one, gain_one)
    gain_grads = lax.psum(jnp.stack([first_grad, second_grad]), ("replica", "shard"))
    gain_grads = lax.dynamic_slice_in_dim(gain_grads, me * owned, owned, 1)
    return (
        block_out.reshape(seqs, span, width),
        token_grad.reshape(seqs, span, width),
        gain_grads[0],
        query_grad,
        key_grad,
        value_grad,
        output_grad,
        gain_grads[1],
        gate_grad,
        up_grad,
        down_grad,
    )


def solution(mesh):
    rows = P("shard", None)
    blocks = P("replica", "shard", None)
    in_specs = (
        blocks, P("replica", "shard"), P("replica", "shard"), blocks, P("shard"),
        rows, rows, rows, rows, P("shard"), rows, rows, rows,
    )
    out_specs = (
        blocks, blocks, P("shard"), rows, rows, rows, rows, P("shard"), rows, rows, rows,
    )
    return jax.shard_map(body, mesh=mesh, in_specs=in_specs, out_specs=out_specs, check_vma=False)
```

time: 2590 us -> 1790 us (0.69)
  waiting for transfers between devices: 1750 us -> 982 us
  matrix products: 549 us -> 289 us
  starting transfers between devices: 0.72 us -> 99.5 us
  Pallas kernels: 0 us -> 78.7 us
  blocking collectives: 54.3 us -> 128 us
  other arithmetic: 121 us -> 77.4 us
    ppermute x0 -> x43, waiting for transfers between devices: none -> 611 us  [the longest x5 276 us: replica_sum(): outward = lax.ppermute(whole, 'replica', [(1, 0), (2, 3)])]
    reduce_scatter x6 -> x4, waiting for transfers between devices: 771 us -> 209 us  [scatter(): lax.psum_scatter(partial.astype(bf16), 'shard', scatter_dimension=0, tile...]
    psum x1 -> x0, waiting for transfers between devices: 442 us -> none  [body(): lax.psum(owned_query.astype(jnp.bfloat16), 'replica').astype(jnp.float32)]
    all_gather x9 -> x4, waiting for transfers between devices: 503 us -> 61.6 us  [gather(): return lax.all_gather(block, 'shard', axis=0, tiled=True)]
    dot_general x42 -> x10, matrix products: 452 us -> 197 us  [the longest x5 100 us: dot_nn(): lax.dot_general(left, right, (((1,), (0,)), ((), ())), preferred_element_...]
    all_to_all x0 -> x4, waiting for transfers between devices: none -> 99.5 us  [exchange(): return lax.all_to_all(blocks, 'shard', 0, 0, tiled=True)]
    ppermute x0 -> x43, starting transfers between devices: none -> 81.7 us  [the longest x5 43.3 us: replica_sum(): inward = lax.ppermute(low, 'replica', [(0, 1), (3, 2)])]
    pallas_call x0 -> x2, Pallas kernels: none -> 78.7 us  [the longest x1 39.7 us: attention_backward(): pl.pallas_call(functools.partial(backward_kernel, heads, 256), grid=(seqs...]
  transfers between devices with their start and end apart: 18 -> 55, of which waited for: 16 -> 31; matrix products, arithmetic and copies ran while one was open for 15% -> 18% of each run, Pallas kernels for 0% -> 4%
where the time goes in v1:
time: 1790 us; the launch traced here: 1780 us
  waiting for transfers between devices  982 us (55%)
  matrix products  289 us (16%)
  blocking collectives  128 us (7%)
  local copies, waits for them, and re-layouts  107 us (6%)
  starting transfers between devices  99.5 us (6%)
  Pallas kernels  78.7 us (4%)
  other arithmetic  77.4 us (4%)
    ppermute x5, waiting for transfers between devices, replica_sum(): outward = lax.ppermute(whole, 'replica', [(1, 0), (2, 3)])  276 us
    reduce_scatter x4, waiting for transfers between devices, scatter(): lax.psum_scatter(partial.astype(bf16), 'shard', scatter_dimension=0, tile...  209 us
    ppermute x28, waiting for transfers between devices, exchange_async(): got = lax.ppermute(sent, 'shard', pairs)  198 us
    ppermute x5, waiting for transfers between devices, replica_sum(): inward = lax.ppermute(low, 'replica', [(0, 1), (3, 2)])  137 us
    dot_general x5, matrix products, dot_nn(): lax.dot_general(left, right, (((1,), (0,)), ((), ())), preferred_element_...  100 us
    all_to_all x4, waiting for transfers between devices, exchange(): return lax.all_to_all(blocks, 'shard', 0, 0, tiled=True)  99.5 us
    dot_general x5, matrix products, dot_nt(): lax.dot_general(left, right, (((1,), (1,)), ((), ())), preferred_element_...  96.6 us
    dot_general x5, matrix products, outer_sum(): lax.dot_general(left, right, (((0,), (0,)), ((), ())), preferred_element_...  91.5 us
  transfers between devices with their start and end apart: 55, of which 31 were waited for; matrix products, arithmetic and copies ran while one was open for 18% of the time, Pallas kernels for 4%

profile of v1, /device:TPU:0, one launch (start us, length us, event | category | flops | bytes accessed | tf_op | source)
XLA Modules:
  0.0 1776.9 jit_solution(9709094203149953111)
XLA Ops:
  31.9 61.6 %all-gather.5.cloned.1.call-done = bf16[2048,3072]{0,1:T(8,128)(2,1)} async-done(((bf16[256,3072]{0,1:T(8,128)(2,1)}), bf16[2048,3072]{0,1:T(8,128)(2,1)}) %all-gather.5.cloned.1.call-update) | async-done | bytes 12582928 | tf_op jit(solution)/shard_map/all_gather | solution.py:214
  112.0 56.2 %all_gather.20 = s32[2,4,1024]{2,0,1:T(2,128)S(1)} all-gather(s32[2,4,128]{2,0,1:T(2,128)S(1)} %pad_add_fusion), channel_id=1, replica_groups=mesh['replica'=4,'shard'=8] {'shard'}, dimensions={2}, use_global_device_ids=true | all-gather | bytes 36864 | tf_op jit(solution)/shard_map/all_gather | solution.py:260
  174.1 39.0 %shard_map.212 = (bf16[8,4,128,256]{3,2,1,0:T(8,128)(2,1)S(1)}, f32[4,4,1024]{2,1,0:T(4,128)S(1)}) custom-call(bf16[8,4,128,384]{3,2,1,0:T(8,128)(2,1)} %bitcast.176, s32[4,1024,1]{2,1,0:T(8,128)S(1)} %copy.55.seg_col_ref, s32[4,1,1024]{2,1,0:T(1,128)S(1)} %get-tuple-element.79.seg_row_ref), custom_call_target="tpu_custom_call" | custom-call | flops 4294967296 | bytes 6291456 | tf_op jit(solution)/shard_map/pallas_call | solution.py:135
  222.8 49.3 %all-to-all-done.1 = bf16[8,512,256]{1,2,0:T(8,128)(2,1)} async-done(((bf16[8,512,256]{1,2,0:T(8,128)(2,1)}), bf16[8,512,256]{1,2,0:T(8,128)(2,1)}, u32[]{:S(2)}, u32[]{:S(2)}) %all-to-all-start.1) | async-done | bytes 2097184 | tf_op jit(solution)/shard_map/all_to_all | solution.py:175
  319.8 19.1 %collective-permute-done.2 = bf16[1,256,1024]{1,2,0:T(8,128)(2,1)} collective-permute-done((bf16[1,256,1024]{1,2,0:T(8,128)(2,1)}, bf16[1,256,1024]{1,2,0:T(8,128)(2,1)}, u32[]{:S(2)}, u32[]{:S(2)}) %collective-permute-start.2) | collective-permute-done | bytes 524320 | tf_op jit(solution)/shard_map/ppermute | solution.py:186
  386.9 13.8 collective-permute-done.9
  425.6 19.1 %collective-permute-done.13 = bf16[1,256,1024]{1,2,0:T(8,128)(2,1)} collective-permute-done((bf16[1,256,1024]{1,2,0:T(8,128)(2,1)S(1)}, bf16[1,256,1024]{1,2,0:T(8,128)(2,1)}, u32[]{:S(2)}, u32[]{:S(2)}) %collective-permute-start.13) | collective-permute-done | bytes 524320 | tf_op jit(solution)/shard_map/ppermute | solution.py:186
  452.9 23.6 %fusion.26 = f32[4096,1024]{1,0:T(8,128)} fusion(bf16[4096,2048]{1,0:T(8,128)(2,1)} %all-gather.11.cloned.1.call-done, bf16[1024,2048]{1,0:T(8,128)(2,1)} %param.25), kind=kOutput, calls=%fused_computation.144 | convolution fusion | flops 17179869184 | bytes 37748736 | tf_op jit(solution)/shard_map/dot_general | solution.py:33
  476.6 23.4 %fusion.25 = f32[4096,1024]{1,0:T(8,128)} fusion(bf16[4096,2048]{1,0:T(8,128)(2,1)} %all-gather.9.cloned.1.call-done, bf16[2048,1024]{1,0:T(8,128)(2,1)} %bitcast.171), kind=kOutput, calls=%fused_computation.143 | convolution fusion | flops 17179869184 | bytes 37748736 | tf_op jit(solution)/shard_map/dot_general | solution.py:37
  499.9 33.3 %multiply_convert_fusion.1 = (bf16[4096,1024]{1,0:T(8,128)(2,1)}, bf16[4096,1024]{1,0:T(8,128)(2,1)}, bf16[4096,1024]{1,0:T(8,128)(2,1)}) fusion(f32[4096,1024]{1,0:T(8,128)} %fusion.26, f32[4096,1024]{1,0:T(8,128)} %fusion.25, bf16[4096,2048]{1,0:T(8,128)(2,1)} %all-gather.9.cloned.1.call-done, bf16[2048,1024]{1,0:T(8,128)(2,1)} %bitcast.173), kind=kOutput, calls=%fused_computation.2 | convolution fusion | flops 17238589440 | bytes 79691776 | tf_op jit(solution)/shard_map/dot_general | solution.py:37
  533.2 25.4 %fusion.27 = f32[4096,2048]{1,0:T(8,128)} fusion(bf16[4096,1024]{1,0:T(8,128)(2,1)} %get-tuple-element.43, bf16[2048,1024]{1,0:T(8,128)(2,1)} %bitcast.174), kind=kOutput, calls=%fused_computation.145 | convolution fusion | flops 17179869184 | bytes 46137344 | tf_op jit(solution)/shard_map/dot_general | solution.py:33
  558.6 27.0 %add_convert_fusion = bf16[4096,2048]{1,0:T(8,128)(2,1)} fusion(f32[4096,2048]{1,0:T(8,128)} %fusion.27, bf16[4096,1024]{1,0:T(8,128)(2,1)} %get-tuple-element.41, bf16[2048,1024]{1,0:T(8,128)(2,1)S(1)} %bitcast.172), kind=kOutput, calls=%fused_computation | convolution fusion | flops 17196646400 | bytes 62914560 | tf_op jit(solution)/shard_map/dot_general | solution.py:33
  585.6 24.1 %convolution_convert_fusion = bf16[4096,2048]{1,0:T(8,128)(2,1)} fusion(bf16[4096,1024]{1,0:T(8,128)(2,1)} %get-tuple-element.42, bf16[1024,2048]{1,0:T(8,128)(2,1)} %param.25), kind=kOutput, calls=%fused_computation.5 | convolution fusion | flops 17188257792 | bytes 29360128 | tf_op jit(solution)/shard_map/dot_general | solution.py:37
  609.8 94.2 %reduce-scatter.7.cloned.1.call-done = bf16[512,2048]{1,0:T(8,128)(2,1)} async-done(((bf16[4096,2048]{1,0:T(8,128)(2,1)}), bf16[512,2048]{1,0:T(8,128)(2,1)}) %reduce-scatter.7.cloned.1.call-update) | async-done | bytes 2097168 | tf_op jit(solution)/shard_map/reduce_scatter | solution.py:218
  708.6 114.8 %reduce-scatter.5.cloned.1.call-done = bf16[512,2048]{1,0:T(8,128)(2,1)} async-done(((bf16[4096,2048]{1,0:T(8,128)(2,1)}), bf16[512,2048]{1,0:T(8,128)(2,1)}) %reduce-scatter.5.cloned.1.call-update) | async-done | bytes 2097168 | tf_op jit(solution)/shard_map/reduce_scatter | solution.py:218
  857.4 38.7 %all-to-all-done.2 = bf16[8,512,256]{2,1,0:T(8,128)(2,1)} async-done(((bf16[8,512,256]{2,1,0:T(8,128)(2,1)}), bf16[8,512,256]{2,1,0:T(8,128)(2,1)}, u32[]{:S(2)}, u32[]{:S(2)}) %all-to-all-start.2) | async-done | bytes 2097184 | tf_op jit(solution)/shard_map/all_to_all | solution.py:175
  896.2 39.7 %shard_map.213 = bf16[8,4,128,384]{3,2,1,0:T(8,128)(2,1)} custom-call(bf16[8,4,128,384]{3,2,1,0:T(8,128)(2,1)} %bitcast.177, bf16[8,4,128,256]{3,2,1,0:T(8,128)(2,1)} %bitcast.46.grad_ref, f32[4,4,1024]{2,1,0:T(4,128)S(1)} %get-tuple-element.14.norm_ref, s32[4,1024,1]{2,1,0:T(8,128)S(1)} %copy.55.seg_col_ref, s32[4,1,1024]{2,1,0:T(1,128)S(1)} %copy-done.2, ...), custom_call_target="tpu_custom_call" | custom-call | flops 10737418240 | bytes 9437184 | tf_op jit(solution)/shard_map/pallas_call | solution.py:158
  944.2 23.1 %convolution_convert_fusion.4 = bf16[2048,1024]{1,0:T(8,128)(2,1)S(1)} fusion(bf16[4096,2048]{1,0:T(8,128)(2,1)} %all-gather.9.cloned.1.call-done, bf16[4096,1024]{1,0:T(8,128)(2,1)} %get-tuple-element.41), kind=kOutput, calls=%fused_computation.45 | convolution fusion | flops 17181966336 | bytes 29360128 | tf_op jit(solution)/shard_map/dot_general | solution.py:29
  994.5 23.2 %convolution_convert_fusion.3 = bf16[2048,1024]{1,0:T(8,128)(2,1)S(1)} fusion(bf16[4096,2048]{1,0:T(8,128)(2,1)} %all-gather.9.cloned.1.call-done, bf16[4096,1024]{1,0:T(8,128)(2,1)} %get-tuple-element.43), kind=kOutput, calls=%fused_computation.44 | convolution fusion | flops 17181966336 | bytes 29360128 | tf_op jit(solution)/shard_map/dot_general | solution.py:29
  1023.1 24.3 %fusion.23 = (bf16[1024,2048]{1,0:T(8,128)(2,1)S(1)}, f32[1024,2048]{1,0:T(8,128)}) fusion(bf16[4096,1024]{1,0:T(8,128)(2,1)} %get-tuple-element.42, bf16[4096,2048]{1,0:T(8,128)(2,1)} %all-gather.11.cloned.1.call-done), kind=kOutput, calls=%fused_computation.141 | convolution fusion | flops 17181966336 | bytes 37748736 | tf_op jit(solution)/shard_map/dot_general | solution.py:29
  1051.0 13.4 collective-permute-done.22
  1072.5 14.4 collective-permute-done.25
  1113.0 19.0 %collective-permute-done.32 = bf16[1,256,1024]{2,1,0:T(8,128)(2,1)S(1)} collective-permute-done((bf16[1,256,1024]{2,1,0:T(8,128)(2,1)S(1)}, bf16[1,256,1024]{2,1,0:T(8,128)(2,1)S(1)}, u32[]{:S(2)}, u32[]{:S(2)}) %collective-permute-start.32) | collective-permute-done | bytes 524320 | tf_op jit(solution)/shard_map/ppermute | solution.py:186
  1178.3 53.2 %collective-permute-done.27 = bf16[8,256,1024]{2,1,0:T(8,128)(2,1)} collective-permute-done((bf16[8,256,1024]{2,1,0:T(8,128)(2,1)S(1)}, bf16[8,256,1024]{2,1,0:T(8,128)(2,1)}, u32[]{:S(2)}, u32[]{:S(2)}) %collective-permute-start.27) | collective-permute-done | bytes 4194336 | tf_op jit(solution)/shard_map/ppermute | solution.py:198
  1236.9 83.7 %collective-permute-done.37 = bf16[8,256,1024]{2,1,0:T(8,128)(2,1)} collective-permute-done((bf16[8,256,1024]{2,1,0:T(8,128)(2,1)S(1)}, bf16[8,256,1024]{2,1,0:T(8,128)(2,1)}, u32[]{:S(2)}, u32[]{:S(2)}) %collective-permute-start.37) | collective-permute-done | bytes 4194336 | tf_op jit(solution)/shard_map/ppermute | solution.py:198
  1344.3 85.7 %collective-permute-done.42 = bf16[1024,2048]{1,0:T(8,128)(2,1)} collective-permute-done((bf16[1024,2048]{1,0:T(8,128)(2,1)}, bf16[1024,2048]{1,0:T(8,128)(2,1)}, u32[]{:S(2)}, u32[]{:S(2)}) %collective-permute-start.42) | collective-permute-done | bytes 4194336 | tf_op jit(solution)/shard_map/ppermute | solution.py:202
  1436.2 27.7 %collective-permute-start.17 = (bf16[256,2048]{1,0:T(8,128)(2,1)}, bf16[256,2048]{1,0:T(8,128)(2,1)}, u32[]{:S(2)}, u32[]{:S(2)}) collective-permute-start(bf16[256,2048]{1,0:T(8,128)(2,1)} %reduce-scatter.11.cloned.1.call-done), channel_id=1, source_target_pairs={{0,8},{24,16},{1,9},{25,17},{2,10},{26,18},{3,11},{27,19},{4,12},{... | collective-permute-start | bytes 3145736 | tf_op jit(solution)/shard_map/ppermute | solution.py:198
  1465.5 54.4 %collective-permute-done.29 = bf16[8,256,1024]{2,1,0:T(8,128)(2,1)} collective-permute-done((bf16[8,256,1024]{2,1,0:T(8,128)(2,1)}, bf16[8,256,1024]{2,1,0:T(8,128)(2,1)}, u32[]{:S(2)}, u32[]{:S(2)}) %collective-permute-start.29) | collective-permute-done | bytes 4194336 | tf_op jit(solution)/shard_map/ppermute | solution.py:202
  1519.9 88.2 %collective-permute-done.39 = bf16[8,256,1024]{2,1,0:T(8,128)(2,1)} collective-permute-done((bf16[8,256,1024]{2,1,0:T(8,128)(2,1)}, bf16[8,256,1024]{2,1,0:T(8,128)(2,1)}, u32[]{:S(2)}, u32[]{:S(2)}) %collective-permute-start.39) | collective-permute-done | bytes 4194336 | tf_op jit(solution)/shard_map/ppermute | solution.py:202
  1639.4 61.6 %psum.7 = f32[2,2048]{1,0:T(2,128)S(1)} all-reduce(f32[2,2048]{1,0:T(2,128)S(1)} %pad_maximum_fusion.2), channel_id=1, replica_groups=mesh['replica'=4,'shard'=8] {'replica','shard'}, use_global_device_ids=true, to_apply=%region_8.9 | all-reduce | flops 4096 | bytes 32768 | tf_op jit(solution)/shard_map/psum | solution.py:342
  1714.3 17.3 collective-permute-done.19
  1733.1 30.3 %collective-permute-done.16 = bf16[256,3072]{1,0:T(8,128)(2,1)S(1)} collective-permute-done((bf16[256,3072]{1,0:T(8,128)(2,1)S(1)}, bf16[256,3072]{1,0:T(8,128)(2,1)S(1)}, u32[]{:S(2)}, u32[]{:S(2)}) %collective-permute-start.16) | collective-permute-done | bytes 1572896 | tf_op jit(solution)/shard_map/ppermute | solution.py:202
  (272 shorter events, 439.6 us)
Async XLA Ops:
  7.2 86.3 %all-gather.5.cloned.1.call-start = ((), (), s32[]{:S(2)}) async-start(), calls=%async_computation.8 | async-start | bytes 14155776 | tf_op jit(solution)/shard_map/all_gather | solution.py:214
  16.1 206.7 %all-gather.7.cloned.1.call-start = ((), (), s32[]{:S(2)}) async-start(), calls=%async_computation.9 | async-start | bytes 9437184 | tf_op jit(solution)/shard_map/all_gather | solution.py:214
  16.8 436.1 %all-gather.11.cloned.1.call-start = ((), (), s32[]{:S(2)}) async-start(), calls=%async_computation.12 | async-start | bytes 18874368 | tf_op jit(solution)/shard_map/all_gather | solution.py:214
  107.4 62.0 %all-to-all-start = ((bf16[8,512,384]{1,2,0:T(8,128)(2,1)}), bf16[8,512,384]{1,2,0:T(8,128)(2,1)}, u32[]{:S(2)}, u32[]{:S(2)}) async-start(bf16[8,512,384]{1,2,0:T(8,128)(2,1)} %maximum_bitcast_fusion), calls=%async_computation | async-start | bytes 6291456 | tf_op jit(solution)/shard_map/all_to_all | solution.py:175
  218.3 53.8 %all-to-all-start.1 = ((bf16[8,512,256]{1,2,0:T(8,128)(2,1)}), bf16[8,512,256]{1,2,0:T(8,128)(2,1)}, u32[]{:S(2)}, u32[]{:S(2)}) async-start(bf16[8,512,256]{1,2,0:T(8,128)(2,1)} %copy.56), calls=%async_computation.1 | async-start | bytes 4194304 | tf_op jit(solution)/shard_map/all_to_all | solution.py:175
  222.7 253.9 %all-gather.9.cloned.1.call-start = ((), (), s32[]{:S(2)}) async-start(), calls=%async_computation.10 | async-start | bytes 18874368 | tf_op jit(solution)/shard_map/all_gather | solution.py:214
  285.7 418.4 %reduce-scatter.7.cloned.1.call-start = ((), (), s32[]{:S(2)}) async-start(), calls=%async_computation.13 | async-start | bytes 18874368 | tf_op jit(solution)/shard_map/reduce_scatter | solution.py:218
  317.9 48.6 %collective-permute-start.6 = (bf16[1,256,1024]{1,2,0:T(8,128)(2,1)S(1)}, bf16[1,256,1024]{1,2,0:T(8,128)(2,1)S(1)}, u32[]{:S(2)}, u32[]{:S(2)}) collective-permute-start(bf16[1,256,1024]{1,2,0:T(8,128)(2,1)S(1)} %copy-done.16), channel_id=1, source_target_pairs={{0,7},{1,6},{2,5},{3,4},{4,3},{5,2},{6,1},{7,0},{8,15},{9,14},{10,... | collective-permute-start | bytes 1572872 | tf_op jit(solution)/shard_map/ppermute | solution.py:186
  344.3 56.4 %collective-permute-start.9 = (bf16[1,256,1024]{1,2,0:T(8,128)(2,1)}, bf16[1,256,1024]{1,2,0:T(8,128)(2,1)}, u32[]{:S(2)}, u32[]{:S(2)}) collective-permute-start(bf16[1,256,1024]{1,2,0:T(8,128)(2,1)} %get-tuple-element.73), channel_id=1, source_target_pairs={{0,3},{1,2},{2,1},{3,0},{4,7},{5,6},{6,5},{7,4},{8,11},{9,10},{10,... | collective-permute-start | bytes 1572872 | tf_op jit(solution)/shard_map/ppermute | solution.py:186
  369.0 54.7 %collective-permute-start.12 = (bf16[1,256,1024]{1,2,0:T(8,128)(2,1)S(1)}, bf16[1,256,1024]{1,2,0:T(8,128)(2,1)}, u32[]{:S(2)}, u32[]{:S(2)}) collective-permute-start(bf16[1,256,1024]{1,2,0:T(8,128)(2,1)S(1)} %get-tuple-element.70), channel_id=1, source_target_pairs={{0,6},{1,7},{2,4},{3,5},{4,2},{5,3},{6,0},{7,1},{8,14},{9,15},{10,... | collective-permute-start | bytes 1572872 | tf_op jit(solution)/shard_map/ppermute | solution.py:186
  379.6 65.1 %collective-permute-start.13 = (bf16[1,256,1024]{1,2,0:T(8,128)(2,1)S(1)}, bf16[1,256,1024]{1,2,0:T(8,128)(2,1)}, u32[]{:S(2)}, u32[]{:S(2)}) collective-permute-start(bf16[1,256,1024]{1,2,0:T(8,128)(2,1)S(1)} %get-tuple-element.69), channel_id=1, source_target_pairs={{0,7},{1,6},{2,5},{3,4},{4,3},{5,2},{6,1},{7,0},{8,15},{9,14},{10,... | collective-permute-start | bytes 1572872 | tf_op jit(solution)/shard_map/ppermute | solution.py:186
  585.6 237.8 %reduce-scatter.5.cloned.1.call-start = ((), (), s32[]{:S(2)}) async-start(), calls=%async_computation.11 | async-start | bytes 18874368 | tf_op jit(solution)/shard_map/reduce_scatter | solution.py:218
  609.7 826.4 %reduce-scatter.11.cloned.1.call-start = ((), (), s32[]{:S(2)}) async-start(), calls=%async_computation.15 | async-start | bytes 9437184 | tf_op jit(solution)/shard_map/reduce_scatter | solution.py:218
  944.2 519.7 %reduce-scatter.9.cloned.1.call-start = ((), (), s32[]{:S(2)}) async-start(), calls=%async_computation.14 | async-start | bytes 14155776 | tf_op jit(solution)/shard_map/reduce_scatter | solution.py:218
  970.2 47.5 %collective-permute-start.20 = (bf16[1,256,1024]{2,1,0:T(8,128)(2,1)}, bf16[1,256,1024]{2,1,0:T(8,128)(2,1)}, u32[]{:S(2)}, u32[]{:S(2)}) collective-permute-start(bf16[1,256,1024]{2,1,0:T(8,128)(2,1)} %constant_dynamic-slice_fusion.14), channel_id=1, source_target_pairs={{0,1},{1,0},{2,3},{3,2},{4,5},{5,4},{6,7},{7,6},{8,9},{9,8},{10,11... | collective-permute-start | bytes 1572872 | tf_op jit(solution)/shard_map/ppermute | solution.py:186
  1021.3 51.0 %collective-permute-start.24 = (bf16[1,256,1024]{2,1,0:T(8,128)(2,1)S(1)}, bf16[1,256,1024]{2,1,0:T(8,128)(2,1)S(1)}, u32[]{:S(2)}, u32[]{:S(2)}) collective-permute-start(bf16[1,256,1024]{2,1,0:T(8,128)(2,1)S(1)} %get-tuple-element.55), channel_id=1, source_target_pairs={{0,5},{1,4},{2,7},{3,6},{4,1},{5,0},{6,3},{7,2},{8,13},{9,12},{10,... | collective-permute-start | bytes 1572872 | tf_op jit(solution)/shard_map/ppermute | solution.py:186
  1022.8 64.1 %collective-permute-start.25 = (bf16[1,256,1024]{2,1,0:T(8,128)(2,1)S(1)}, bf16[1,256,1024]{2,1,0:T(8,128)(2,1)S(1)}, u32[]{:S(2)}, u32[]{:S(2)}) collective-permute-start(bf16[1,256,1024]{2,1,0:T(8,128)(2,1)S(1)} %get-tuple-element.54), channel_id=1, source_target_pairs={{0,6},{1,7},{2,4},{3,5},{4,2},{5,3},{6,0},{7,1},{8,14},{9,15},{10,... | collective-permute-start | bytes 1572872 | tf_op jit(solution)/shard_map/ppermute | solution.py:186
  1047.4 120.0 %collective-permute-start.40 = (bf16[1024,2048]{1,0:T(8,128)(2,1)S(1)}, bf16[1024,2048]{1,0:T(8,128)(2,1)S(1)}, u32[]{:S(2)}, u32[]{:S(2)}) collective-permute-start(bf16[1024,2048]{1,0:T(8,128)(2,1)S(1)} %get-tuple-element.94), channel_id=1, source_target_pairs={{0,8},{24,16},{1,9},{25,17},{2,10},{26,18},{3,11},{27,19},{4,12},{... | collective-permute-start | bytes 12582920 | tf_op jit(solution)/shard_map/ppermute | solution.py:198
  1065.3 47.3 %collective-permute-start.31 = (bf16[1,256,1024]{2,1,0:T(8,128)(2,1)S(1)}, bf16[1,256,1024]{2,1,0:T(8,128)(2,1)S(1)}, u32[]{:S(2)}, u32[]{:S(2)}) collective-permute-start(bf16[1,256,1024]{2,1,0:T(8,128)(2,1)S(1)} %get-tuple-element.51), channel_id=1, source_target_pairs={{0,2},{1,3},{2,0},{3,1},{4,6},{5,7},{6,4},{7,5},{8,10},{9,11},{10,... | collective-permute-start | bytes 1572872 | tf_op jit(solution)/shard_map/ppermute | solution.py:186
  1072.4 59.6 %collective-permute-start.32 = (bf16[1,256,1024]{2,1,0:T(8,128)(2,1)S(1)}, bf16[1,256,1024]{2,1,0:T(8,128)(2,1)S(1)}, u32[]{:S(2)}, u32[]{:S(2)}) collective-permute-start(bf16[1,256,1024]{2,1,0:T(8,128)(2,1)S(1)} %get-tuple-element.50), channel_id=1, source_target_pairs={{0,3},{1,2},{2,1},{3,0},{4,7},{5,6},{6,5},{7,4},{8,11},{9,10},{10,... | collective-permute-start | bytes 1572872 | tf_op jit(solution)/shard_map/ppermute | solution.py:186
  1132.6 98.9 %collective-permute-start.27 = (bf16[8,256,1024]{2,1,0:T(8,128)(2,1)S(1)}, bf16[8,256,1024]{2,1,0:T(8,128)(2,1)}, u32[]{:S(2)}, u32[]{:S(2)}) collective-permute-start(bf16[8,256,1024]{2,1,0:T(8,128)(2,1)S(1)} %constant_dynamic-update-slice_fusion.7), channel_id=1, source_target_pairs={{0,8},{24,16},{1,9},{25,17},{2,10},{26,18},{3,11},{27,19},{4,12},{... | collective-permute-start | bytes 12582920 | tf_op jit(solution)/shard_map/ppermute | solution.py:198
  1162.1 158.5 %collective-permute-start.37 = (bf16[8,256,1024]{2,1,0:T(8,128)(2,1)S(1)}, bf16[8,256,1024]{2,1,0:T(8,128)(2,1)}, u32[]{:S(2)}, u32[]{:S(2)}) collective-permute-start(bf16[8,256,1024]{2,1,0:T(8,128)(2,1)S(1)} %constant_dynamic-update-slice_fusion), channel_id=1, source_target_pairs={{0,8},{24,16},{1,9},{25,17},{2,10},{26,18},{3,11},{27,19},{4,12},{... | collective-permute-start | bytes 12582920 | tf_op jit(solution)/shard_map/ppermute | solution.py:198
  1175.5 150.3 %collective-permute-start.41 = (bf16[1024,2048]{1,0:T(8,128)(2,1)S(1)}, bf16[1024,2048]{1,0:T(8,128)(2,1)}, u32[]{:S(2)}, u32[]{:S(2)}) collective-permute-start(bf16[1024,2048]{1,0:T(8,128)(2,1)S(1)} %add_convert_fusion.2), channel_id=1, source_target_pairs={{8,16},{16,8},{9,17},{17,9},{10,18},{18,10},{11,19},{19,11},{12,20... | collective-permute-start | bytes 12582920 | tf_op jit(solution)/shard_map/ppermute | solution.py:200
  1235.8 97.4 %collective-permute-start.28 = (bf16[8,256,1024]{2,1,0:T(8,128)(2,1)S(1)}, bf16[8,256,1024]{2,1,0:T(8,128)(2,1)S(1)}, u32[]{:S(2)}, u32[]{:S(2)}) collective-permute-start(bf16[8,256,1024]{2,1,0:T(8,128)(2,1)S(1)} %add_convert_fusion.6), channel_id=1, source_target_pairs={{8,16},{16,8},{9,17},{17,9},{10,18},{18,10},{11,19},{19,11},{12,20... | collective-permute-start | bytes 12582920 | tf_op jit(solution)/shard_map/ppermute | solution.py:200
  1331.9 98.1 %collective-permute-start.42 = (bf16[1024,2048]{1,0:T(8,128)(2,1)}, bf16[1024,2048]{1,0:T(8,128)(2,1)}, u32[]{:S(2)}, u32[]{:S(2)}) collective-permute-start(bf16[1024,2048]{1,0:T(8,128)(2,1)} %add_convert_fusion.1), channel_id=1, source_target_pairs={{8,0},{16,24},{9,1},{17,25},{10,2},{18,26},{11,3},{19,27},{12,4},{... | collective-permute-start | bytes 12582920 | tf_op jit(solution)/shard_map/ppermute | solution.py:202
  1337.5 182.5 %collective-permute-start.29 = (bf16[8,256,1024]{2,1,0:T(8,128)(2,1)}, bf16[8,256,1024]{2,1,0:T(8,128)(2,1)}, u32[]{:S(2)}, u32[]{:S(2)}) collective-permute-start(bf16[8,256,1024]{2,1,0:T(8,128)(2,1)} %add_convert_fusion.5), channel_id=1, source_target_pairs={{8,0},{16,24},{9,1},{17,25},{10,2},{18,26},{11,3},{19,27},{12,4},{... | collective-permute-start | bytes 12582920 | tf_op jit(solution)/shard_map/ppermute | solution.py:202
  1343.0 265.1 %collective-permute-start.39 = (bf16[8,256,1024]{2,1,0:T(8,128)(2,1)}, bf16[8,256,1024]{2,1,0:T(8,128)(2,1)}, u32[]{:S(2)}, u32[]{:S(2)}) collective-permute-start(bf16[8,256,1024]{2,1,0:T(8,128)(2,1)} %add_convert_fusion.3), channel_id=1, source_target_pairs={{8,0},{16,24},{9,1},{17,25},{10,2},{18,26},{11,3},{19,27},{12,4},{... | collective-permute-start | bytes 12582920 | tf_op jit(solution)/shard_map/ppermute | solution.py:202
  1436.2 184.5 %collective-permute-start.17 = (bf16[256,2048]{1,0:T(8,128)(2,1)}, bf16[256,2048]{1,0:T(8,128)(2,1)}, u32[]{:S(2)}, u32[]{:S(2)}) collective-permute-start(bf16[256,2048]{1,0:T(8,128)(2,1)} %reduce-scatter.11.cloned.1.call-done), channel_id=1, source_target_pairs={{0,8},{24,16},{1,9},{25,17},{2,10},{26,18},{3,11},{27,19},{4,12},{... | collective-permute-start | bytes 3145736 | tf_op jit(solution)/shard_map/ppermute | solution.py:198
  1463.9 160.4 %collective-permute-start.14 = (bf16[256,3072]{1,0:T(8,128)(2,1)}, bf16[256,3072]{1,0:T(8,128)(2,1)S(1)}, u32[]{:S(2)}, u32[]{:S(2)}) collective-permute-start(bf16[256,3072]{1,0:T(8,128)(2,1)} %reduce-scatter.9.cloned.1.call-done), channel_id=1, source_target_pairs={{0,8},{24,16},{1,9},{25,17},{2,10},{26,18},{3,11},{27,19},{4,12},{... | collective-permute-start | bytes 4718600 | tf_op jit(solution)/shard_map/ppermute | solution.py:198
  1622.5 79.2 %collective-permute-start.18 = (bf16[256,2048]{1,0:T(8,128)(2,1)S(1)}, bf16[256,2048]{1,0:T(8,128)(2,1)}, u32[]{:S(2)}, u32[]{:S(2)}) collective-permute-start(bf16[256,2048]{1,0:T(8,128)(2,1)S(1)} %add_convert_fusion.12), channel_id=1, source_target_pairs={{8,16},{16,8},{9,17},{17,9},{10,18},{18,10},{11,19},{19,11},{12,20... | collective-permute-start | bytes 3145736 | tf_op jit(solution)/shard_map/ppermute | solution.py:200
  1626.0 78.9 %collective-permute-start.15 = (bf16[256,3072]{1,0:T(8,128)(2,1)}, bf16[256,3072]{1,0:T(8,128)(2,1)}, u32[]{:S(2)}, u32[]{:S(2)}) collective-permute-start(bf16[256,3072]{1,0:T(8,128)(2,1)} %add_convert_fusion.9), channel_id=1, source_target_pairs={{8,16},{16,8},{9,17},{17,9},{10,18},{18,10},{11,19},{19,11},{12,20... | collective-permute-start | bytes 4718600 | tf_op jit(solution)/shard_map/ppermute | solution.py:200
  1707.4 55.9 %collective-permute-start.16 = (bf16[256,3072]{1,0:T(8,128)(2,1)S(1)}, bf16[256,3072]{1,0:T(8,128)(2,1)S(1)}, u32[]{:S(2)}, u32[]{:S(2)}) collective-permute-start(bf16[256,3072]{1,0:T(8,128)(2,1)S(1)} %add_convert_fusion.8), channel_id=1, source_target_pairs={{8,0},{16,24},{9,1},{17,25},{10,2},{18,26},{11,3},{19,27},{12,4},{... | collective-permute-start | bytes 4718600 | tf_op jit(solution)/shard_map/ppermute | solution.py:202
  (56 other events, 1510.0 us)
Sparse Core Ops, SparseCore 0:
  16.2 77.2 all-gather.4
  95.3 80.5 all-gather.6
  177.8 112.3 all-gather.10
  292.5 168.4 all-gather.8
  585.7 118.2 reduce-scatter.6
  707.4 115.9 reduce-scatter.4
  840.3 84.8 reduce-scatter.10
  994.6 171.6 reduce-scatter.8

commit v2 on v1

--- a/solution.py
+++ b/solution.py
@@ -171,36 +171,372 @@
     )(*args)
 
 
+def chip_at(chip, distance):
+    result, bit = chip, 1
+    while bit <= distance:
+        if distance & bit:
+            result = result + bit * (1 - 2 * ((chip // bit) % 2))
+        bit *= 2
+    return result
+
+
+def pieces_of(chips):
+    if chips == 4:
+        return [[(0, 0), (0, 1)], [(1, 0), (2, 0)], [(1, 1), (2, 1)], [(3, 0), (3, 1)]]
+    return [[(d, 0), (d, 1)] for d in range(chips)]
+
+
+def feed_kernel(
+    normed_ref, cot_ref, own_ref, other_ref, down_own_ref, down_other_ref,
+    partial_ref, out_ref, mixed_ref, gate_ref, up_ref,
+    down_own_out, gate_own_out, up_own_out, down_got, gate_got, up_got,
+    weights, normed, cot, inner, sent, out_stage,
+    weight_sem, normed_send, normed_recv, cot_sem, inner_sem, sum_send, sum_recv, own_sem, out_sem,
+    core_send, core_recv, core_sem, load_sem,
+):
+    chips, rows, width = normed.shape
+    units = mixed_ref.shape[1]
+    half_rows, half_units = rows // 2, units // 2
+    replicas, _, _, share, _ = own_ref.shape
+    me = lax.axis_index("shard")
+    replica = lax.axis_index("replica")
+    chip, core = me // 2, me % 2
+    sibling = chip * 2 + (1 - core)
+    partner = [chip_at(chip, d) * 2 + core for d in range(chips)]
+    steps = pieces_of(chips)
+
+    def remote(source, target, send, recv, shard):
+        return pltpu.make_async_remote_copy(
+            src_ref=source, dst_ref=target, send_sem=send, recv_sem=recv,
+            device_id=(replica, shard), device_id_type=pl.DeviceIdType.MESH,
+        )
+
+    barrier = pltpu.get_barrier_semaphore()
+    for shard in partner[1:] + [sibling]:
+        pl.semaphore_signal(
+            barrier, inc=1, device_id=(replica, shard), device_id_type=pl.DeviceIdType.MESH
+        )
+    pl.semaphore_wait(barrier, chips)
+
+    def half(index):
+        return pl.ds(index * half_rows, half_rows)
+
+    def token_copy(distance, part, source, target):
+        return remote(
+            source, normed.at[distance, half(part)],
+            normed_send.at[distance, part], normed_recv.at[distance, part], target,
+        )
+
+    relay = chips == 4
+    direct = range(1, 3) if relay else range(1, chips)
+    for part in range(2):
+        for d in direct:
+            token_copy(d, part, normed_ref.at[half(part)], partner[d]).start()
+    own_copy = pltpu.make_async_copy(normed_ref, normed.at[0], own_sem.at[0])
+    own_copy.start()
+
+    def cot_copies(index):
+        return [
+            pltpu.make_async_copy(
+                cot_ref.at[chip_at(chip, d), half(part)], cot.at[index % 2, half(at)],
+                cot_sem.at[index % 2, at],
+            )
+            for at, (d, part) in enumerate(steps[index])
+        ]
+
+    for copy in cot_copies(0):
+        copy.start()
+    owned = share * replicas
+    for which in range(2):
+        for k in range(chips):
+            for z in range(replicas):
+                for ref, c in ((own_ref, core), (other_ref, 1 - core)):
+                    pltpu.make_async_copy(
+                        ref.at[z, which, k],
+                        weights.at[which, pl.ds((2 * k + c) * owned + z * share, share), pl.ds(0, units)],
+                        weight_sem.at[which],
+                    ).start()
+    down_own = pltpu.make_async_copy(
+        down_own_ref, weights.at[2, pl.ds(core * half_units, half_units)], weight_sem.at[2]
+    )
+    down_other = pltpu.make_async_copy(
+        down_other_ref, weights.at[2, pl.ds((1 - core) * half_units, half_units)], weight_sem.at[3]
+    )
+    down_own.start()
+    down_other.start()
+    own_copy.wait()
+    for which in range(2):
+        whole = weights.at[which, pl.ds(0, width), pl.ds(0, units)]
+        pltpu.make_async_copy(whole, whole, weight_sem.at[which]).wait()
+    down_own.wait()
+    down_other.wait()
+
+    def inner_copies(index):
+        return [
+            pltpu.make_async_copy(
+                inner.at[which, half(at), pl.ds(0, units)],
+                ref.at[pl.ds(d * rows + part * half_rows, half_rows)],
+                inner_sem.at[which, at],
+            )
+            for at, (d, part) in enumerate(steps[index])
+            for which, ref in enumerate((mixed_ref, gate_ref, up_ref))
+        ]
+
+    def out_copies(index):
+        return [
+            pltpu.make_async_copy(
+                out_stage.at[half(at)], out_ref.at[chip_at(chip, d), half(part)], out_sem.at[at]
+            )
+            for at, (d, part) in enumerate(steps[index])
+        ]
+
+    def sum_copy(index, at):
+        d, part = steps[index][at]
+        return remote(
+            sent.at[index % (chips - 1), half(at)], partial_ref.at[d, half(part)],
+            sum_send.at[d, part], sum_recv.at[d, part], partner[d],
+        )
+
+    own_sums = [
+        pltpu.make_async_copy(sent.at[0, half(at)], partial_ref.at[0, half(at)], own_sem.at[1 + at])
+        for at in range(2)
+    ]
+    tile = min(512, units)
+    for index in range(chips):
+        parts = steps[index]
+        for d, part in parts:
+            if d > 0:
+                if relay and d == 3:
+                    source, way = (1, 2) if part == 0 else (2, 1)
+                    copy = token_copy(3, part, normed.at[source, half(part)], partner[way])
+                else:
+                    copy = token_copy(d, part, normed_ref.at[half(part)], partner[d])
+                copy.wait_recv()
+        if relay and index in (1, 2):
+            part, source, way = (0, 1, 2) if index == 1 else (1, 2, 1)
+            token_copy(3, part, normed.at[source, half(part)], partner[way]).start()
+        for copy in cot_copies(index):
+            copy.wait()
+        if index + 1 < chips:
+            for copy in cot_copies(index + 1):
+                copy.start()
+        if index > 0:
+            for copy in inner_copies(index - 1):
+                copy.wait()
+        (d0, p0), (d1, p1) = parts
+
+        @pl.loop(0, units // tile)
+        def _(j):
+            columns = pl.ds(pl.multiple_of(j * tile, tile), tile)
+            if d0 == d1:
+                block = normed[d0]
+            else:
+                block = jnp.concatenate([normed[d0, half(p0)], normed[d1, half(p1)]], 0)
+            gate = dot_nn(block, weights[0, :width, columns])
+            up = dot_nn(block, weights[1, :width, columns])
+            grad = dot_nt(cot[index % 2], weights[2, columns, :])
+            sigmoid = jax.nn.sigmoid(gate)
+            swish = gate * sigmoid
+            inner[0, :, columns] = (swish * up).astype(bf16)
+            inner[1, :, columns] = (grad * up * (sigmoid + swish * (1.0 - sigmoid))).astype(bf16)
+            inner[2, :, columns] = (grad * swish).astype(bf16)
+
+        for copy in inner_copies(index):
+            copy.start()
+        if index > 0:
+            for copy in out_copies(index - 1):
+                copy.wait()
+        slot = index % (chips - 1)
+        if index == chips - 1:
+            for copy in own_sums:
+                copy.wait()
+
+        @pl.loop(0, width // 512)
+        def _(j):
+            columns = pl.ds(pl.multiple_of(j * 512, 512), 512)
+            sent[slot, :, columns] = (
+                dot_nt(inner[1, :, :units], weights[0, columns, :units])
+                + dot_nt(inner[2, :, :units], weights[1, columns, :units])
+            ).astype(bf16)
+
+        if index == 0:
+            for copy in own_sums:
+                copy.start()
+        else:
+            for at in range(2):
+                sum_copy(index, at).start()
+
+        @pl.loop(0, width // 512)
+        def _(j):
+            columns = pl.ds(pl.multiple_of(j * 512, 512), 512)
+            out_stage[:, columns] = dot_nn(
+                inner[0, :, :units], weights[2, :units, columns]
+            ).astype(bf16)
+
+        for copy in out_copies(index):
+            copy.start()
+
+    for copy in inner_copies(chips - 1):
+        copy.wait()
+    for copy in out_copies(chips - 1):
+        copy.wait()
+
+    tokens = chips * rows
+
+    def load(ref, which):
+        return pltpu.make_async_copy(
+            ref, weights.at[which, pl.ds(0, tokens), pl.ds(0, units)], load_sem.at[which]
+        )
+
+    loads = [load(mixed_ref, 0), load(gate_ref, 1)]
+    cot_loads = [
+        pltpu.make_async_copy(
+            cot_ref.at[chip_at(chip, d)], weights.at[2, pl.ds(d * rows, rows)], load_sem.at[3 + d]
+        )
+        for d in range(chips)
+    ]
+    for copy in loads + cot_loads:
+        copy.start()
+    for copy in cot_loads + loads:
+        copy.wait()
+    tiles = width // rows
+    per_slot = width // half_units
+
+    def stage_copies(which, owner, stage, local, landing):
+        result = []
+        for t in range(tiles):
+            if which == 0:
+                if t >= half_units // rows:
+                    break
+                source, place = stage.at[t], (pl.ds(t * rows, rows),)
+            else:
+                source = stage.at[t // per_slot, :, pl.ds((t % per_slot) * half_units, half_units)]
+                place = (pl.ds(t * rows, rows),)
+            if owner == 0:
+                result.append(
+                    remote(
+                        source, landing.at[place], core_send.at[which, t], core_recv.at[which, t],
+                        sibling,
+                    )
+                )
+            else:
+                result.append(
+                    pltpu.make_async_copy(source, local.at[place], core_sem.at[which, t])
+                )
+        return result
+
+    outs = ((down_own_out, down_got), (gate_own_out, gate_got), (up_own_out, up_got))
+    started = {}
+    for which in range(3):
+        if which == 2:
+            copy = load(up_ref, 1)
+            copy.start()
+            copy.wait()
+        for owner in range(2):
+            stage = cot if owner == 0 else inner
+            first = ((1 - core) if owner == 0 else core) * half_units
+            copies = stage_copies(which, owner, stage, *outs[which])
+            started[which, owner] = copies
+            if which > 0:
+                for copy in started[which - 1, owner]:
+                    if owner == 0:
+                        copy.wait_send()
+                    else:
+                        copy.wait()
+            for t, copy in enumerate(copies):
+                if which == 0:
+                    left = weights[0, :tokens, pl.ds(pl.multiple_of(first + t * rows, rows), rows)]
+                    for j in range(width // 1024):
+                        columns = pl.ds(j * 1024, 1024)
+                        stage[t, :, columns] = lax.dot_general(
+                            left, weights[2, :tokens, columns], (((0,), (0,)), ((), ())),
+                            preferred_element_type=f32,
+                        ).astype(bf16)
+                else:
+                    left = normed[:, :, t * rows : (t + 1) * rows].reshape(tokens, rows)
+                    right = weights[1, :tokens, pl.ds(pl.multiple_of(first, half_units), half_units)]
+                    stage[t // per_slot, :, pl.ds((t % per_slot) * half_units, half_units)] = (
+                        lax.dot_general(
+                            left, right, (((0,), (0,)), ((), ())), preferred_element_type=f32
+                        ).astype(bf16)
+                    )
+                copy.start()
+    for owner in range(2):
+        for copy in started[2, owner]:
+            if owner == 0:
+                copy.wait_send()
+            else:
+                copy.wait()
+    for which in range(3):
+        for copy in started[which, 0]:
+            copy.wait_recv()
+    for index in range(1, chips):
+        for at in range(2):
+            sum_copy(index, at).wait_send()
+            sum_copy(index, at).wait_recv()
+    for d in range(1, chips):
+        for part in range(2):
+            if relay and d == 3:
+                source, way = (1, 2) if part == 0 else (2, 1)
+                token_copy(3, part, normed.at[source, half(part)], partner[way]).wait_send()
+            else:
+                token_copy(d, part, normed_ref.at[half(part)], partner[d]).wait_send()
+
+
+def feed_forward(normed, cot, own, other, down_own, down_other):
+    chips, rows, width = cot.shape
+    units = down_own.shape[0] * 2
+    half = units // 2
+    tokens = chips * rows
+    tiles = width // rows
+    hbm = pl.BlockSpec(memory_space=pl.ANY)
+    dma = pltpu.SemaphoreType.DMA
+
+    def low(*shape):
+        return jax.ShapeDtypeStruct(shape, bf16)
+
+    out_shape = (
+        low(chips, rows, width), low(chips, rows, width),
+        low(tokens, units), low(tokens, units), low(tokens, units),
+        low(half, width), low(width, half), low(width, half),
+        low(half, width), low(width, half), low(width, half),
+    )
+    depth = max(width, tokens)
+    return pl.pallas_call(
+        feed_kernel,
+        in_specs=[hbm] * 6,
+        out_specs=(hbm,) * len(out_shape),
+        out_shape=out_shape,
+        scratch_shapes=[
+            pltpu.VMEM((3, depth, width), bf16),
+            pltpu.VMEM((chips, rows, width), bf16),
+            pltpu.VMEM((2, rows, width), bf16),
+            pltpu.VMEM((3, rows, width), bf16),
+            pltpu.VMEM((chips - 1, rows, width), bf16),
+            pltpu.VMEM((rows, width), bf16),
+            dma((4,)), dma((chips, 2)), dma((chips, 2)), dma((2, 2)), dma((3, 2)),
+            dma((chips, 2)), dma((chips, 2)), dma((3,)), dma((2,)),
+            dma((3, tiles)), dma((3, tiles)), dma((3, tiles)), dma((3 + chips,)),
+        ],
+        compiler_params=pltpu.CompilerParams(
+            collective_id=0, has_side_effects=True, vmem_limit_bytes=63 * 2**20
+        ),
+        cost_estimate=pl.CostEstimate(
+            flops=18 * tokens * units * width, bytes_accessed=2**27, transcendentals=tokens * units
+        ),
+    )(normed, cot, own, other, down_own, down_other)
+
+
 def exchange(blocks):
     return lax.all_to_all(blocks, "shard", 0, 0, tiled=True)
 
 
-def exchange_async(blocks):
-    count = blocks.shape[0]
-    me = lax.axis_index("shard")
-    result = blocks
-    for step in range(1, count):
-        pairs = [(i, i ^ step) for i in range(count)]
-        partner = me ^ step
-        sent = lax.dynamic_index_in_dim(blocks, partner, 0, keepdims=True)
-        got = lax.ppermute(sent, "shard", pairs)
-        result = lax.dynamic_update_slice_in_dim(result, got, partner, 0)
-    return result
+def tie(*values):
+    return lax.optimization_barrier(values)
 
 
 def replica_sum(part):
-    count = lax.axis_size("replica")
-    if count != 4:
-        return lax.psum(part.astype(bf16), "replica").astype(f32)
-    me = lax.axis_index("replica")
-    inner = (me == 1) | (me == 2)
-    low = part.astype(bf16)
-    inward = lax.ppermute(low, "replica", [(0, 1), (3, 2)])
-    half = (part.astype(f32) + inward.astype(f32)).astype(bf16)
-    other = lax.ppermute(half, "replica", [(1, 2), (2, 1)])
-    whole = (half.astype(f32) + other.astype(f32)).astype(bf16)
-    outward = lax.ppermute(whole, "replica", [(1, 0), (2, 3)])
-    return jnp.where(inner, whole, outward).astype(f32)
+    return lax.psum(part.astype(bf16), "replica").astype(f32)
 
 
 def norm_back(grad_normed, unit_rows, scale_rows, gain_rows):
@@ -278,6 +614,24 @@
     qkv_rows = jnp.concatenate([turned, projected[:, :, wide + HEAD_DIM :]], -1).astype(bf16)
     qkv = exchange(jnp.swapaxes(qkv_rows, 0, 1)).reshape(shards, seqs, span, part)
 
+    chips = shards // 2
+    same_core = [[2 * k + c for k in range(chips)] for c in range(2)]
+    swap = [(i, i + 1 - 2 * (i % 2)) for i in range(shards)]
+    units = 2 * hidden_share
+    share = owned // lax.axis_size("replica")
+    gate_up_own = lax.dynamic_slice_in_dim(
+        jnp.stack([gate_weight, up_weight]), lax.axis_index("replica") * share, share, 1
+    )
+    gate_up_own = jnp.transpose(gate_up_own.reshape(2, share, chips, units), (0, 2, 1, 3))
+    gate_up_part = lax.all_to_all(
+        gate_up_own, "shard", 1, 1, axis_index_groups=same_core, tiled=True
+    )
+    gate_up = lax.all_gather(gate_up_part, "replica")
+    gate_up_other = lax.ppermute(gate_up, "shard", swap)
+    down_other = lax.ppermute(down_weight, "shard", swap)
+    cot_rows = cotangent.reshape(rows, width)
+    cot_all = lax.all_gather(cot_rows, "shard", axis_index_groups=same_core)
+
     attn_heads, norms = attention_forward(heads, qkv, seg_col, seg_row)
     attn = exchange(attn_heads.reshape(shards, rows, wide))
     attn = jnp.swapaxes(attn, 0, 1).reshape(rows, HEADS * HEAD_DIM)
@@ -286,47 +640,46 @@
     unit_two = hidden * scale_two
     normed_two = (unit_two * gain_two).astype(bf16)
 
-    def to_columns(weight):
-        blocks = jnp.swapaxes(weight.reshape(owned, shards, hidden_share), 0, 1)
-        return exchange_async(blocks).reshape(shards * owned, hidden_share)
-
-    gate_columns, up_columns = to_columns(gate_weight), to_columns(up_weight)
-    cot_rows = cotangent.reshape(rows, width)
-    cot_all = gather(cot_rows)
-    normed_all = gather(normed_two)
-    gate = dot_nn(normed_all, gate_columns)
-    up = dot_nn(normed_all, up_columns)
-    grad_mixed = dot_nt(cot_all, down_weight)
-    sigmoid = jax.nn.sigmoid(gate)
-    swish = gate * sigmoid
-    mixed = (swish * up).astype(bf16)
-    grad_gate = (grad_mixed * up * (sigmoid + swish * (1.0 - sigmoid))).astype(bf16)
-    grad_up = (grad_mixed * swish).astype(bf16)
-    grad_two = scatter(dot_nt(grad_gate, gate_columns) + dot_nt(grad_up, up_columns))
-    down_grad = replica_sum(outer_sum(mixed, cot_all))
-
-    def to_rows(grad):
-        blocks = exchange_async(grad.astype(bf16).reshape(shards, owned, hidden_share))
-        summed = replica_sum(blocks)
-        return jnp.swapaxes(summed, 0, 1).reshape(owned, shards * hidden_share)
-
-    gate_grad = to_rows(outer_sum(normed_all, grad_gate))
-    up_grad = to_rows(outer_sum(normed_all, grad_up))
-    block_out = (hidden + scatter(dot_nn(mixed, down_weight))).astype(bf16)
+    partials, outs, _, _, _, down_one, gate_one, up_one, down_two, gate_two, up_two = feed_forward(
+        normed_two, cot_all, gate_up, gate_up_other, down_weight, down_other
+    )
+    grad_two = jnp.sum(partials.astype(f32), 0)
+    out_sum = lax.psum_scatter(
+        outs, "shard", scatter_dimension=0, axis_index_groups=same_core, tiled=False
+    ).astype(f32)
+
+    def added(one, two):
+        return (one.astype(f32) + two.astype(f32)).astype(bf16)
+
+    down_grad = lax.psum(added(down_one, down_two), "replica")
+    gate_part = exchange(added(gate_one, gate_two).reshape(shards, owned, hidden_share))
+    up_part = exchange(added(up_one, up_two).reshape(shards, owned, hidden_share))
+    block_out = (hidden + out_sum).astype(bf16)
+
+    def to_rows(summed):
+        return jnp.swapaxes(summed, 0, 1).reshape(owned, shards * hidden_share).astype(f32)
 
     second_grad = jnp.sum(grad_two * unit_two, 0)
     grad_hidden = cot_rows.astype(f32) + norm_back(grad_two, unit_two, scale_two, gain_two)
     branch = grad_hidden.astype(bf16)
     grad_attn = dot_nt(branch, output_full).astype(bf16).reshape(rows, shards, wide)
     grad_heads = exchange(jnp.swapaxes(grad_attn, 0, 1)).reshape(shards, seqs, span, wide)
-    output_grad = replica_sum(scatter(outer_sum(attn, branch)))
+    output_sum = scatter(outer_sum(attn, branch))
+    grad_heads, gate_part, up_part = tie(grad_heads, gate_part, up_part)
+    gate_part, down_grad = tie(gate_part, down_grad)
+    gate_sum = lax.psum(gate_part, "replica")
+    up_part, gate_sum = tie(up_part, gate_sum)
+    up_sum = lax.psum(up_part, "replica")
     grad_qkv = attention_backward(
         heads, qkv, grad_heads, norms, seg_col, seg_row, cos_all, sin_all
     )
     grad_qkv = exchange(grad_qkv.reshape(shards, rows, part))
     grad_qkv = jnp.swapaxes(grad_qkv, 0, 1).reshape(rows, shards * part)
     grad_one = dot_nt(grad_qkv, qkv_full)
-    qkv_grad = replica_sum(scatter(outer_sum(normed_one, grad_qkv)))
+    qkv_sum = scatter(outer_sum(normed_one, grad_qkv))
+    qkv_sum, gate_sum, output_sum, up_sum = tie(qkv_sum, gate_sum, output_sum, up_sum)
+    output_grad = replica_sum(output_sum)
+    qkv_grad = replica_sum(qkv_sum)
     qkv_grad = qkv_grad.reshape(owned, shards, part)
 
     def kv_grad(columns):
@@ -350,9 +703,9 @@
         value_grad,
         output_grad,
         gain_grads[1],
-        gate_grad,
-        up_grad,
-        down_grad,
+        to_rows(gate_sum),
+        to_rows(up_sum),
+        down_grad.astype(f32),
     )
 
 

time: 1790 us -> 1630 us (0.911)
  matrix products: 289 us -> 60.5 us
  Pallas kernels: 78.7 us -> 289 us
  waiting for transfers between devices: 982 us -> 876 us
  blocking collectives: 128 us -> 222 us
  starting transfers between devices: 99.5 us -> 19.5 us
  local copies, waits for them, and re-layouts: 107 us -> 54.6 us
    ppermute x43 -> x2, waiting for transfers between devices: 611 us -> 0.01 us  [the longest x1 0.01 us: body(): down_other = lax.ppermute(down_weight, 'shard', swap)]
    psum x0 -> x4, waiting for transfers between devices: none -> 324 us  [the longest x1 156 us: body(): gate_sum = lax.psum(gate_part, 'replica')]
    pallas_call x0 -> x1, Pallas kernels: none -> 211 us  [feed_forward(): pl.pallas_call(feed_kernel, in_specs=[hbm] * 6, out_specs=(hbm,) * len(ou...]
    all_gather x0 -> x2, waiting for transfers between devices: none -> 134 us  [the longest x1 130 us: body(): gate_up = lax.all_gather(gate_up_part, 'replica')]
    all_to_all x0 -> x3, blocking collectives: none -> 113 us  [the longest x2 83 us: exchange(): return lax.all_to_all(blocks, 'shard', 0, 0, tiled=True)]
    dot_general x5 -> x2, matrix products: 100 us -> 17.8 us  [dot_nn(): lax.dot_general(left, right, (((1,), (0,)), ((), ())), preferred_element_...]
    ppermute x43 -> x2, starting transfers between devices: 81.7 us -> 0.45 us  [the longest x1 0.4 us: body(): down_other = lax.ppermute(down_weight, 'shard', swap)]
    dot_general x5 -> x2, matrix products: 96.6 us -> 22.1 us  [dot_nt(): lax.dot_general(left, right, (((1,), (1,)), ((), ())), preferred_element_...]
  transfers between devices with their start and end apart: 55 -> 17, of which waited for: 31 -> 12; matrix products, arithmetic and copies ran while one was open for 18% -> 10% of each run, Pallas kernels for 4% -> 5%
where the time goes in v2:
time: 1630 us; the launch traced here: 1620 us
  waiting for transfers between devices  876 us (54%)
  Pallas kernels  289 us (18%)
  blocking collectives  222 us (14%)
  other arithmetic  80.6 us (5%)
  matrix products  60.5 us (4%)
  local copies, waits for them, and re-layouts  54.6 us (3%)
  starting transfers between devices  19.5 us (1%)
    pallas_call x1, Pallas kernels, feed_forward(): pl.pallas_call(feed_kernel, in_specs=[hbm] * 6, out_specs=(hbm,) * len(ou...  211 us
    reduce_scatter x2, waiting for transfers between devices, scatter(): lax.psum_scatter(partial.astype(bf16), 'shard', scatter_dimension=0, tile...  171 us
    psum x1, waiting for transfers between devices, body(): gate_sum = lax.psum(gate_part, 'replica')  156 us
    all_gather x1, waiting for transfers between devices, body(): gate_up = lax.all_gather(gate_up_part, 'replica')  130 us
    all_to_all x4, waiting for transfers between devices, exchange(): return lax.all_to_all(blocks, 'shard', 0, 0, tiled=True)  128 us
    psum x1, waiting for transfers between devices, body(): down_grad = lax.psum(added(down_one, down_two), 'replica')  112 us
    all_to_all x2, blocking collectives, exchange(): return lax.all_to_all(blocks, 'shard', 0, 0, tiled=True)  83 us
    all_gather x2, waiting for transfers between devices, gather(): return lax.all_gather(block, 'shard', axis=0, tiled=True)  75.2 us
  transfers between devices with their start and end apart: 17, of which 12 were waited for; matrix products, arithmetic and copies ran while one was open for 10% of the time, Pallas kernels for 5%

profile of v2, /device:TPU:0, one launch (start us, length us, event | category | flops | bytes accessed | tf_op | source)
XLA Modules:
  0.0 1617.7 jit_solution(44578960865946997)
XLA Ops:
  14.8 30.3 %all_to_all.35 = bf16[2,4,64,2048]{3,2,0,1:T(8,128)(2,1)S(1)} all-to-all(bf16[2,4,64,2048]{3,2,0,1:T(8,128)(2,1)S(1)} %copy.58), channel_id=1, replica_groups={{0,2,4,6},{1,3,5,7},{8,10,12,14},{9,11,13,15},{16,18,20,22},{17,19,21,2..., dimensions={1} | all-to-all | bytes 4194304 | tf_op jit(solution)/shard_map/all_to_all | solution.py:626
  53.8 8.3 all_gather.21
  66.0 130.1 %all-gather.12.cloned.1.call-done = bf16[8,4,64,2048]{3,2,1,0:T(8,128)(2,1)} async-done(((bf16[2,4,64,2048]{3,2,1,0:T(8,128)(2,1)}), bf16[8,4,64,2048]{3,2,1,0:T(8,128)(2,1)}) %all-gather.12.cloned.1.call-update) | async-done | bytes 8388624 | tf_op jit(solution)/shard_map/all_gather | solution.py:629
  196.2 75.2 %all-gather.6.cloned.1.call-done = bf16[2048,3072]{0,1:T(8,128)(2,1)} async-done(((bf16[256,3072]{0,1:T(8,128)(2,1)}), bf16[2048,3072]{0,1:T(8,128)(2,1)}) %all-gather.6.cloned.1.call-update) | async-done | bytes 12582928 | tf_op jit(solution)/shard_map/all_gather | solution.py:550
  271.3 10.0 fusion.18
  289.9 56.2 %all_gather.23 = s32[2,4,1024]{2,0,1:T(2,128)S(1)} all-gather(s32[2,4,128]{2,0,1:T(2,128)S(1)} %pad_add_fusion), channel_id=1, replica_groups=mesh['replica'=4,'shard'=8] {'shard'}, dimensions={2}, use_global_device_ids=true | all-gather | bytes 36864 | tf_op jit(solution)/shard_map/all_gather | solution.py:596
  352.6 38.9 %shard_map.212 = (bf16[8,4,128,256]{3,2,1,0:T(8,128)(2,1)S(1)}, f32[4,4,1024]{2,1,0:T(4,128)S(1)}) custom-call(bf16[8,4,128,384]{3,2,1,0:T(8,128)(2,1)} %bitcast.126, s32[4,1024,1]{2,1,0:T(8,128)S(1)} %copy.56.seg_col_ref, s32[4,1,1024]{2,1,0:T(1,128)S(1)} %get-tuple-element.88.seg_row_ref), custom_call_target="tpu_custom_call" | custom-call | flops 4294967296 | bytes 6291456 | tf_op jit(solution)/shard_map/pallas_call | solution.py:135
  402.0 48.8 %all-to-all-done.1 = bf16[8,512,256]{1,2,0:T(8,128)(2,1)} async-done(((bf16[8,512,256]{1,2,0:T(8,128)(2,1)}), bf16[8,512,256]{1,2,0:T(8,128)(2,1)}, u32[]{:S(2)}, u32[]{:S(2)}) %all-to-all-start.1) | async-done | bytes 2097184 | tf_op jit(solution)/shard_map/all_to_all | solution.py:531
  450.7 7.8 multiply_reduce_fusion.2
  465.6 210.8 %shard_map.213 = (bf16[4,512,2048]{2,1,0:T(8,128)(2,1)}, bf16[4,512,2048]{2,1,0:T(8,128)(2,1)}, bf16[2048,2048]{1,0:T(8,128)(2,1)}, bf16[2048,2048]{1,0:T(8,128)...) custom-call(bf16[512,2048]{1,0:T(8,128)(2,1)} %multiply_convert_fusi, ...), custom_call_target="tpu_custom_call" | custom-call | flops 154618822656 | bytes 134217728 | tf_op jit(solution)/shard_map/pallas_call | solution.py:505
  676.4 7.7 add_convert_fusion.1
  688.7 7.9 add_convert_fusion.2
  696.5 79.5 %all-to-all-done.5 = bf16[8,256,1024]{2,1,0:T(8,128)(2,1)} async-done(((bf16[8,256,1024]{2,1,0:T(8,128)(2,1)}), bf16[8,256,1024]{2,1,0:T(8,128)(2,1)}, u32[]{:S(2)}, u32[]{:S(2)}) %all-to-all-start.5) | async-done | bytes 4194336 | tf_op jit(solution)/shard_map/all_to_all | solution.py:531
  780.7 8.4 add_convert_fusion
  797.8 43.6 %reduce-scatter.10.cloned.1.call-done = bf16[1,512,2048]{2,1,0:T(8,128)(2,1)} async-done(((bf16[4,512,2048]{2,1,0:T(8,128)(2,1)}), bf16[1,512,2048]{2,1,0:T(8,128)(2,1)}) %reduce-scatter.10.cloned.1.call-update) | async-done | bytes 2097168
  847.4 9.7 convolution_convert_fusion.2
  857.3 41.1 %all_to_all.36 = bf16[8,512,256]{2,1,0:T(8,128)(2,1)} all-to-all(bf16[8,512,256]{2,1,0:T(8,128)(2,1)S(1)} %bitcast.117), channel_id=1, replica_groups=mesh['replica'=4,'shard'=8] {'shard'}, dimensions={0} | all-to-all | bytes 4194304 | tf_op jit(solution)/shard_map/all_to_all | solution.py:531
  898.4 112.1 %all-reduce.7.cloned.1.call-done = bf16[1024,2048]{1,0:T(8,128)(2,1)} async-done(((bf16[1024,2048]{1,0:T(8,128)(2,1)}), bf16[1024,2048]{1,0:T(8,128)(2,1)}) %all-reduce.7.cloned.1.call-update) | async-done | bytes 4194320 | tf_op jit(solution)/shard_map/psum | solution.py:654
  1010.6 156.3 %all-reduce.9.cloned.1.call-done = bf16[8,256,1024]{2,1,0:T(8,128)(2,1)} async-done(((bf16[8,256,1024]{2,1,0:T(8,128)(2,1)}), bf16[8,256,1024]{2,1,0:T(8,128)(2,1)}) %all-reduce.9.cloned.1.call-update) | async-done | bytes 4194320 | tf_op jit(solution)/shard_map/psum | solution.py:670
  1167.0 10.8 convolution_convert_fusion.1
  1181.9 39.6 %shard_map.214 = bf16[8,4,128,384]{3,2,1,0:T(8,128)(2,1)} custom-call(bf16[8,4,128,384]{3,2,1,0:T(8,128)(2,1)} %bitcast.127, bf16[8,4,128,256]{3,2,1,0:T(8,128)(2,1)S(1)} %bitcast.108, f32[4,4,1024]{2,1,0:T(4,128)S(1)} %get-tuple-element.40.norm_ref, s32[4,1024,1]{2,1,0:T(8,128)S(1)} %copy-done.1, s32[4,1,1024]{2,1,0:T(1,128)S(1)} %copy-done.5, ...), custom_call_target="tpu_custom_call" | custom-call | flops 10737418240 | bytes 9437184 | tf_op jit(solution)/shard_map/pallas_call | solution.py:158
  1224.7 41.9 %all_to_all.37 = bf16[8,512,384]{1,2,0:T(8,128)(2,1)S(1)} all-to-all(bf16[8,512,384]{1,2,0:T(8,128)(2,1)S(1)} %copy.62), channel_id=1, replica_groups=mesh['replica'=4,'shard'=8] {'shard'}, dimensions={0} | all-to-all | bytes 6291456 | tf_op jit(solution)/shard_map/all_to_all | solution.py:531
  1268.2 9.9 convolution_convert_fusion
  1284.9 38.5 %all-reduce.11.cloned.1.call-done = bf16[8,256,1024]{2,1,0:T(8,128)(2,1)} async-done(((bf16[8,256,1024]{2,1,0:T(8,128)(2,1)}), bf16[8,256,1024]{2,1,0:T(8,128)(2,1)}) %all-reduce.11.cloned.1.call-update) | async-done | bytes 4194320 | tf_op jit(solution)/shard_map/psum | solution.py:672
  1323.4 74.3 %reduce-scatter.8.cloned.1.call-done = bf16[256,2048]{1,0:T(8,128)(2,1)} async-done(((bf16[2048,2048]{1,0:T(8,128)(2,1)}), bf16[256,2048]{1,0:T(8,128)(2,1)}) %reduce-scatter.8.cloned.1.call-update) | async-done | bytes 1048592 | tf_op jit(solution)/shard_map/reduce_scatter | solution.py:554
  1397.7 96.2 %reduce-scatter.6.cloned.1.call-done = bf16[256,3072]{1,0:T(8,128)(2,1)} async-done(((bf16[2048,3072]{1,0:T(8,128)(2,1)}), bf16[256,3072]{1,0:T(8,128)(2,1)}) %reduce-scatter.6.cloned.1.call-update) | async-done | bytes 1572880 | tf_op jit(solution)/shard_map/reduce_scatter | solution.py:554
  1496.5 12.4 fusion.8
  1508.9 44.4 %psum.42 = f32[2,2048]{1,0:T(2,128)S(1)} all-reduce(f32[2,2048]{1,0:T(2,128)S(1)} %pad_maximum_fusion.2), channel_id=1, replica_groups=mesh['replica'=4,'shard'=8] {'replica','shard'}, use_global_device_ids=true, to_apply=%region_8.0 | all-reduce | flops 4096 | bytes 32768 | tf_op jit(solution)/shard_map/psum | solution.py:695
  1554.0 7.0 fusion.7
  1561.0 11.7 convert_bitcast_fusion
  1572.7 8.6 copy.72
  1585.6 17.0 %all-reduce.13.cloned.1.call-done = (bf16[256,8,384]{0,2,1:T(8,128)(2,1)}, bf16[256,2048]{1,0:T(8,128)(2,1)}) async-done(((bf16[256,8,384]{0,2,1:T(8,128)(2,1)}, bf16[256,2048]{1,0:T(8,128)(2,1)}), (bf16[256,8,384]{0,2,1:T(8,128)(2,1)}, bf16[256,2048]{1,0:T(8,128)(2,1)})) %all-reduce.13.cloned.1.call-update) | async-done | bytes 2621456 | tf_op jit(solution)/shard_map/psum | solution.py:539
  (157 shorter events, 108.1 us)
Async XLA Ops:
  7.2 188.9 %all-gather.12.cloned.1.call-start = ((), (), s32[]{:S(2)}) async-start(), calls=%async_computation.18 | async-start | bytes 10485760 | tf_op jit(solution)/shard_map/all_gather | solution.py:629
  46.6 224.8 %all-gather.6.cloned.1.call-start = ((), (), s32[]{:S(2)}) async-start(), calls=%async_computation.10 | async-start | bytes 14155776 | tf_op jit(solution)/shard_map/all_gather | solution.py:550
  49.4 12.7 copy-start.10
  52.4 10.8 copy-start.28
  52.4 349.5 %all-gather.8.cloned.1.call-start = ((), (), s32[]{:S(2)}) async-start(), calls=%async_computation.11 | async-start | bytes 9437184 | tf_op jit(solution)/shard_map/all_gather | solution.py:550
  53.2 412.5 %all-gather.10.cloned.1.call-start = ((), (), s32[]{:S(2)}) async-start(), calls=%async_computation.12 | async-start | bytes 10485760 | tf_op jit(solution)/shard_map/all_gather | solution.py:633
  63.5 395.0 %copy-start.21 = (f32[1,2048]{1,0:T(1,128)}, f32[1,2048]{1,0:T(1,128)S(1)}, u32[]{:S(2)}) copy-start(f32[1,2048]{1,0:T(1,128)S(1)} %get-tuple-element.94) | copy-start | bytes 24580
  196.1 269.5 %collective-permute-start = (bf16[4,2,4,64,2048]{4,3,2,1,0:T(8,128)(2,1)}, bf16[4,2,4,64,2048]{4,3,2,1,0:T(8,128)(2,1)}, u32[]{:S(2)}, u32[]{:S(2)}) collective-permute-start(bf16[4,2,4,64,2048]{4,3,2,1,0:T(8,128)(2,1)} %bitcast.154), channel_id=1, source_target_pairs={{0,1},{1,0},{2,3},{3,2},{4,5},{5,4},{6,7},{7,6},{8,9},{9,8},{10,11... | collective-permute-start | bytes 25165832 | tf_op jit(solution)/shard_map/ppermute | solution.py:630
  285.3 62.1 %all-to-all-start = ((bf16[8,512,384]{1,2,0:T(8,128)(2,1)}), bf16[8,512,384]{1,2,0:T(8,128)(2,1)}, u32[]{:S(2)}, u32[]{:S(2)}) async-start(bf16[8,512,384]{1,2,0:T(8,128)(2,1)} %maximum_bitcast_fusion), calls=%async_computation | async-start | bytes 6291456 | tf_op jit(solution)/shard_map/all_to_all | solution.py:531
  347.4 44.2 %copy-start = (s32[4,1024,1]{2,1,0:T(8,128)}, s32[4,1024,1]{2,1,0:T(8,128)S(1)}, u32[]{:S(2)}) copy-start(s32[4,1024,1]{2,1,0:T(8,128)S(1)} %copy.56.seg_col_ref) | copy-start | bytes 49156
  392.9 57.8 %copy-start.11 = (bf16[4,128,2048]{2,1,0:T(8,128)(2,1)S(1)}, bf16[4,128,2048]{2,1,0:T(8,128)(2,1)}, u32[]{:S(2)}) copy-start(bf16[4,128,2048]{2,1,0:T(8,128)(2,1)} %param.13) | copy-start | bytes 6291460
  397.0 53.8 %all-to-all-start.1 = ((bf16[8,512,256]{1,2,0:T(8,128)(2,1)}), bf16[8,512,256]{1,2,0:T(8,128)(2,1)}, u32[]{:S(2)}, u32[]{:S(2)}) async-start(bf16[8,512,256]{1,2,0:T(8,128)(2,1)} %copy.57), calls=%async_computation.1 | async-start | bytes 4194304 | tf_op jit(solution)/shard_map/all_to_all | solution.py:531
  401.3 440.0 %reduce-scatter.10.cloned.1.call-start = ((), (), s32[]{:S(2)}) async-start(), calls=%async_computation.19 | async-start | bytes 10485760
  401.6 60.7 %collective-permute-start.1 = (bf16[1024,2048]{1,0:T(8,128)(2,1)}, bf16[1024,2048]{1,0:T(8,128)(2,1)}, u32[]{:S(2)}, u32[]{:S(2)}) collective-permute-start(bf16[1024,2048]{1,0:T(8,128)(2,1)} %down_own_ref.1), channel_id=1, source_target_pairs={{0,1},{1,0},{2,3},{3,2},{4,5},{5,4},{6,7},{7,6},{8,9},{9,8},{10,11... | collective-permute-start | bytes 12582920 | tf_op jit(solution)/shard_map/ppermute | solution.py:631
  684.1 92.0 %all-to-all-start.5 = ((bf16[8,256,1024]{2,1,0:T(8,128)(2,1)}), bf16[8,256,1024]{2,1,0:T(8,128)(2,1)}, u32[]{:S(2)}, u32[]{:S(2)}) async-start(bf16[8,256,1024]{2,1,0:T(8,128)(2,1)} %bitcast.112), calls=%async_computation.5 | async-start | bytes 8388608 | tf_op jit(solution)/shard_map/all_to_all | solution.py:531
  776.1 81.2 %all-to-all-start.4 = ((bf16[8,256,1024]{2,1,0:T(8,128)(2,1)}), bf16[8,256,1024]{2,1,0:T(8,128)(2,1)}, u32[]{:S(2)}, u32[]{:S(2)}) async-start(bf16[8,256,1024]{2,1,0:T(8,128)(2,1)} %bitcast.111), calls=%async_computation.4 | async-start | bytes 8388608 | tf_op jit(solution)/shard_map/all_to_all | solution.py:531
  780.6 229.9 %all-reduce.7.cloned.1.call-start = ((), (), s32[]{:S(2)}) async-start(), calls=%async_computation.14 | async-start | bytes 8388608 | tf_op jit(solution)/shard_map/psum | solution.py:654
  789.2 377.7 %all-reduce.9.cloned.1.call-start = ((), (), s32[]{:S(2)}) async-start(), calls=%async_computation.15 | async-start | bytes 8388608 | tf_op jit(solution)/shard_map/psum | solution.py:670
  789.4 6.1 copy-start.7
  789.4 6.1 copy-start.22
  789.4 6.1 copy-start.27
  795.6 45.8 %copy-start.14 = (bf16[4,128,2048]{2,1,0:T(8,128)(2,1)S(1)}, bf16[4,128,2048]{2,1,0:T(8,128)(2,1)}, u32[]{:S(2)}) copy-start(bf16[4,128,2048]{2,1,0:T(8,128)(2,1)} %param.16) | copy-start | bytes 6291460
  847.4 9.7 copy-start.13
  1010.5 312.9 %all-reduce.11.cloned.1.call-start = ((), (), s32[]{:S(2)}) async-start(), calls=%async_computation.17 | async-start | bytes 8388608 | tf_op jit(solution)/shard_map/psum | solution.py:672
  1166.9 230.8 %reduce-scatter.8.cloned.1.call-start = ((), (), s32[]{:S(2)}) async-start(), calls=%async_computation.16 | async-start | bytes 9437184 | tf_op jit(solution)/shard_map/reduce_scatter | solution.py:554
  1177.8 316.2 %reduce-scatter.6.cloned.1.call-start = ((), (), s32[]{:S(2)}) async-start(), calls=%async_computation.13 | async-start | bytes 14155776 | tf_op jit(solution)/shard_map/reduce_scatter | solution.py:554
  1224.7 43.6 %copy-start.17 = (bf16[4,128,2048]{2,1,0:T(8,128)(2,1)S(1)}, bf16[4,128,2048]{2,1,0:T(8,128)(2,1)}, u32[]{:S(2)}) copy-start(bf16[4,128,2048]{2,1,0:T(8,128)(2,1)} %fusion.11) | copy-start | bytes 6291460
  1278.1 324.4 %all-reduce.13.cloned.1.call-start = ((), (), s32[]{:S(2)}) async-start(), calls=%async_computation.20 | async-start | bytes 5242880 | tf_op jit(solution)/shard_map/psum | solution.py:539
  1284.9 211.6 %copy-start.12 = (bf16[4,128,2048]{2,1,0:T(8,128)(2,1)S(1)}, bf16[4,128,2048]{2,1,0:T(8,128)(2,1)}, u32[]{:S(2)}) copy-start(bf16[4,128,2048]{2,1,0:T(8,128)(2,1)} %param.13) | copy-start | bytes 6291460
  1284.9 211.6 %copy-start.24 = (f32[1,2048]{1,0:T(1,128)S(1)}, f32[1,2048]{1,0:T(1,128)}, u32[]{:S(2)}) copy-start(f32[1,2048]{1,0:T(1,128)} %copy-done.23) | copy-start | bytes 24580
  1284.9 211.6 %copy-start.29 = (f32[512]{0:T(512)S(1)}, f32[512]{0:T(512)}, u32[]{:S(2)}) copy-start(f32[512]{0:T(512)} %get-tuple-element.98) | copy-start | bytes 6148
  1572.7 8.6 copy-start.9
  (20 other events, 47.7 us)
Sparse Core Ops, SparseCore 0:
  46.7 149.3 all-gather.11
  198.5 72.7 all-gather.5
  273.2 80.5 all-gather.7
  355.5 110.0 all-gather.9
  676.5 164.7 reduce-scatter.9
  844.3 166.1 all-reduce.6
  1012.9 153.9 all-reduce.8
  1169.4 153.9 all-reduce.10
  1327.4 70.2 reduce-scatter.7
  1401.5 92.3 reduce-scatter.5
  1497.1 105.4 all-reduce.12

commit v3 on v2

--- a/solution.py
+++ b/solution.py
@@ -80,32 +80,28 @@
     return [lower * cosine + upper * sine, upper * cosine - lower * sine]
 
 
-def backward_kernel(
-    heads, rows, qkv_ref, grad_ref, norm_ref, seg_col_ref, seg_row_ref, cos_ref, sin_ref,
-    out_ref, key_sum, value_sum,
-):
-    shards, _, span, _ = qkv_ref.shape
+def attention_back(heads, rows, qkv_ref, grad_ref, norm, seg_col, seg_row, cos, sin, out_ref, sums):
+    shards, span, _ = qkv_ref.shape
     length = shards * span
     wide = heads * HEAD_DIM
-    seg_col, seg_row = seg_col_ref[0], seg_row_ref[0]
-    keys = qkv_ref[:, 0, :, wide : wide + HEAD_DIM].reshape(length, HEAD_DIM)
-    values = qkv_ref[:, 0, :, wide + HEAD_DIM :].reshape(length, HEAD_DIM)
+    keys = qkv_ref[:, :, wide : wide + HEAD_DIM].reshape(length, HEAD_DIM)
+    values = qkv_ref[:, :, wide + HEAD_DIM :].reshape(length, HEAD_DIM)
     keys_t = keys.astype(f32).T.astype(bf16)
-    key_sum[...] = jnp.zeros_like(key_sum)
-    value_sum[...] = jnp.zeros_like(value_sum)
+    sums[...] = jnp.zeros_like(sums)
+    key_sum, value_sum = sums.at[0], sums.at[1]
     for first in range(0, length, rows):
         last = first + rows
         at = slice(first // span, last // span)
         bias = score_bias(seg_col, seg_row, first, rows)
-        queries = qkv_ref[at, 0, :, :wide].reshape(rows, wide) * HEAD_DIM ** (-0.5)
-        grads = grad_ref[at, 0].reshape(rows, wide)
-        cosine, sine = cos_ref[0, :, first:last], sin_ref[0, :, first:last]
+        queries = qkv_ref[at, :, :wide].reshape(rows, wide) * HEAD_DIM ** (-0.5)
+        grads = grad_ref[at].reshape(rows, wide)
+        cosine, sine = cos[:, first:last], sin[:, first:last]
         parts = []
         for head in range(heads):
             lanes = slice(head * HEAD_DIM, (head + 1) * HEAD_DIM)
             one, grad = queries[:, lanes], grads[:, lanes]
             scores = dot_nt(keys[:last], one) + bias
-            probs = jnp.exp(scores - norm_ref[0, head : head + 1, first:last])
+            probs = jnp.exp(scores - norm[head : head + 1, first:last])
             grad_probs = dot_nt(values[:last], grad)
             level = jnp.sum(probs * grad_probs, 0, keepdims=True)
             grad_scores = (probs * (grad_probs - level)).astype(bf16)
@@ -114,10 +110,10 @@
             turned = dot_nn(keys_t[:, :last], grad_scores) * HEAD_DIM ** (-0.5)
             parts.extend(turn_back(turned, cosine, sine))
         out = jnp.concatenate(parts, 0).T.astype(bf16)
-        out_ref[at, 0, :, :wide] = out.reshape(rows // span, span, wide)
-    key_parts = turn_back(key_sum[...].T, cos_ref[0], sin_ref[0])
+        out_ref[at, :, :wide] = out.reshape(rows // span, span, wide)
+    key_parts = turn_back(key_sum[...].T, cos[...], sin[...])
     both = jnp.concatenate([jnp.concatenate(key_parts, 0).T, value_sum[...]], -1)
-    out_ref[:, 0, :, wide:] = both.astype(bf16).reshape(shards, span, 2 * HEAD_DIM)
+    out_ref[:, :, wide:] = both.astype(bf16).reshape(shards, span, 2 * HEAD_DIM)
 
 
 def by_sequence(shape, axis):
@@ -149,26 +145,6 @@
             transcendentals=seqs * heads * length * length,
         ),
     )(qkv, seg_col, seg_row)
-
-
-def attention_backward(heads, qkv, grads, norms, seg_col, seg_row, cosine, sine):
-    shards, seqs, span, _ = qkv.shape
-    length = shards * span
-    args = (qkv, grads, norms, seg_col, seg_row, cosine, sine)
-    return pl.pallas_call(
-        functools.partial(backward_kernel, heads, 256),
-        grid=(seqs,),
-        in_specs=[by_sequence(a.shape, 1 if i < 2 else 0) for i, a in enumerate(args)],
-        out_specs=by_sequence(qkv.shape, 1),
-        out_shape=jax.ShapeDtypeStruct(qkv.shape, bf16),
-        scratch_shapes=[pltpu.VMEM((length, HEAD_DIM), f32), pltpu.VMEM((length, HEAD_DIM), f32)],
-        compiler_params=pltpu.CompilerParams(vmem_limit_bytes=48 * 2**20),
-        cost_estimate=pl.CostEstimate(
-            flops=10 * seqs * heads * length * length * HEAD_DIM,
-            bytes_accessed=3 * qkv.size * 2,
-            transcendentals=seqs * heads * length * length,
-        ),
-    )(*args)
 
 
 def chip_at(chip, distance):
@@ -426,50 +402,62 @@
         return result
 
     outs = ((down_own_out, down_got), (gate_own_out, gate_got), (up_own_out, up_got))
+    order = [(0, 0), (1, 0), (0, 1), (1, 1), (2, 0), (2, 1)]
     started = {}
-    for which in range(3):
-        if which == 2:
-            copy = load(up_ref, 1)
-            copy.start()
-            copy.wait()
-        for owner in range(2):
-            stage = cot if owner == 0 else inner
-            first = ((1 - core) if owner == 0 else core) * half_units
-            copies = stage_copies(which, owner, stage, *outs[which])
-            started[which, owner] = copies
-            if which > 0:
-                for copy in started[which - 1, owner]:
-                    if owner == 0:
-                        copy.wait_send()
-                    else:
-                        copy.wait()
-            for t, copy in enumerate(copies):
-                if which == 0:
-                    left = weights[0, :tokens, pl.ds(pl.multiple_of(first + t * rows, rows), rows)]
-                    for j in range(width // 1024):
-                        columns = pl.ds(j * 1024, 1024)
-                        stage[t, :, columns] = lax.dot_general(
-                            left, weights[2, :tokens, columns], (((0,), (0,)), ((), ())),
-                            preferred_element_type=f32,
-                        ).astype(bf16)
-                else:
-                    left = normed[:, :, t * rows : (t + 1) * rows].reshape(tokens, rows)
-                    right = weights[1, :tokens, pl.ds(pl.multiple_of(first, half_units), half_units)]
-                    stage[t // per_slot, :, pl.ds((t % per_slot) * half_units, half_units)] = (
-                        lax.dot_general(
-                            left, right, (((0,), (0,)), ((), ())), preferred_element_type=f32
-                        ).astype(bf16)
-                    )
-                copy.start()
-    for owner in range(2):
-        for copy in started[2, owner]:
-            if owner == 0:
+    up_load = load(up_ref, 0)
+
+    def finish(at):
+        for copy in started[order[at]]:
+            if order[at][1] == 0:
                 copy.wait_send()
             else:
                 copy.wait()
-    for which in range(3):
-        for copy in started[which, 0]:
-            copy.wait_recv()
+
+    for at, (which, owner) in enumerate(order):
+        stage = cot if at % 2 == 0 else inner
+        first = ((1 - core) if owner == 0 else core) * half_units
+        copies = stage_copies(which, owner, stage, *outs[which])
+        started[which, owner] = copies
+        if at >= 2:
+            finish(at - 2)
+        if (which, owner) == (1, 1):
+            up_load.start()
+        if (which, owner) == (2, 0):
+            up_load.wait()
+        for t, copy in enumerate(copies):
+            across = width if which == 0 else half_units
+            got = None
+            if owner == 1:
+                started[which, 0][t].wait_recv()
+                got = pltpu.make_async_copy(
+                    outs[which][1].at[pl.ds(t * rows, rows)],
+                    out_stage.at[:, pl.ds(0, across)],
+                    core_sem.at[3, t],
+                )
+                got.start()
+            if which == 0:
+                left = weights[0, :tokens, pl.ds(pl.multiple_of(first + t * rows, rows), rows)]
+                right = weights.at[2]
+                slot, begin = t, 0
+            else:
+                left = normed[:, :, t * rows : (t + 1) * rows].reshape(tokens, rows)
+                right = weights.at[1 if which == 1 else 0]
+                slot, begin = t // per_slot, (t % per_slot) * half_units
+            wide = min(1024, across)
+            for j in range(across // wide):
+                if which == 0:
+                    columns = pl.ds(j * wide, wide)
+                else:
+                    columns = pl.ds(pl.multiple_of(first, half_units), half_units)
+                product = outer_sum(left, right[:tokens, columns])
+                if owner == 1:
+                    if j == 0:
+                        got.wait()
+                    product = product + out_stage[:, j * wide : (j + 1) * wide].astype(f32)
+                stage[slot, :, pl.ds(begin + j * wide, wide)] = product.astype(bf16)
+            copy.start()
+    finish(4)
+    finish(5)
     for index in range(1, chips):
         for at in range(2):
             sum_copy(index, at).wait_send()
@@ -516,7 +504,7 @@
             pltpu.VMEM((rows, width), bf16),
             dma((4,)), dma((chips, 2)), dma((chips, 2)), dma((2, 2)), dma((3, 2)),
             dma((chips, 2)), dma((chips, 2)), dma((3,)), dma((2,)),
-            dma((3, tiles)), dma((3, tiles)), dma((3, tiles)), dma((3 + chips,)),
+            dma((3, tiles)), dma((3, tiles)), dma((4, tiles)), dma((3 + chips,)),
         ],
         compiler_params=pltpu.CompilerParams(
             collective_id=0, has_side_effects=True, vmem_limit_bytes=63 * 2**20
@@ -527,16 +515,445 @@
     )(normed, cot, own, other, down_own, down_other)
 
 
+def tail_kernel(
+    heads,
+    down_ref, gate_ref, up_ref, outs_ref, grad_ref, qkv_ref, normed_ref, attn_ref, branch_ref,
+    norm_ref, seg_col_ref, seg_row_ref, cos_ref, sin_ref,
+    inner_land, grad_land, turn_land, end_land, mid_land, out_land, total,
+    down_result, gate_result, up_result, rest_result,
+    qkv, grads, turned, sums, turned_all, normed, attn, branch, sent, core_land, sum_land,
+    mine, theirs, half, whole,
+    inner_send, inner_recv, grad_send, grad_recv, turn_send, turn_recv, core_send, core_recv,
+    sum_send, sum_recv, part_send, part_recv, end_send, end_recv, mid_send, mid_recv, out_send, out_recv,
+    self_sem, load_sem, seq_sem, tick_sem, whole_sem, total_sem,
+):
+    shards, seqs, span, part = qkv_ref.shape
+    rows, width = normed_ref.shape
+    _, owned, units = inner_land.shape[1:]
+    chips = shards // 2
+    chunks = end_land.shape[0]
+    qkv_width = shards * part
+    line = lax.axis_size("replica") == 4
+    me, replica = lax.axis_index("shard"), lax.axis_index("replica")
+    chip, core = me // 2, me % 2
+    partner = [
+        chip_at(chip, d // 2) * 2 + (core if d % 2 == 0 else 1 - core) for d in range(shards)
+    ]
+    is_inner = (replica == 1) | (replica == 2)
+    inward = jnp.where(replica < 2, 1, 2)
+    outward = jnp.where(replica < 2, 0, 3)
+
+    def remote(source, target, send, recv, shard, to=None):
+        return pltpu.make_async_remote_copy(
+            src_ref=source, dst_ref=target, send_sem=send, recv_sem=recv,
+            device_id=(replica if to is None else to, shard),
+            device_id_type=pl.DeviceIdType.MESH,
+        )
+
+    barrier = pltpu.get_barrier_semaphore()
+
+    def greet(to, shard):
+        pl.semaphore_signal(
+            barrier, inc=1, device_id=(to, shard), device_id_type=pl.DeviceIdType.MESH
+        )
+
+    for d in range(1, shards):
+        greet(replica, partner[d])
+    if line:
+
+        @pl.when(is_inner)
+        def _():
+            greet(outward, me)
+            greet(3 - replica, me)
+            pl.semaphore_wait(barrier, shards + 1)
+
+        @pl.when(jnp.logical_not(is_inner))
+        def _():
+            greet(inward, me)
+            pl.semaphore_wait(barrier, shards)
+
+    else:
+        pl.semaphore_wait(barrier, shards - 1)
+
+    def grad_copy(d, s):
+        at = pl.ds(pl.multiple_of(s * span, span), span)
+        return remote(
+            grad_ref.at[partner[d], at], grad_land.at[me, at],
+            grad_send.at[d, s], grad_recv.at[d, s], partner[d],
+        )
+
+    def inner_copy(which, d):
+        source = (gate_ref, up_ref)[which]
+        return remote(
+            source.at[pl.ds(pl.multiple_of(partner[d] * owned, owned), owned)],
+            inner_land.at[which, me],
+            inner_send.at[which, d], inner_recv.at[which, d], partner[d],
+        )
+
+    own_grad = pltpu.make_async_copy(grad_ref.at[me], grad_land.at[me], self_sem.at[0])
+    own_grad.start()
+    for s in range(seqs):
+        for d in range(1, shards):
+            grad_copy(d, s).start()
+    own_inner = [
+        pltpu.make_async_copy(
+            ref.at[pl.ds(pl.multiple_of(me * owned, owned), owned)],
+            inner_land.at[which, me], self_sem.at[1 + which],
+        )
+        for which, ref in enumerate((gate_ref, up_ref))
+    ]
+
+    def start_inner(which):
+        own_inner[which].start()
+        for d in range(1, shards):
+            inner_copy(which, d).start()
+
+    loads = [
+        pltpu.make_async_copy(ref, target, load_sem.at[i])
+        for i, (ref, target) in enumerate(
+            ((normed_ref, normed), (attn_ref, attn), (branch_ref, branch))
+        )
+    ]
+    for copy in loads:
+        copy.start()
+
+    down_across = width // units
+    down_chunks = down_ref.shape[0] // owned * down_across
+    last_inner = down_chunks + 2 * shards
+
+    def block(ref, row, column):
+        return ref.at[
+            pl.ds(pl.multiple_of(row * owned, owned), owned),
+            pl.ds(pl.multiple_of(column * units, units), units),
+        ]
+
+    def source_of(c):
+        if not isinstance(c, int) or c < down_chunks:
+            return block(down_ref, c // down_across, c % down_across)
+        if c < last_inner:
+            which, d = divmod(c - down_chunks, shards)
+            return inner_land.at[which, partner[d]]
+        return total.at[c - last_inner]
+
+    def place_of(c):
+        if not isinstance(c, int) or c < down_chunks:
+            return block(down_result, c // down_across, c % down_across)
+        if c < last_inner:
+            which, d = divmod(c - down_chunks, shards)
+            return block((gate_result, up_result)[which], 0, partner[d])
+        return block(rest_result, 0, c - last_inner)
+
+    def end_copy(c):
+        return remote(
+            source_of(c), end_land.at[c], end_send.at[c], end_recv.at[c], me, inward
+        )
+
+    def mid_copy(c):
+        return remote(
+            half.at[c % 2], mid_land.at[c], mid_send.at[c], mid_recv.at[c], me, 3 - replica
+        )
+
+    def out_copy(c):
+        return remote(
+            whole.at[c % 2], place_of(c), out_send.at[c], out_recv.at[c], me, outward
+        )
+
+    def keep_copy(c):
+        return pltpu.make_async_copy(whole.at[c % 2], place_of(c), whole_sem.at[c % 2])
+
+    def from_end(c):
+        @pl.when(jnp.logical_not(is_inner))
+        def _():
+            end_copy(c).start()
+
+    def settle(c):
+        which, d = divmod(c - down_chunks, shards)
+        if d == 0:
+            own_inner[which].wait()
+        else:
+            inner_copy(which, d).wait_recv()
+
+    def middle(c):
+        later = not isinstance(c, int)
+
+        @pl.when(is_inner)
+        def _():
+            one = pltpu.make_async_copy(source_of(c), mine, tick_sem.at[0])
+            one.start()
+            end_copy(c).wait_recv()
+            two = pltpu.make_async_copy(end_land.at[c], theirs.at[0], tick_sem.at[1])
+            two.start()
+            one.wait()
+            two.wait()
+            if later or c >= 2:
+                mid_copy(c - 2).wait_send()
+            half[c % 2] = (mine[...].astype(f32) + theirs[0].astype(f32)).astype(bf16)
+            mid_copy(c).start()
+            if later or c >= 1:
+                finish(c - 1)
+
+    def finish(c):
+        mid_copy(c).wait_recv()
+        two = pltpu.make_async_copy(mid_land.at[c], theirs.at[1], tick_sem.at[2])
+        two.start()
+        two.wait()
+        if not isinstance(c, int) or c >= 2:
+            out_copy(c - 2).wait_send()
+            keep_copy(c - 2).wait()
+        whole[c % 2] = (half[c % 2].astype(f32) + theirs[1].astype(f32)).astype(bf16)
+        out_copy(c).start()
+        keep_copy(c).start()
+
+    lead = 4
+    position = [0]
+
+    def ticks(count):
+        for _ in range(count):
+            c = position[0]
+            if c >= last_inner:
+                return
+            position[0] += 1
+            ahead = c + lead
+            if down_chunks <= ahead < last_inner:
+                settle(ahead)
+                if line:
+                    from_end(ahead)
+            if line:
+                middle(c)
+
+    if line:
+        for c in range(down_chunks):
+            from_end(c)
+    own_grad.wait()
+    ticks(3)
+    start_inner(0)
+
+    def seq_loads(s):
+        at = pl.ds(pl.multiple_of(s * span, span), span)
+        return [
+            pltpu.make_async_copy(qkv_ref.at[:, s], qkv, seq_sem.at[0]),
+            pltpu.make_async_copy(grad_land.at[:, at], grads, seq_sem.at[1]),
+        ]
+
+    def turn_copy(d, s):
+        at = pl.ds(pl.multiple_of(s * span, span), span)
+        return remote(
+            turned.at[s, partner[d]], turn_land.at[me, at],
+            turn_send.at[d, s], turn_recv.at[d, s], partner[d],
+        )
+
+    def own_turn(s):
+        at = pl.ds(pl.multiple_of(s * span, span), span)
+        return pltpu.make_async_copy(turned.at[s, me], turn_land.at[me, at], seq_sem.at[2 + s])
+
+    @pl.loop(0, seqs)
+    def _(s):
+        for d in range(1, shards):
+            grad_copy(d, s).wait_recv()
+        for copy in seq_loads(s):
+            copy.start()
+        for copy in seq_loads(s):
+            copy.wait()
+        attention_back(
+            heads, 256, qkv, grads, norm_ref.at[s], seg_col_ref[s], seg_row_ref[s],
+            cos_ref.at[s], sin_ref.at[s], turned.at[s], sums,
+        )
+        own_turn(s).start()
+        for d in range(1, shards):
+            turn_copy(d, s).start()
+        if line:
+            middle(3 + s)
+
+    if line:
+        position[0] = 3 + seqs
+        for c in range(down_chunks, 3 + seqs + lead):
+            settle(c)
+            from_end(c)
+    start_inner(1)
+    for s in range(seqs):
+        own_turn(s).wait()
+        for d in range(1, shards):
+            turn_copy(d, s).wait_recv()
+    take = pltpu.make_async_copy(turn_land, turned_all, load_sem.at[3])
+    take.start()
+    ticks(1)
+    for copy in loads:
+        copy.wait()
+    take.wait()
+
+    def block_of(owner, target, more=None):
+        columns = pl.ds(pl.multiple_of(owner * owned, owned), owned)
+        left, left_out = normed[:, columns], attn[:, columns]
+        for k in range(shards + width // units):
+            if k < shards:
+                value = outer_sum(left, turned_all[k])
+                place = slice(k * part, (k + 1) * part)
+            else:
+                at = (k - shards) * units
+                value = outer_sum(left_out, branch[:, at : at + units])
+                place = slice(qkv_width + at, qkv_width + at + units)
+            if more is not None:
+                value = value + more[:, place].astype(f32)
+            target[:, place] = value.astype(bf16)
+
+    def core_copy(d):
+        return remote(
+            sent.at[d], core_land.at[d], core_send.at[d], core_recv.at[d], partner[1]
+        )
+
+    def sum_copy(d):
+        return remote(
+            core_land.at[d], sum_land.at[d], sum_send.at[d], sum_recv.at[d], partner[2 * d]
+        )
+
+    def part_copy(d):
+        return remote(
+            outs_ref.at[chip_at(chip, d)], out_land.at[d],
+            part_send.at[d], part_recv.at[d], partner[2 * d],
+        )
+
+    order = list(range(chips - 1, -1, -1))
+    for d in order:
+        block_of(chip_at(chip, d) * 2 + 1 - core, sent.at[d])
+        core_copy(d).start()
+        if d % 2 == 0:
+            ticks(1)
+    for d in order:
+        core_copy(d).wait_recv()
+        block_of(chip_at(chip, d) * 2 + core, core_land.at[d], core_land.at[d])
+        if d > 0:
+            sum_copy(d).start()
+        if d % 2 == 0:
+            ticks(1)
+    for d in order[:-1]:
+        part_copy(d).start()
+    ticks(last_inner)
+    for d in range(1, chips):
+        sum_copy(d).wait_recv()
+    across = total.shape[0]
+    puts = []
+    core_copy(0).wait_send()
+    for k in range(across):
+        columns = pl.ds(k * units, units)
+        value = core_land[0, :, columns].astype(f32)
+        for d in range(1, chips):
+            value = value + sum_land[d, :, columns].astype(f32)
+        sent[0, :, columns] = value.astype(bf16)
+    for k in range(across):
+        put = pltpu.make_async_copy(
+            sent.at[0, :, pl.ds(k * units, units)], total.at[k], total_sem.at[k]
+        )
+        put.start()
+        puts.append(put)
+    for k in range(across):
+        puts[k].wait()
+        if line:
+            from_end(last_inner + k)
+    if line:
+        for k in range(across):
+            middle(last_inner + k)
+
+        @pl.when(is_inner)
+        def _():
+            finish(chunks - 1)
+
+    for s in range(seqs):
+        for d in range(1, shards):
+            grad_copy(d, s).wait_send()
+            turn_copy(d, s).wait_send()
+    for which in range(2):
+        for d in range(1, shards):
+            inner_copy(which, d).wait_send()
+    for d in range(chips):
+        if d > 0:
+            core_copy(d).wait_send()
+            sum_copy(d).wait_send()
+            part_copy(d).wait_send()
+            part_copy(d).wait_recv()
+    if line:
+
+        @pl.when(is_inner)
+        def _():
+            for c in (chunks - 2, chunks - 1):
+                mid_copy(c).wait_send()
+                out_copy(c).wait_send()
+                keep_copy(c).wait()
+
+        @pl.when(jnp.logical_not(is_inner))
+        def _():
+            for c in range(chunks):
+                end_copy(c).wait_send()
+                out_copy(c).wait_recv()
+
+
+def tail(heads, down, gate, up, outs, grads, qkv, normed, attn, branch, norms, *tables):
+    shards, seqs, span, part = qkv.shape
+    rows, width = normed.shape
+    units = gate.shape[1]
+    owned = width // shards
+    chips = shards // 2
+    full = shards * part + width
+    across = full // units
+    chunks = (down.shape[0] // owned) * (width // units) + 2 * shards + across
+    hbm = pl.BlockSpec(memory_space=pl.ANY)
+    vmem = pl.BlockSpec(memory_space=pltpu.VMEM)
+    dma = pltpu.SemaphoreType.DMA
+
+    def low(*shape):
+        return jax.ShapeDtypeStruct(shape, bf16)
+
+    out_shape = (
+        low(2, shards, owned, units), low(*grads.shape), low(shards, rows, part),
+        low(chunks, owned, units), low(chunks, owned, units), low(*outs.shape),
+        low(across, owned, units),
+        low(*down.shape), low(owned, shards * units), low(owned, shards * units), low(owned, full),
+    )
+    length = shards * span
+    wide = grads.shape[2]
+    return pl.pallas_call(
+        functools.partial(tail_kernel, heads),
+        in_specs=[hbm] * 9 + [vmem] * 5,
+        out_specs=(hbm,) * len(out_shape),
+        out_shape=out_shape,
+        scratch_shapes=[
+            pltpu.VMEM((shards, span, part), bf16),
+            pltpu.VMEM((shards, span, wide), bf16),
+            pltpu.VMEM((seqs, shards, span, part), bf16),
+            pltpu.VMEM((2, length, HEAD_DIM), f32),
+            pltpu.VMEM((shards, rows, part), bf16),
+            pltpu.VMEM((rows, width), bf16),
+            pltpu.VMEM((rows, width), bf16),
+            pltpu.VMEM((rows, width), bf16),
+            pltpu.VMEM((chips, owned, full), bf16),
+            pltpu.VMEM((chips, owned, full), bf16),
+            pltpu.VMEM((chips, owned, full), bf16),
+            pltpu.VMEM((owned, units), bf16),
+            pltpu.VMEM((2, owned, units), bf16),
+            pltpu.VMEM((2, owned, units), bf16),
+            pltpu.VMEM((2, owned, units), bf16),
+            dma((2, shards)), dma((2, shards)), dma((shards, seqs)), dma((shards, seqs)),
+            dma((shards, seqs)), dma((shards, seqs)), dma((chips,)), dma((chips,)),
+            dma((chips,)), dma((chips,)), dma((chips,)), dma((chips,)), dma((chunks,)), dma((chunks,)),
+            dma((chunks,)), dma((chunks,)), dma((chunks,)), dma((chunks,)),
+            dma((3,)), dma((4,)), dma((2 + seqs,)), dma((3,)), dma((2,)), dma((across,)),
+        ],
+        compiler_params=pltpu.CompilerParams(
+            collective_id=1, has_side_effects=True, vmem_limit_bytes=62 * 2**20
+        ),
+        cost_estimate=pl.CostEstimate(
+            flops=10 * seqs * heads * length * length * HEAD_DIM,
+            bytes_accessed=2**29,
+            transcendentals=seqs * heads * length * length,
+        ),
+    )(down, gate, up, outs, grads, qkv, normed, attn, branch, norms, *tables)
+
+
 def exchange(blocks):
     return lax.all_to_all(blocks, "shard", 0, 0, tiled=True)
 
 
 def tie(*values):
     return lax.optimization_barrier(values)
-
-
-def replica_sum(part):
-    return lax.psum(part.astype(bf16), "replica").astype(f32)
 
 
 def norm_back(grad_normed, unit_rows, scale_rows, gain_rows):
@@ -548,12 +965,6 @@
 
 def gather(block):
     return lax.all_gather(block, "shard", axis=0, tiled=True)
-
-
-def scatter(partial):
-    return lax.psum_scatter(partial.astype(bf16), "shard", scatter_dimension=0, tiled=True).astype(
-        f32
-    )
 
 
 def body(
@@ -583,6 +994,38 @@
     part = wide + 2 * HEAD_DIM
     hidden_share = down_weight.shape[0]
 
+    chips = shards // 2
+    same_core = [[2 * k + c for k in range(chips)] for c in range(2)]
+    swap = [(i, i + 1 - 2 * (i % 2)) for i in range(shards)]
+    units = 2 * hidden_share
+    share = owned // lax.axis_size("replica")
+    gate_up_own = lax.dynamic_slice_in_dim(
+        jnp.stack([gate_weight, up_weight]), lax.axis_index("replica") * share, share, 1
+    )
+    gate_up_own = jnp.transpose(gate_up_own.reshape(2, share, chips, units), (0, 2, 1, 3))
+    gate_up_part = lax.all_to_all(
+        gate_up_own, "shard", 1, 1, axis_index_groups=same_core, tiled=True
+    )
+    replicas = lax.axis_size("replica")
+    replica = lax.axis_index("replica")
+
+    def line_step(step, right, left):
+        up_pairs = [(i, i + 1) for i in range(step - 1, replicas - 1)]
+        down_pairs = [(replicas - 1 - i, replicas - 1 - j) for i, j in up_pairs]
+        return lax.ppermute(right, "replica", up_pairs), lax.ppermute(left, "replica", down_pairs)
+
+    rights, lefts = [gate_up_part], [gate_up_part]
+
+    def advance():
+        right, left = line_step(len(rights), rights[-1], lefts[-1])
+        rights.append(right)
+        lefts.append(left)
+
+    advance()
+    down_other = lax.ppermute(down_weight, "shard", swap)
+    cot_rows = cotangent.reshape(rows, width)
+    cot_all = lax.all_gather(cot_rows, "shard", axis_index_groups=same_core)
+
     def per_head(weight):
         return jnp.repeat(weight.reshape(owned, KV_HEADS, HEAD_DIM), copies, axis=1)
 
@@ -612,27 +1055,14 @@
         [lower * cosine - upper * sine, upper * cosine + lower * sine], -1
     ).reshape(rows, shards, wide + HEAD_DIM)
     qkv_rows = jnp.concatenate([turned, projected[:, :, wide + HEAD_DIM :]], -1).astype(bf16)
+    qkv_rows, rights[-1], lefts[-1] = tie(qkv_rows, rights[-1], lefts[-1])
+    advance()
     qkv = exchange(jnp.swapaxes(qkv_rows, 0, 1)).reshape(shards, seqs, span, part)
 
-    chips = shards // 2
-    same_core = [[2 * k + c for k in range(chips)] for c in range(2)]
-    swap = [(i, i + 1 - 2 * (i % 2)) for i in range(shards)]
-    units = 2 * hidden_share
-    share = owned // lax.axis_size("replica")
-    gate_up_own = lax.dynamic_slice_in_dim(
-        jnp.stack([gate_weight, up_weight]), lax.axis_index("replica") * share, share, 1
-    )
-    gate_up_own = jnp.transpose(gate_up_own.reshape(2, share, chips, units), (0, 2, 1, 3))
-    gate_up_part = lax.all_to_all(
-        gate_up_own, "shard", 1, 1, axis_index_groups=same_core, tiled=True
-    )
-    gate_up = lax.all_gather(gate_up_part, "replica")
-    gate_up_other = lax.ppermute(gate_up, "shard", swap)
-    down_other = lax.ppermute(down_weight, "shard", swap)
-    cot_rows = cotangent.reshape(rows, width)
-    cot_all = lax.all_gather(cot_rows, "shard", axis_index_groups=same_core)
-
     attn_heads, norms = attention_forward(heads, qkv, seg_col, seg_row)
+    attn_heads, rights[-1], lefts[-1] = tie(attn_heads, rights[-1], lefts[-1])
+    while len(rights) < replicas:
+        advance()
     attn = exchange(attn_heads.reshape(shards, rows, wide))
     attn = jnp.swapaxes(attn, 0, 1).reshape(rows, HEADS * HEAD_DIM)
     hidden = x + dot_nn(attn, output_full)
@@ -640,47 +1070,49 @@
     unit_two = hidden * scale_two
     normed_two = (unit_two * gain_two).astype(bf16)
 
-    partials, outs, _, _, _, down_one, gate_one, up_one, down_two, gate_two, up_two = feed_forward(
+    gate_up = jnp.zeros((replicas,) + gate_up_part.shape, bf16)
+    gate_up = lax.dynamic_update_index_in_dim(gate_up, gate_up_part, replica, 0)
+    for step in range(1, replicas):
+        block = jnp.where(replica >= step, rights[step], lefts[replicas - step])
+        gate_up = lax.dynamic_update_index_in_dim(gate_up, block, (replica - step) % replicas, 0)
+    gate_up_other = lax.ppermute(gate_up, "shard", swap)
+    partials, outs, _, _, _, down_part, gate_part, up_part, _, _, _ = feed_forward(
         normed_two, cot_all, gate_up, gate_up_other, down_weight, down_other
     )
     grad_two = jnp.sum(partials.astype(f32), 0)
-    out_sum = lax.psum_scatter(
-        outs, "shard", scatter_dimension=0, axis_index_groups=same_core, tiled=False
-    ).astype(f32)
-
-    def added(one, two):
-        return (one.astype(f32) + two.astype(f32)).astype(bf16)
-
-    down_grad = lax.psum(added(down_one, down_two), "replica")
-    gate_part = exchange(added(gate_one, gate_two).reshape(shards, owned, hidden_share))
-    up_part = exchange(added(up_one, up_two).reshape(shards, owned, hidden_share))
-    block_out = (hidden + out_sum).astype(bf16)
-
-    def to_rows(summed):
-        return jnp.swapaxes(summed, 0, 1).reshape(owned, shards * hidden_share).astype(f32)
-
-    second_grad = jnp.sum(grad_two * unit_two, 0)
     grad_hidden = cot_rows.astype(f32) + norm_back(grad_two, unit_two, scale_two, gain_two)
     branch = grad_hidden.astype(bf16)
     grad_attn = dot_nt(branch, output_full).astype(bf16).reshape(rows, shards, wide)
-    grad_heads = exchange(jnp.swapaxes(grad_attn, 0, 1)).reshape(shards, seqs, span, wide)
-    output_sum = scatter(outer_sum(attn, branch))
-    grad_heads, gate_part, up_part = tie(grad_heads, gate_part, up_part)
-    gate_part, down_grad = tie(gate_part, down_grad)
-    gate_sum = lax.psum(gate_part, "replica")
-    up_part, gate_sum = tie(up_part, gate_sum)
-    up_sum = lax.psum(up_part, "replica")
-    grad_qkv = attention_backward(
-        heads, qkv, grad_heads, norms, seg_col, seg_row, cos_all, sin_all
-    )
-    grad_qkv = exchange(grad_qkv.reshape(shards, rows, part))
+    inner_blocks, _, grad_qkv, _, _, out_land, total, *summed = tail(
+        heads, down_part, gate_part, up_part, outs, jnp.swapaxes(grad_attn, 0, 1), qkv, normed_one,
+        attn, branch, norms, seg_col, seg_row, cos_all, sin_all,
+    )
+    out_sum = lax.dynamic_index_in_dim(outs, me // 2, 0, keepdims=False).astype(f32)
+    out_sum = out_sum + jnp.sum(out_land[1:].astype(f32), 0)
+    block_out = (hidden + out_sum).astype(bf16)
     grad_qkv = jnp.swapaxes(grad_qkv, 0, 1).reshape(rows, shards * part)
     grad_one = dot_nt(grad_qkv, qkv_full)
-    qkv_sum = scatter(outer_sum(normed_one, grad_qkv))
-    qkv_sum, gate_sum, output_sum, up_sum = tie(qkv_sum, gate_sum, output_sum, up_sum)
-    output_grad = replica_sum(output_sum)
-    qkv_grad = replica_sum(qkv_sum)
-    qkv_grad = qkv_grad.reshape(owned, shards, part)
+    if replicas != 4:
+
+        def side_by_side(some):
+            return jnp.swapaxes(some, 0, 1).reshape(owned, some.shape[0] * hidden_share)
+
+        summed = lax.psum(
+            (
+                down_part, side_by_side(inner_blocks[0]), side_by_side(inner_blocks[1]),
+                side_by_side(total),
+            ),
+            "replica",
+        )
+    down_grad, gate_grad, up_grad, rest = [some.astype(f32) for some in summed]
+    qkv_grad = rest[:, : shards * part].reshape(owned, shards, part)
+    output_grad = rest[:, shards * part :]
+
+    own_one, own_two = attention_gain.astype(f32), mlp_gain.astype(f32)
+    gain_one_grad = jnp.sum(qkv_owned.astype(f32) * rest[:, : shards * part], 1) / own_one
+    gain_two_grad = (
+        jnp.sum(gate_weight.astype(f32) * gate_grad + up_weight.astype(f32) * up_grad, 1) / own_two
+    )
 
     def kv_grad(columns):
         return jnp.sum(columns.reshape(owned, KV_HEADS, copies, HEAD_DIM), 2).reshape(
@@ -690,22 +1122,19 @@
     query_grad = qkv_grad[:, :, :wide].reshape(owned, HEADS * HEAD_DIM)
     key_grad = kv_grad(qkv_grad[:, :, wide : wide + HEAD_DIM])
     value_grad = kv_grad(qkv_grad[:, :, wide + HEAD_DIM :])
-    first_grad = jnp.sum(grad_one * unit_one, 0)
     token_grad = grad_hidden + norm_back(grad_one, unit_one, scale_one, gain_one)
-    gain_grads = lax.psum(jnp.stack([first_grad, second_grad]), ("replica", "shard"))
-    gain_grads = lax.dynamic_slice_in_dim(gain_grads, me * owned, owned, 1)
     return (
         block_out.reshape(seqs, span, width),
         token_grad.reshape(seqs, span, width),
-        gain_grads[0],
+        gain_one_grad,
         query_grad,
         key_grad,
         value_grad,
         output_grad,
-        gain_grads[1],
-        to_rows(gate_sum),
-        to_rows(up_sum),
-        down_grad.astype(f32),
+        gain_two_grad,
+        gate_grad,
+        up_grad,
+        down_grad,
     )
 
 

time: 1630 us -> 1090 us (0.67)
  waiting for transfers between devices: 876 us -> 94.7 us
  Pallas kernels: 289 us -> 659 us
  blocking collectives: 222 us -> 93.7 us
  local copies, waits for them, and re-layouts: 54.6 us -> 80.5 us
  matrix products: 60.5 us -> 39.4 us
    pallas_call x1, Pallas kernels: 39.6 us -> 392 us  [tail(): pl.pallas_call(functools.partial(tail_kernel, heads), in_specs=[hbm] * 9...]
    psum x4 -> x0, waiting for transfers between devices: 324 us -> none  [the longest x1 156 us: body(): gate_sum = lax.psum(gate_part, 'replica')]
    reduce_scatter x2 -> x0, waiting for transfers between devices: 171 us -> none  [scatter(): lax.psum_scatter(partial.astype(bf16), 'shard', scatter_dimension=0, tile...]
    all_gather x1 -> x0, waiting for transfers between devices: 130 us -> none  [body(): gate_up = lax.all_gather(gate_up_part, 'replica')]
    all_to_all x3 -> x0, blocking collectives: 113 us -> none  [the longest x2 83 us: exchange(): return lax.all_to_all(blocks, 'shard', 0, 0, tiled=True)]
    all_to_all x4 -> x2, waiting for transfers between devices: 128 us -> 22 us  [exchange(): return lax.all_to_all(blocks, 'shard', 0, 0, tiled=True)]
    psum x1 -> x0, blocking collectives: 44.4 us -> none  [body(): lax.psum(jnp.stack([first_grad, second_grad]), ('replica', 'shard'))]
    unnamed x12 -> x3, waiting for transfers between devices: 44.9 us -> 0.73 us
  transfers between devices with their start and end apart: 17 -> 14, of which waited for: 12 -> 3; matrix products, arithmetic and copies ran while one was open for 10% -> 8% of each run, Pallas kernels for 5% -> 4%
where the time goes in v3:
time: 1090 us; the launch traced here: 1080 us
  Pallas kernels  659 us (60%)
  waiting for transfers between devices  94.7 us (9%)
  blocking collectives  93.7 us (9%)
  local copies, waits for them, and re-layouts  80.5 us (7%)
  other arithmetic  70.6 us (6%)
  matrix products  39.4 us (4%)
  starting transfers between devices  26.8 us (2%)
  between operations  14.9 us (1%)
    pallas_call x1, Pallas kernels, tail(): pl.pallas_call(functools.partial(tail_kernel, heads), in_specs=[hbm] * 9...  392 us
    pallas_call x1, Pallas kernels, feed_forward(): pl.pallas_call(feed_kernel, in_specs=[hbm] * 6, out_specs=(hbm,) * len(ou...  227 us
    all_gather x1, blocking collectives, body(): lax.all_gather(jnp.stack([segments, positions]), 'shard', axis=2, tiled=T...  53.3 us
    all_gather x1, blocking collectives, body(): lax.all_gather(jnp.stack([attention_gain, mlp_gain]), 'shard', axis=1, ti...  40.5 us
    ppermute x3, waiting for transfers between devices, line_step(): lax.ppermute(left, 'replica', down_pairs)  40.3 us
    pallas_call x1, Pallas kernels, attention_forward(): pl.pallas_call(functools.partial(forward_kernel, heads, 256), grid=(seqs,...  39.8 us
    all_gather x2, waiting for transfers between devices, gather(): return lax.all_gather(block, 'shard', axis=0, tiled=True)  31.7 us
    unnamed x81, local copies, waits for them, and re-layouts  22 us
  transfers between devices with their start and end apart: 14, of which 3 were waited for; matrix products, arithmetic and copies ran while one was open for 8% of the time, Pallas kernels for 4%

profile of v3, /device:TPU:0, one launch (start us, length us, event | category | flops | bytes accessed | tf_op | source)
XLA Modules:
  0.0 1079.7 jit_solution(12156809860906029910)
XLA Ops:
  18.6 4.2 copy.52
  22.8 5.3 all-to-all-start
  28.7 40.5 %all_gather.15 = bf16[2,2048]{1,0:T(2,128)(2,1)S(1)} all-gather(bf16[2,256]{1,0:T(2,128)(2,1)S(1)} %pad_maximum_fusion.3), channel_id=1, replica_groups=mesh['replica'=4,'shard'=8] {'shard'}, dimensions={1}, use_global_device_ids=true | all-gather | bytes 9216 | tf_op jit(solution)/shard_map/all_gather | solution.py:1037
  73.1 4.7 collective-permute-start
  79.1 31.7 %all-gather.4.cloned.1.call-done = bf16[2048,3072]{1,0:T(8,128)(2,1)} async-done(((bf16[256,3072]{1,0:T(8,128)(2,1)}), bf16[2048,3072]{1,0:T(8,128)(2,1)}) %all-gather.4.cloned.1.call-update) | async-done | bytes 12582928 | tf_op jit(solution)/shard_map/all_gather | solution.py:967
  110.9 16.6 %copy.67 = bf16[3072,2048]{1,0:T(8,128)(2,1)} copy(bf16[3072,2048]{0,1:T(8,128)(2,1)} %bitcast.103) | data formatting | bytes 25165824 | tf_op jit(solution)/shard_map/dot_general | solution.py:37
  127.4 10.0 fusion.17
  141.7 4.6 all-to-all-start.1
  149.7 53.3 %all_gather.17 = s32[2,4,1024]{2,0,1:T(2,128)S(1)} all-gather(s32[2,4,128]{2,0,1:T(2,128)S(1)} %pad_add_fusion), channel_id=1, replica_groups=mesh['replica'=4,'shard'=8] {'shard'}, dimensions={2}, use_global_device_ids=true | all-gather | bytes 36864 | tf_op jit(solution)/shard_map/all_gather | solution.py:1039
  203.6 5.2 copy.55
  208.9 39.8 %shard_map.212 = (bf16[8,4,128,256]{3,2,1,0:T(8,128)(2,1)}, f32[4,4,1024]{2,1,0:T(4,128)S(1)}) custom-call(bf16[8,4,128,384]{3,2,1,0:T(8,128)(2,1)} %bitcast.115, s32[4,1024,1]{2,1,0:T(8,128)S(1)} %copy.56.seg_col_ref, s32[4,1,1024]{2,1,0:T(1,128)S(1)} %get-tuple-element.81.seg_row_ref), custom_call_target="tpu_custom_call" | custom-call | flops 4294967296 | bytes 6291456 | tf_op jit(solution)/shard_map/pallas_call | solution.py:131
  251.5 4.5 broadcast_in_dim.28
  256.0 3.2 bitcast_dynamic-update-slice_fusion.3
  259.1 40.3 %collective-permute-done.4 = bf16[2,4,64,2048]{3,2,1,0:T(8,128)(2,1)} collective-permute-done((bf16[2,4,64,2048]{3,2,1,0:T(8,128)(2,1)}, bf16[2,4,64,2048]{3,2,1,0:T(8,128)(2,1)}, u32[]{:S(2)}, u32[]{:S(2)}) %collective-permute-start.4) | collective-permute-done | bytes 2097184 | tf_op jit(solution)/shard_map/ppermute | solution.py:1015
  299.4 3.8 bitcast_dynamic-update-slice_fusion.2
  303.2 3.8 bitcast_dynamic-update-slice_fusion.1
  307.1 3.7 bitcast_dynamic-update-slice_fusion.own_ref
  311.3 4.9 all-to-all-start.2
  320.9 22.0 %all-to-all-done.2 = bf16[8,512,256]{2,1,0:T(8,128)(2,1)} async-done(((bf16[8,512,256]{2,1,0:T(8,128)(2,1)}), bf16[8,512,256]{2,1,0:T(8,128)(2,1)}, u32[]{:S(2)}, u32[]{:S(2)}) %all-to-all-start.2) | async-done | bytes 2097184 | tf_op jit(solution)/shard_map/all_to_all | solution.py:952
  342.8 3.2 copy.71
  346.0 7.7 multiply_reduce_fusion.1
  357.5 226.9 %shard_map.213 = (bf16[4,512,2048]{2,1,0:T(8,128)(2,1)}, bf16[4,512,2048]{2,1,0:T(8,128)(2,1)}, bf16[2048,2048]{1,0:T(8,128)(2,1)}, bf16[2048,2048]{1,0:T(8,128)...) custom-call(bf16[512,2048]{1,0:T(8,128)(2,1)} %multiply_convert_fusi, ...), custom_call_target="tpu_custom_call" | custom-call | flops 154618822656 | bytes 134217728 | tf_op jit(solution)/shard_map/pallas_call | solution.py:493
  584.5 5.8 convert_reduce_fusion
  596.0 9.1 convolution_convert_fusion
  610.7 392.4 %shard_map.214 = (bf16[2,8,256,1024]{3,2,1,0:T(8,128)(2,1)}, bf16[8,512,256]{2,1,0:T(8,128)(2,1)}, bf16[8,512,384]{2,1,0:T(8,128)(2,1)}, bf16[29,256,1024]{2,1,0...) custom-call(bf16[1024,2048]{1,0:T(8,128)(2,1)} %get-tuple-element.38, ...), custom_call_target="tpu_custom_call" | custom-call | flops 10737418240 | bytes 536870912 | tf_op jit(solution)/shard_map/pallas_call | solution.py:913
  1003.1 4.9 convert_element_type.112
  1013.3 5.0 copy.62
  1018.3 12.6 %fusion.6 = (f32[512]{0:T(512)S(1)}, f32[512,2048]{1,0:T(8,128)}) fusion(bf16[4,128,2048]{2,1,0:T(8,128)(2,1)S(1)} %copy-done.10, f32[2048]{0:T(1024)S(1)} %bitcast.136, f32[512]{0:T(512)S(1)} %copy-done.26, bf16[512,3072]{0,1:T(8,128)(2,1)} %bitcast.118, bf16[2048,3072]{1,0:T(8,128)(2,1)} %all-gather.4.cloned.1.call-done), kind=kOutput, calls=%fused_computation.17 | convolution fusion | flops 6447693312 | bytes 22032384 | tf_op jit(solution)/shard_map/dot_general | solution.py:33
  1030.9 3.4 convert_reduce_fusion.1
  1046.6 6.8 convert_element_type.119
  1053.5 11.1 %add_reduce_fusion = (f32[256]{0:T(256)S(1)}, f32[256,8192]{1,0:T(8,128)}, f32[256,8192]{1,0:T(8,128)}) fusion(bf16[256,8192]{1,0:T(8,128)(2,1)S(1)} %copy-done.15, bf16[256,8192]{1,0:T(8,128)(2,1)S(1)} %copy-done.14, bf16[256,8192]{1,0:T(8,128)(2,1)} %get-tuple-element.46, bf16[256,8192]{1,0:T(8,128)(2,1)} %get-tuple-element.47), kind=kLoop, calls=%fused_computation.4 | loop fusion | flops 16776960 | bytes 33555456 | tf_op jit(solution)/shard_map/reduce_sum | solution.py:1114
  1065.1 7.6 fusion.9
  (146 shorter events, 66.4 us)
Async XLA Ops:
  7.2 103.7 %all-gather.4.cloned.1.call-start = ((), (), s32[]{:S(2)}) async-start(), calls=%async_computation.3 | async-start | bytes 14155776 | tf_op jit(solution)/shard_map/all_gather | solution.py:967
  13.4 332.6 %all-gather.6.cloned.1.call-start = ((), (), s32[]{:S(2)}) async-start(), calls=%async_computation.4 | async-start | bytes 9437184 | tf_op jit(solution)/shard_map/all_gather | solution.py:967
  18.6 9.5 copy-start.29
  18.6 9.5 copy-start.31
  18.6 9.5 copy-start.8
  22.8 46.3 %copy-start.27 = (s32[4,128]{1,0:T(4,128)S(1)}, s32[4,128]{1,0:T(4,128)}, u32[]{:S(2)}) copy-start(s32[4,128]{1,0:T(4,128)} %param.15) | copy-start | bytes 6148
  22.8 48.6 %all-to-all-start = ((bf16[2,4,64,2048]{3,2,0,1:T(8,128)(2,1)}), bf16[2,4,64,2048]{3,2,0,1:T(8,128)(2,1)}, u32[]{:S(2)}, u32[]{:S(2)}) async-start(bf16[2,4,64,2048]{3,2,0,1:T(8,128)(2,1)} %copy.52), calls=%async_computation | async-start | bytes 4194304 | tf_op jit(solution)/shard_map/all_to_all | solution.py:1006
  28.6 290.3 %copy-start.25 = (f32[512]{0:T(512)}, f32[512]{0:T(512)S(1)}, u32[]{:S(2)}) copy-start(f32[512]{0:T(512)S(1)} %get-tuple-element.89) | copy-start | bytes 6148
  69.5 249.5 %copy-start.21 = (f32[1,2048]{1,0:T(1,128)}, f32[1,2048]{1,0:T(1,128)S(1)}, u32[]{:S(2)}) copy-start(f32[1,2048]{1,0:T(1,128)S(1)} %get-tuple-element.86) | copy-start | bytes 24580
  69.5 284.3 %copy-start.19 = (f32[1,2048]{1,0:T(1,128)}, f32[1,2048]{1,0:T(1,128)S(1)}, u32[]{:S(2)}) copy-start(f32[1,2048]{1,0:T(1,128)S(1)} %get-tuple-element.85) | copy-start | bytes 24580
  73.1 68.5 %collective-permute-start = (bf16[2,4,64,2048]{3,2,1,0:T(8,128)(2,1)S(1)}, bf16[2,4,64,2048]{3,2,1,0:T(8,128)(2,1)}, u32[]{:S(2)}, u32[]{:S(2)}) collective-permute-start(bf16[2,4,64,2048]{3,2,1,0:T(8,128)(2,1)S(1)} %copy.53), channel_id=1, source_target_pairs={{0,8},{8,16},{16,24},{1,9},{9,17},{17,25},{2,10},{10,18},{18,26},{... | collective-permute-start | bytes 6291464 | tf_op jit(solution)/shard_map/ppermute | solution.py:1015
  77.8 63.8 %collective-permute-start.1 = (bf16[2,4,64,2048]{3,2,1,0:T(8,128)(2,1)S(1)}, bf16[2,4,64,2048]{3,2,1,0:T(8,128)(2,1)}, u32[]{:S(2)}, u32[]{:S(2)}) collective-permute-start(bf16[2,4,64,2048]{3,2,1,0:T(8,128)(2,1)S(1)} %copy.53), channel_id=1, source_target_pairs={{24,16},{16,8},{8,0},{25,17},{17,9},{9,1},{26,18},{18,10},{10,2},{... | collective-permute-start | bytes 6291464 | tf_op jit(solution)/shard_map/ppermute | solution.py:1015
  141.7 8.0 copy-start.28
  141.7 62.0 %all-to-all-start.1 = ((bf16[8,512,384]{1,2,0:T(8,128)(2,1)}), bf16[8,512,384]{1,2,0:T(8,128)(2,1)}, u32[]{:S(2)}, u32[]{:S(2)}) async-start(bf16[8,512,384]{1,2,0:T(8,128)(2,1)} %bitcast.14), calls=%async_computation.1 | async-start | bytes 6291456 | tf_op jit(solution)/shard_map/all_to_all | solution.py:952
  146.3 211.3 %all-gather.8.cloned.1.call-start = ((), (), s32[]{:S(2)}) async-start(), calls=%async_computation.5 | async-start | bytes 10485760 | tf_op jit(solution)/shard_map/all_gather | solution.py:1027
  146.3 103.0 %collective-permute-start.2 = (bf16[2,4,64,2048]{3,2,1,0:T(8,128)(2,1)}, bf16[2,4,64,2048]{3,2,1,0:T(8,128)(2,1)}, u32[]{:S(2)}, u32[]{:S(2)}) collective-permute-start(bf16[2,4,64,2048]{3,2,1,0:T(8,128)(2,1)} %collective-permute-done), channel_id=1, source_target_pairs={{8,16},{16,24},{9,17},{17,25},{10,18},{18,26},{11,19},{19,27},{12,... | collective-permute-start | bytes 6291464 | tf_op jit(solution)/shard_map/ppermute | solution.py:1015
  148.3 101.0 %collective-permute-start.3 = (bf16[2,4,64,2048]{3,2,1,0:T(8,128)(2,1)}, bf16[2,4,64,2048]{3,2,1,0:T(8,128)(2,1)}, u32[]{:S(2)}, u32[]{:S(2)}) collective-permute-start(bf16[2,4,64,2048]{3,2,1,0:T(8,128)(2,1)} %collective-permute-done.1), channel_id=1, source_target_pairs={{16,8},{8,0},{17,9},{9,1},{18,10},{10,2},{19,11},{11,3},{20,12},{1... | collective-permute-start | bytes 6291464 | tf_op jit(solution)/shard_map/ppermute | solution.py:1015
  203.6 45.1 %copy-start = (s32[4,1024,1]{2,1,0:T(8,128)}, s32[4,1024,1]{2,1,0:T(8,128)S(1)}, u32[]{:S(2)}) copy-start(s32[4,1024,1]{2,1,0:T(8,128)S(1)} %copy.56.seg_col_ref) | copy-start | bytes 49156
  249.3 50.1 %collective-permute-start.4 = (bf16[2,4,64,2048]{3,2,1,0:T(8,128)(2,1)}, bf16[2,4,64,2048]{3,2,1,0:T(8,128)(2,1)}, u32[]{:S(2)}, u32[]{:S(2)}) collective-permute-start(bf16[2,4,64,2048]{3,2,1,0:T(8,128)(2,1)} %collective-permute-done.3), channel_id=1, source_target_pairs={{8,0},{9,1},{10,2},{11,3},{12,4},{13,5},{14,6},{15,7}} | collective-permute-start | bytes 6291464 | tf_op jit(solution)/shard_map/ppermute | solution.py:1015
  250.6 56.4 %collective-permute-start.5 = (bf16[2,4,64,2048]{3,2,1,0:T(8,128)(2,1)}, bf16[2,4,64,2048]{3,2,1,0:T(8,128)(2,1)S(1)}, u32[]{:S(2)}, u32[]{:S(2)}) collective-permute-start(bf16[2,4,64,2048]{3,2,1,0:T(8,128)(2,1)} %collective-permute-done.2), channel_id=1, source_target_pairs={{16,24},{17,25},{18,26},{19,27},{20,28},{21,29},{22,30},{23,31}} | collective-permute-start | bytes 6291464 | tf_op jit(solution)/shard_map/ppermute | solution.py:1015
  310.8 8.2 copy-start.9
  310.8 46.8 %collective-permute-start.6 = (bf16[4,2,4,64,2048]{4,3,2,1,0:T(8,128)(2,1)}, bf16[4,2,4,64,2048]{4,3,2,1,0:T(8,128)(2,1)}, u32[]{:S(2)}, u32[]{:S(2)}) collective-permute-start(bf16[4,2,4,64,2048]{4,3,2,1,0:T(8,128)(2,1)} %bitcast_dynamic-update-slice_fusion.own_ref), channel_id=1, source_target_pairs={{0,1},{1,0},{2,3},{3,2},{4,5},{5,4},{6,7},{7,6},{8,9},{9,8},{10,11... | collective-permute-start | bytes 25165832 | tf_op jit(solution)/shard_map/ppermute | solution.py:1078
  310.8 46.8 %collective-permute-start.7 = (bf16[1024,2048]{1,0:T(8,128)(2,1)}, bf16[1024,2048]{1,0:T(8,128)(2,1)}, u32[]{:S(2)}, u32[]{:S(2)}) collective-permute-start(bf16[1024,2048]{1,0:T(8,128)(2,1)} %down_own_ref.1), channel_id=1, source_target_pairs={{0,1},{1,0},{2,3},{3,2},{4,5},{5,4},{6,7},{7,6},{8,9},{9,8},{10,11... | collective-permute-start | bytes 12582920 | tf_op jit(solution)/shard_map/ppermute | solution.py:1025
  311.3 31.6 %all-to-all-start.2 = ((bf16[8,512,256]{2,1,0:T(8,128)(2,1)}), bf16[8,512,256]{2,1,0:T(8,128)(2,1)}, u32[]{:S(2)}, u32[]{:S(2)}) async-start(bf16[8,512,256]{2,1,0:T(8,128)(2,1)} %bitcast.20), calls=%async_computation.2 | async-start | bytes 4194304 | tf_op jit(solution)/shard_map/all_to_all | solution.py:952
  1018.3 12.6 %slice-start = ((s8[8388608]{0:T(1024)(128)(4,1)}), s8[4194304]{0:T(1024)(128)(4,1)S(1)}, s32[]{:S(2)}) async-start(s8[8388608]{0:T(1024)(128)(4,1)} %bitcast.111), calls=%async_computation.6 | async-start | bytes 8388608
  1018.3 12.6 %slice-start.1 = ((s8[8388608]{0:T(1024)(128)(4,1)}), s8[4194304]{0:T(1024)(128)(4,1)S(1)}, s32[]{:S(2)}) async-start(s8[8388608]{0:T(1024)(128)(4,1)} %bitcast.111), calls=%async_computation.7 | async-start | bytes 8388608
  1046.6 6.8 copy-start.15
  1053.4 11.1 %copy-start.30 = (bf16[256]{0:T(256)(128)(2,1)S(1)}, bf16[256]{0:T(256)(128)(2,1)}, u32[]{:S(2)}) copy-start(bf16[256]{0:T(256)(128)(2,1)} %param.22) | copy-start | bytes 1540
  1053.4 11.1 %copy-start.32 = (bf16[256]{0:T(256)(128)(2,1)S(1)}, bf16[256]{0:T(256)(128)(2,1)}, u32[]{:S(2)}) copy-start(bf16[256]{0:T(256)(128)(2,1)} %param.17) | copy-start | bytes 1540
  1053.4 11.7 %copy-start.4 = (f32[512,2048]{1,0:T(8,128)S(1)}, f32[512,2048]{1,0:T(8,128)}, u32[]{:S(2)}) copy-start(f32[512,2048]{1,0:T(8,128)} %copy-done.3) | copy-start | bytes 12582916
  1053.4 11.7 %copy-start.7 = (f32[512,2048]{1,0:T(8,128)S(1)}, f32[512,2048]{1,0:T(8,128)}, u32[]{:S(2)}) copy-start(f32[512,2048]{1,0:T(8,128)} %copy-done.5) | copy-start | bytes 12582916
  1053.4 11.7 %copy-start.13 = (bf16[4,128,2048]{2,1,0:T(8,128)(2,1)S(1)}, bf16[4,128,2048]{2,1,0:T(8,128)(2,1)}, u32[]{:S(2)}) copy-start(bf16[4,128,2048]{2,1,0:T(8,128)(2,1)} %param.16) | copy-start | bytes 6291460
  (17 other events, 69.1 us)
Sparse Core Ops, SparseCore 0:
  13.5 97.3 all-gather.3
  112.7 78.6 all-gather.5
  193.3 96.0 all-gather.7

commit v4 on v3

--- a/solution.py
+++ b/solution.py
@@ -45,21 +45,18 @@
     return jnp.where(allowed, 0.0, masked_score)
 
 
-def forward_kernel(heads, rows, qkv_ref, seg_col_ref, seg_row_ref, out_ref, norm_ref):
-    shards, _, span, _ = qkv_ref.shape
+def attention_fore(heads, rows, qkv_ref, seg_col, seg_row, out_ref, norm_ref):
+    shards, span, _ = qkv_ref.shape
     length = shards * span
     wide = heads * HEAD_DIM
-    seg_col, seg_row = seg_col_ref[0], seg_row_ref[0]
-    keys = qkv_ref[:, 0, :, wide : wide + HEAD_DIM].reshape(length, HEAD_DIM)
-    values = qkv_ref[:, 0, :, wide + HEAD_DIM :].reshape(length, HEAD_DIM)
+    keys = qkv_ref[:, :, wide : wide + HEAD_DIM].reshape(length, HEAD_DIM)
+    values = qkv_ref[:, :, wide + HEAD_DIM :].reshape(length, HEAD_DIM)
     values_t = values.astype(f32).T.astype(bf16)
     for first in range(0, length, rows):
         last = first + rows
+        at = slice(first // span, last // span)
         bias = score_bias(seg_col, seg_row, first, rows)
-        queries = (
-            qkv_ref[first // span : last // span, 0, :, :wide].reshape(rows, wide)
-            * HEAD_DIM ** (-0.5)
-        )
+        queries = qkv_ref[at, :, :wide].reshape(rows, wide) * HEAD_DIM ** (-0.5)
         parts = []
         for head in range(heads):
             one = queries[:, head * HEAD_DIM : (head + 1) * HEAD_DIM]
@@ -69,9 +66,9 @@
             total = jnp.sum(lifted, 0, keepdims=True)
             probs = (lifted * (1.0 / total)).astype(bf16)
             parts.append(dot_nn(values_t[:, :last], probs))
-            norm_ref[0, head : head + 1, first:last] = top + jnp.log(total)
+            norm_ref[head : head + 1, first:last] = top + jnp.log(total)
         out = jnp.concatenate(parts, 0).T.astype(bf16)
-        out_ref[first // span : last // span, 0] = out.reshape(rows // span, span, wide)
+        out_ref[at] = out.reshape(rows // span, span, wide)
 
 
 def turn_back(part, cosine, sine):
@@ -116,37 +113,6 @@
     out_ref[:, :, wide:] = both.astype(bf16).reshape(shards, span, 2 * HEAD_DIM)
 
 
-def by_sequence(shape, axis):
-    block = tuple(1 if at == axis else size for at, size in enumerate(shape))
-    return pl.BlockSpec(block, lambda i: tuple(i if at == axis else 0 for at in range(len(shape))))
-
-
-def attention_forward(heads, qkv, seg_col, seg_row):
-    shards, seqs, span, _ = qkv.shape
-    length = shards * span
-    out_shape = (
-        jax.ShapeDtypeStruct((shards, seqs, span, heads * HEAD_DIM), bf16),
-        jax.ShapeDtypeStruct((seqs, heads, length), f32),
-    )
-    return pl.pallas_call(
-        functools.partial(forward_kernel, heads, 256),
-        grid=(seqs,),
-        in_specs=[
-            by_sequence(qkv.shape, 1),
-            by_sequence(seg_col.shape, 0),
-            by_sequence(seg_row.shape, 0),
-        ],
-        out_specs=(by_sequence(out_shape[0].shape, 1), by_sequence(out_shape[1].shape, 0)),
-        out_shape=out_shape,
-        compiler_params=pltpu.CompilerParams(vmem_limit_bytes=48 * 2**20),
-        cost_estimate=pl.CostEstimate(
-            flops=4 * seqs * heads * length * length * HEAD_DIM,
-            bytes_accessed=2 * qkv.size * 2,
-            transcendentals=seqs * heads * length * length,
-        ),
-    )(qkv, seg_col, seg_row)
-
-
 def chip_at(chip, distance):
     result, bit = chip, 1
     while bit <= distance:
@@ -156,6 +122,358 @@
     return result
 
 
+def head_kernel(
+    heads,
+    share_ref, weight_ref, output_ref, normed_ref, cos_ref, sin_ref, seg_col_ref, seg_row_ref,
+    share_land, weight_out, output_land, qkv_land, attn_land, norm_ref,
+    weights, normed, made, qkv, attended,
+    share_send, share_recv, line_send, line_recv, swap_send, swap_recv,
+    weight_send, weight_recv, near_send, near_recv, output_send, output_recv, close_send, close_recv,
+    qkv_send, qkv_recv, attn_send, attn_recv, self_sem, load_sem,
+):
+    shards, owned, columns = weights.shape
+    chips = shards // 2
+    rows, width = normed_ref.shape
+    _, seqs, span, part = qkv_land.shape
+    wide = heads * HEAD_DIM
+    replicas = lax.axis_size("replica")
+    me, replica = lax.axis_index("shard"), lax.axis_index("replica")
+    chip, core = me // 2, me % 2
+    partner = [
+        chip_at(chip, d // 2) * 2 + (core if d % 2 == 0 else 1 - core) for d in range(shards)
+    ]
+    relay = chips == 4
+    half_owned = owned // 2
+
+    def remote(source, target, send, recv, shard, to=None):
+        return pltpu.make_async_remote_copy(
+            src_ref=source, dst_ref=target, send_sem=send, recv_sem=recv,
+            device_id=(replica if to is None else to, shard),
+            device_id_type=pl.DeviceIdType.MESH,
+        )
+
+    barrier = pltpu.get_barrier_semaphore()
+
+    def greet(to, shard):
+        pl.semaphore_signal(
+            barrier, inc=1, device_id=(to, shard), device_id_type=pl.DeviceIdType.MESH
+        )
+
+    for d in range(1, shards):
+        greet(replica, partner[d])
+    has_left, has_right = replica > 0, replica < replicas - 1
+
+    @pl.when(has_left)
+    def _():
+        greet(replica - 1, me)
+
+    @pl.when(has_right)
+    def _():
+        greet(replica + 1, me)
+
+    @pl.when(has_left & has_right)
+    def _():
+        pl.semaphore_wait(barrier, shards + 1)
+
+    @pl.when(jnp.logical_not(has_left & has_right))
+    def _():
+        pl.semaphore_wait(barrier, shards)
+
+    def share_copy(d):
+        return remote(
+            share_ref.at[chip_at(chip, d)], share_land.at[core, replica, chip],
+            share_send.at[d], share_recv.at[d], partner[2 * d],
+        )
+
+    own_share = pltpu.make_async_copy(
+        share_ref.at[chip], share_land.at[core, replica, chip], self_sem.at[0]
+    )
+    own_share.start()
+    for d in range(1, chips):
+        share_copy(d).start()
+
+    def rows_copies(ref, land, far_send, far_recv, side_send, side_recv):
+        def half(index):
+            return pl.ds(index * half_owned, half_owned)
+
+        def far(d, index):
+            if relay and d == 3:
+                origin, way = (1, 2) if index == 0 else (2, 1)
+                at = partner[2 * origin]
+                return remote(
+                    land.at[at, half(index)], land.at[at, half(index)],
+                    far_send.at[d, index], far_recv.at[d, index], partner[2 * way],
+                )
+            return remote(
+                ref.at[half(index)], land.at[me, half(index)],
+                far_send.at[d, index], far_recv.at[d, index], partner[2 * d],
+            )
+
+        def near(d, index):
+            at = partner[2 * d]
+            source = ref.at[half(index)] if d == 0 else land.at[at, half(index)]
+            return remote(
+                source, land.at[at, half(index)],
+                side_send.at[d, index], side_recv.at[d, index], partner[1],
+            )
+
+        return far, near
+
+    def start_rows(far, near):
+        for index in range(2):
+            for d in range(1, chips):
+                if not (relay and d == 3):
+                    far(d, index).start()
+        for index in range(2):
+            near(0, index).start()
+
+    def pass_rows(far, near):
+        if relay:
+            for index in range(2):
+                for d in (1, 2):
+                    far(d, index).wait_recv()
+                far(3, index).start()
+                for d in (1, 2):
+                    near(d, index).start()
+            for index in range(2):
+                far(3, index).wait_recv()
+                near(3, index).start()
+        else:
+            for d in range(1, chips):
+                for index in range(2):
+                    far(d, index).wait_recv()
+                    near(d, index).start()
+
+    def end_rows(far, near):
+        for d in range(chips):
+            for index in range(2):
+                near(d, index).wait_recv()
+
+    def sent_rows(far, near):
+        for d in range(chips):
+            for index in range(2):
+                near(d, index).wait_send()
+                if d > 0:
+                    far(d, index).wait_send()
+
+    weight_rows = rows_copies(
+        weight_ref, weights, weight_send, weight_recv, near_send, near_recv
+    )
+    output_rows = rows_copies(
+        output_ref, output_land, output_send, output_recv, close_send, close_recv
+    )
+    start_rows(*weight_rows)
+    own_weight = pltpu.make_async_copy(weight_ref, weights.at[me], self_sem.at[1])
+    own_weight.start()
+    own_output = pltpu.make_async_copy(output_ref, output_land.at[me], self_sem.at[2])
+    own_output.start()
+    take_normed = pltpu.make_async_copy(normed_ref, normed, load_sem.at[0])
+    take_normed.start()
+
+    def right_copy(step):
+        at = share_land.at[core, replica - step]
+        return remote(at, at, line_send.at[0, step], line_recv.at[0, step], me, replica + 1)
+
+    def left_copy(step):
+        at = share_land.at[core, replica + step]
+        return remote(at, at, line_send.at[1, step], line_recv.at[1, step], me, replica - 1)
+
+    def came(way, step):
+        at = share_land.at[core, replica - step - 1 if way == 0 else replica + step + 1]
+        return remote(at, at, line_send.at[way, step], line_recv.at[way, step], me)
+
+    def swap_copy(way, step):
+        at = share_land.at[core, replica - step if way == 0 else replica + step]
+        return remote(at, at, swap_send.at[way, step], swap_recv.at[way, step], partner[1])
+
+    def line_step(step):
+        if step == 0:
+            own_share.wait()
+            for d in range(1, chips):
+                share_copy(d).wait_recv()
+            swap_copy(0, 0).start()
+        for way in range(2):
+            room = replica - step >= 0 if way == 0 else replica + step < replicas
+            onward = has_right if way == 0 else has_left
+            if step > 0:
+
+                @pl.when(room)
+                def _():
+                    came(way, step - 1).wait_recv()
+                    swap_copy(way, step).start()
+
+            if step < replicas - 1:
+
+                @pl.when(room & onward)
+                def _():
+                    (right_copy if way == 0 else left_copy)(step).start()
+
+    line_step(0)
+    pass_rows(*weight_rows)
+    own_weight.wait()
+    take_normed.wait()
+    end_rows(*weight_rows)
+    keep_weight = pltpu.make_async_copy(weights, weight_out, self_sem.at[1])
+    keep_weight.start()
+
+    lane = lax.broadcasted_iota(jnp.int32, (rows, part), 1)
+    lower = lane % HEAD_DIM < HEAD_DIM // 2
+
+    def project(owner):
+        at = pl.ds(pl.multiple_of(owner * part, part), part)
+        value = dot_nn(normed[...], weights[:, :, at].reshape(width, part))
+        swapped = jnp.where(
+            lower,
+            pltpu.roll(value, part - HEAD_DIM // 2, 1),
+            pltpu.roll(value, HEAD_DIM // 2, 1),
+        )
+        turned = value * cos_ref[...] + swapped * sin_ref[...]
+        made[owner] = turned.astype(bf16)
+
+    @pl.loop(0, shards)
+    def _(k):
+        project(k)
+
+    def at_seq(s):
+        return pl.ds(pl.multiple_of(s * span, span), span)
+
+    def qkv_copy(d, s):
+        return remote(
+            made.at[partner[d], at_seq(s)], qkv_land.at[me, s],
+            qkv_send.at[d, s], qkv_recv.at[d, s], partner[d],
+        )
+
+    def own_qkv(s):
+        return pltpu.make_async_copy(made.at[me, at_seq(s)], qkv_land.at[me, s], load_sem.at[1 + s])
+
+    for s in range(seqs):
+        own_qkv(s).start()
+        for d in range(shards - 1, 0, -1):
+            qkv_copy(d, s).start()
+    start_rows(*output_rows)
+    if replicas > 2:
+        line_step(1)
+
+    def attn_copy(d, s):
+        return remote(
+            attended.at[s, partner[d]],
+            attn_land.at[at_seq(s), pl.ds(pl.multiple_of(me * wide, wide), wide)],
+            attn_send.at[d, s], attn_recv.at[d, s], partner[d],
+        )
+
+    def own_attn(s):
+        return pltpu.make_async_copy(
+            attended.at[s, me],
+            attn_land.at[at_seq(s), pl.ds(pl.multiple_of(me * wide, wide), wide)],
+            load_sem.at[1 + s],
+        )
+
+    @pl.loop(0, seqs)
+    def _(s):
+        own_qkv(s).wait()
+        for d in range(1, shards):
+            qkv_copy(d, s).wait_recv()
+        take = pltpu.make_async_copy(qkv_land.at[:, s], qkv, load_sem.at[0])
+        take.start()
+        take.wait()
+        attention_fore(
+            heads, 256, qkv, seg_col_ref[s], seg_row_ref[s], attended.at[s], norm_ref.at[s]
+        )
+        own_attn(s).start()
+        for d in range(1, shards):
+            attn_copy(d, s).start()
+
+    for step in range(2 if replicas > 2 else 1, replicas - 1):
+        line_step(step)
+    pass_rows(*output_rows)
+    for s in range(seqs):
+        own_attn(s).wait()
+        for d in range(1, shards):
+            attn_copy(d, s).wait_recv()
+    line_step(replicas - 1)
+
+    end_rows(*output_rows)
+    own_output.wait()
+    keep_weight.wait()
+    sent_rows(*weight_rows)
+    sent_rows(*output_rows)
+    for d in range(1, chips):
+        share_copy(d).wait_send()
+    for s in range(seqs):
+        for d in range(1, shards):
+            qkv_copy(d, s).wait_send()
+            attn_copy(d, s).wait_send()
+    swap_copy(0, 0).wait_send()
+    swap_copy(0, 0).wait_recv()
+    for way in range(2):
+        for step in range(replicas):
+            room = replica - step >= 0 if way == 0 else replica + step < replicas
+            onward = has_right if way == 0 else has_left
+            if step > 0:
+
+                @pl.when(room)
+                def _():
+                    swap_copy(way, step).wait_send()
+                    swap_copy(way, step).wait_recv()
+
+            if step < replicas - 1:
+
+                @pl.when(room & onward)
+                def _():
+                    (right_copy if way == 0 else left_copy)(step).wait_send()
+
+
+def head(heads, seqs, share, weight, output, normed, cosine, sine, seg_col, seg_row):
+    chips = share.shape[0]
+    shards = 2 * chips
+    rows, width = normed.shape
+    span = rows // seqs
+    owned, columns = weight.shape
+    part = columns // shards
+    wide = heads * HEAD_DIM
+    length = shards * span
+    replicas = lax.axis_size("replica")
+    hbm = pl.BlockSpec(memory_space=pl.ANY)
+    vmem = pl.BlockSpec(memory_space=pltpu.VMEM)
+    dma = pltpu.SemaphoreType.DMA
+
+    def low(*shape):
+        return jax.ShapeDtypeStruct(shape, bf16)
+
+    out_shape = (
+        low(2, replicas, *share.shape), low(shards, owned, columns), low(shards, owned, width),
+        low(shards, seqs, span, part), low(rows, shards * wide),
+        jax.ShapeDtypeStruct((seqs, heads, length), f32),
+    )
+    return pl.pallas_call(
+        functools.partial(head_kernel, heads),
+        in_specs=[hbm] * 4 + [vmem] * 4,
+        out_specs=(hbm,) * 5 + (vmem,),
+        out_shape=out_shape,
+        scratch_shapes=[
+            pltpu.VMEM((shards, owned, columns), bf16),
+            pltpu.VMEM((rows, width), bf16),
+            pltpu.VMEM((shards, rows, part), bf16),
+            pltpu.VMEM((shards, span, part), bf16),
+            pltpu.VMEM((seqs, shards, span, wide), bf16),
+            dma((chips,)), dma((chips,)), dma((2, replicas)), dma((2, replicas)),
+            dma((2, replicas)), dma((2, replicas)),
+            dma((chips, 2)), dma((chips, 2)), dma((chips, 2)), dma((chips, 2)),
+            dma((chips, 2)), dma((chips, 2)), dma((chips, 2)), dma((chips, 2)),
+            dma((shards, seqs)), dma((shards, seqs)), dma((shards, seqs)), dma((shards, seqs)),
+            dma((3,)), dma((1 + seqs,)),
+        ],
+        compiler_params=pltpu.CompilerParams(
+            collective_id=2, has_side_effects=True, vmem_limit_bytes=56 * 2**20
+        ),
+        cost_estimate=pl.CostEstimate(
+            flops=4 * seqs * heads * length * length * HEAD_DIM,
+            bytes_accessed=2**28,
+            transcendentals=seqs * heads * length * length,
+        ),
+    )(share, weight, output, normed, cosine, sine, seg_col, seg_row)
+
+
 def pieces_of(chips):
     if chips == 4:
         return [[(0, 0), (0, 1)], [(1, 0), (2, 0)], [(1, 1), (2, 1)], [(3, 0), (3, 1)]]
@@ -163,17 +481,17 @@
 
 
 def feed_kernel(
-    normed_ref, cot_ref, own_ref, other_ref, down_own_ref, down_other_ref,
-    partial_ref, out_ref, mixed_ref, gate_ref, up_ref,
+    normed_ref, cot_own_ref, share_ref, down_own_ref, down_other_ref,
+    cot_ref, partial_ref, out_ref, mixed_ref, gate_ref, up_ref,
     down_own_out, gate_own_out, up_own_out, down_got, gate_got, up_got,
     weights, normed, cot, inner, sent, out_stage,
-    weight_sem, normed_send, normed_recv, cot_sem, inner_sem, sum_send, sum_recv, own_sem, out_sem,
+    weight_sem, normed_send, normed_recv, far_send, far_recv, cot_sem, inner_sem, sum_send, sum_recv, own_sem, out_sem,
     core_send, core_recv, core_sem, load_sem,
 ):
     chips, rows, width = normed.shape
     units = mixed_ref.shape[1]
     half_rows, half_units = rows // 2, units // 2
-    replicas, _, _, share, _ = own_ref.shape
+    _, replicas, _, _, share, _ = share_ref.shape
     me = lax.axis_index("shard")
     replica = lax.axis_index("replica")
     chip, core = me // 2, me % 2
@@ -203,19 +521,29 @@
             normed_send.at[distance, part], normed_recv.at[distance, part], target,
         )
 
+    def far_copy(distance, part, source, target):
+        return remote(
+            source, cot_ref.at[distance, half(part)],
+            far_send.at[distance, part], far_recv.at[distance, part], target,
+        )
+
     relay = chips == 4
     direct = range(1, 3) if relay else range(1, chips)
     for part in range(2):
         for d in direct:
             token_copy(d, part, normed_ref.at[half(part)], partner[d]).start()
+        for d in direct:
+            far_copy(d, part, cot_own_ref.at[half(part)], partner[d]).start()
     own_copy = pltpu.make_async_copy(normed_ref, normed.at[0], own_sem.at[0])
     own_copy.start()
+    own_cot = pltpu.make_async_copy(cot_own_ref, cot_ref.at[0], own_sem.at[3])
+    own_cot.start()
 
     def cot_copies(index):
         return [
             pltpu.make_async_copy(
-                cot_ref.at[chip_at(chip, d), half(part)], cot.at[index % 2, half(at)],
-                cot_sem.at[index % 2, at],
+                (cot_own_ref if d == 0 else cot_ref.at[d]).at[half(part)],
+                cot.at[index % 2, half(at)], cot_sem.at[index % 2, at],
             )
             for at, (d, part) in enumerate(steps[index])
         ]
@@ -226,9 +554,9 @@
     for which in range(2):
         for k in range(chips):
             for z in range(replicas):
-                for ref, c in ((own_ref, core), (other_ref, 1 - core)):
+                for c in range(2):
                     pltpu.make_async_copy(
-                        ref.at[z, which, k],
+                        share_ref.at[c, z, k, which],
                         weights.at[which, pl.ds((2 * k + c) * owned + z * share, share), pl.ds(0, units)],
                         weight_sem.at[which],
                     ).start()
@@ -282,20 +610,24 @@
         parts = steps[index]
         for d, part in parts:
             if d > 0:
-                if relay and d == 3:
-                    source, way = (1, 2) if part == 0 else (2, 1)
-                    copy = token_copy(3, part, normed.at[source, half(part)], partner[way])
-                else:
-                    copy = token_copy(d, part, normed_ref.at[half(part)], partner[d])
-                copy.wait_recv()
+                for arrive, block, own in (
+                    (token_copy, normed, normed_ref), (far_copy, cot_ref, cot_own_ref)
+                ):
+                    if relay and d == 3:
+                        origin, way = (1, 2) if part == 0 else (2, 1)
+                        copy = arrive(3, part, block.at[origin, half(part)], partner[way])
+                    else:
+                        copy = arrive(d, part, own.at[half(part)], partner[d])
+                    copy.wait_recv()
         if relay and index in (1, 2):
-            part, source, way = (0, 1, 2) if index == 1 else (1, 2, 1)
-            token_copy(3, part, normed.at[source, half(part)], partner[way]).start()
+            part, origin, way = (0, 1, 2) if index == 1 else (1, 2, 1)
+            token_copy(3, part, normed.at[origin, half(part)], partner[way]).start()
+            far_copy(3, part, cot_ref.at[origin, half(part)], partner[way]).start()
+        if index > 0:
+            for copy in cot_copies(index):
+                copy.start()
         for copy in cot_copies(index):
             copy.wait()
-        if index + 1 < chips:
-            for copy in cot_copies(index + 1):
-                copy.start()
         if index > 0:
             for copy in inner_copies(index - 1):
                 copy.wait()
@@ -364,10 +696,11 @@
             ref, weights.at[which, pl.ds(0, tokens), pl.ds(0, units)], load_sem.at[which]
         )
 
+    own_cot.wait()
     loads = [load(mixed_ref, 0), load(gate_ref, 1)]
     cot_loads = [
         pltpu.make_async_copy(
-            cot_ref.at[chip_at(chip, d)], weights.at[2, pl.ds(d * rows, rows)], load_sem.at[3 + d]
+            cot_ref.at[d], weights.at[2, pl.ds(d * rows, rows)], load_sem.at[3 + d]
         )
         for d in range(chips)
     ]
@@ -465,14 +798,17 @@
     for d in range(1, chips):
         for part in range(2):
             if relay and d == 3:
-                source, way = (1, 2) if part == 0 else (2, 1)
-                token_copy(3, part, normed.at[source, half(part)], partner[way]).wait_send()
+                origin, way = (1, 2) if part == 0 else (2, 1)
+                token_copy(3, part, normed.at[origin, half(part)], partner[way]).wait_send()
+                far_copy(3, part, cot_ref.at[origin, half(part)], partner[way]).wait_send()
             else:
                 token_copy(d, part, normed_ref.at[half(part)], partner[d]).wait_send()
-
-
-def feed_forward(normed, cot, own, other, down_own, down_other):
-    chips, rows, width = cot.shape
+                far_copy(d, part, cot_own_ref.at[half(part)], partner[d]).wait_send()
+
+
+def feed_forward(normed, cot, share, down_own, down_other):
+    chips = share.shape[2]
+    rows, width = normed.shape
     units = down_own.shape[0] * 2
     half = units // 2
     tokens = chips * rows
@@ -484,7 +820,7 @@
         return jax.ShapeDtypeStruct(shape, bf16)
 
     out_shape = (
-        low(chips, rows, width), low(chips, rows, width),
+        low(chips, rows, width), low(chips, rows, width), low(chips, rows, width),
         low(tokens, units), low(tokens, units), low(tokens, units),
         low(half, width), low(width, half), low(width, half),
         low(half, width), low(width, half), low(width, half),
@@ -492,7 +828,7 @@
     depth = max(width, tokens)
     return pl.pallas_call(
         feed_kernel,
-        in_specs=[hbm] * 6,
+        in_specs=[hbm] * 5,
         out_specs=(hbm,) * len(out_shape),
         out_shape=out_shape,
         scratch_shapes=[
@@ -502,8 +838,8 @@
             pltpu.VMEM((3, rows, width), bf16),
             pltpu.VMEM((chips - 1, rows, width), bf16),
             pltpu.VMEM((rows, width), bf16),
-            dma((4,)), dma((chips, 2)), dma((chips, 2)), dma((2, 2)), dma((3, 2)),
-            dma((chips, 2)), dma((chips, 2)), dma((3,)), dma((2,)),
+            dma((4,)), dma((chips, 2)), dma((chips, 2)), dma((chips, 2)), dma((chips, 2)),
+            dma((2, 2)), dma((3, 2)), dma((chips, 2)), dma((chips, 2)), dma((4,)), dma((2,)),
             dma((3, tiles)), dma((3, tiles)), dma((4, tiles)), dma((3 + chips,)),
         ],
         compiler_params=pltpu.CompilerParams(
@@ -512,7 +848,7 @@
         cost_estimate=pl.CostEstimate(
             flops=18 * tokens * units * width, bytes_accessed=2**27, transcendentals=tokens * units
         ),
-    )(normed, cot, own, other, down_own, down_other)
+    )(normed, cot, share, down_own, down_other)
 
 
 def tail_kernel(
@@ -948,23 +1284,11 @@
     )(down, gate, up, outs, grads, qkv, normed, attn, branch, norms, *tables)
 
 
-def exchange(blocks):
-    return lax.all_to_all(blocks, "shard", 0, 0, tiled=True)
-
-
-def tie(*values):
-    return lax.optimization_barrier(values)
-
-
 def norm_back(grad_normed, unit_rows, scale_rows, gain_rows):
     scaled_grad = grad_normed * gain_rows
     return scale_rows * (
         scaled_grad - unit_rows * jnp.mean(scaled_grad * unit_rows, -1, keepdims=True)
     )
-
-
-def gather(block):
-    return lax.all_gather(block, "shard", axis=0, tiled=True)
 
 
 def body(
@@ -995,36 +1319,30 @@
     hidden_share = down_weight.shape[0]
 
     chips = shards // 2
-    same_core = [[2 * k + c for k in range(chips)] for c in range(2)]
+    replicas = lax.axis_size("replica")
     swap = [(i, i + 1 - 2 * (i % 2)) for i in range(shards)]
+
+    small = jnp.concatenate(
+        [
+            attention_gain.astype(f32), mlp_gain.astype(f32),
+            segments.astype(f32).reshape(rows), positions.astype(f32).reshape(rows),
+        ]
+    )
+    small = lax.all_gather(small, "shard")
+    gain_one, gain_two = small[:, :owned].reshape(width), small[:, owned : 2 * owned].reshape(width)
+    places = jnp.swapaxes(small[:, 2 * owned :].reshape(shards, 2, seqs, span), 0, 1)
+    places = jnp.swapaxes(places, 1, 2).reshape(2, seqs, length)
+    seg_row, seg_col = places[0][:, None, :], places[0][:, :, None]
+    angle_all = jnp.swapaxes(angles(places[1]), 1, 2)
+    cos_all, sin_all = jnp.cos(angle_all), jnp.sin(angle_all)
+
+    share = owned // replicas
     units = 2 * hidden_share
-    share = owned // lax.axis_size("replica")
-    gate_up_own = lax.dynamic_slice_in_dim(
+    share_own = lax.dynamic_slice_in_dim(
         jnp.stack([gate_weight, up_weight]), lax.axis_index("replica") * share, share, 1
     )
-    gate_up_own = jnp.transpose(gate_up_own.reshape(2, share, chips, units), (0, 2, 1, 3))
-    gate_up_part = lax.all_to_all(
-        gate_up_own, "shard", 1, 1, axis_index_groups=same_core, tiled=True
-    )
-    replicas = lax.axis_size("replica")
-    replica = lax.axis_index("replica")
-
-    def line_step(step, right, left):
-        up_pairs = [(i, i + 1) for i in range(step - 1, replicas - 1)]
-        down_pairs = [(replicas - 1 - i, replicas - 1 - j) for i, j in up_pairs]
-        return lax.ppermute(right, "replica", up_pairs), lax.ppermute(left, "replica", down_pairs)
-
-    rights, lefts = [gate_up_part], [gate_up_part]
-
-    def advance():
-        right, left = line_step(len(rights), rights[-1], lefts[-1])
-        rights.append(right)
-        lefts.append(left)
-
-    advance()
+    share_own = jnp.transpose(share_own.reshape(2, share, chips, units), (2, 0, 1, 3))
     down_other = lax.ppermute(down_weight, "shard", swap)
-    cot_rows = cotangent.reshape(rows, width)
-    cot_all = lax.all_gather(cot_rows, "shard", axis_index_groups=same_core)
 
     def per_head(weight):
         return jnp.repeat(weight.reshape(owned, KV_HEADS, HEAD_DIM), copies, axis=1)
@@ -1033,51 +1351,30 @@
         [query_weight.reshape(owned, shards, wide), per_head(key_weight), per_head(value_weight)],
         -1,
     ).reshape(owned, shards * part)
-    qkv_full = gather(qkv_owned)
-    gains = lax.all_gather(jnp.stack([attention_gain, mlp_gain]), "shard", axis=1, tiled=True)
-    gain_one, gain_two = gains[0].astype(f32), gains[1].astype(f32)
-    places = lax.all_gather(jnp.stack([segments, positions]), "shard", axis=2, tiled=True)
-    seg_row, seg_col = places[0][:, None, :], places[0][:, :, None]
-    angle_all = jnp.swapaxes(angles(places[1]), 1, 2)
-    cos_all, sin_all = jnp.cos(angle_all), jnp.sin(angle_all)
-    output_full = gather(output_weight)
 
     x = tokens.reshape(rows, width).astype(f32)
     scale_one = lax.rsqrt(jnp.mean(x * x, -1, keepdims=True) + epsilon)
     unit_one = x * scale_one
     normed_one = (unit_one * gain_one).astype(bf16)
-    projected = dot_nn(normed_one, qkv_full).reshape(rows, shards, part)
-    angle = angles(positions).reshape(rows, 1, 1, HEAD_DIM // 2)
+    angle = angles(positions).reshape(rows, HEAD_DIM // 2)
     cosine, sine = jnp.cos(angle), jnp.sin(angle)
-    turning = projected[:, :, : wide + HEAD_DIM].reshape(rows, shards, heads + 1, HEAD_DIM)
-    lower, upper = turning[..., : HEAD_DIM // 2], turning[..., HEAD_DIM // 2 :]
-    turned = jnp.concatenate(
-        [lower * cosine - upper * sine, upper * cosine + lower * sine], -1
-    ).reshape(rows, shards, wide + HEAD_DIM)
-    qkv_rows = jnp.concatenate([turned, projected[:, :, wide + HEAD_DIM :]], -1).astype(bf16)
-    qkv_rows, rights[-1], lefts[-1] = tie(qkv_rows, rights[-1], lefts[-1])
-    advance()
-    qkv = exchange(jnp.swapaxes(qkv_rows, 0, 1)).reshape(shards, seqs, span, part)
-
-    attn_heads, norms = attention_forward(heads, qkv, seg_col, seg_row)
-    attn_heads, rights[-1], lefts[-1] = tie(attn_heads, rights[-1], lefts[-1])
-    while len(rights) < replicas:
-        advance()
-    attn = exchange(attn_heads.reshape(shards, rows, wide))
-    attn = jnp.swapaxes(attn, 0, 1).reshape(rows, HEADS * HEAD_DIM)
+    still = jnp.ones((rows, HEAD_DIM), f32)
+    cos_lanes = jnp.concatenate([cosine] * (2 * heads + 2) + [still], 1)
+    sin_lanes = jnp.concatenate([-sine, sine] * (heads + 1) + [still * 0.0], 1)
+    shares, qkv_full, output_full, qkv, attn, norms = head(
+        heads, seqs, share_own, qkv_owned, output_weight, normed_one, cos_lanes, sin_lanes,
+        seg_col, seg_row,
+    )
+    qkv_full = qkv_full.reshape(width, shards * part)
+    output_full = output_full.reshape(width, width)
     hidden = x + dot_nn(attn, output_full)
     scale_two = lax.rsqrt(jnp.mean(hidden * hidden, -1, keepdims=True) + epsilon)
     unit_two = hidden * scale_two
     normed_two = (unit_two * gain_two).astype(bf16)
 
-    gate_up = jnp.zeros((replicas,) + gate_up_part.shape, bf16)
-    gate_up = lax.dynamic_update_index_in_dim(gate_up, gate_up_part, replica, 0)
-    for step in range(1, replicas):
-        block = jnp.where(replica >= step, rights[step], lefts[replicas - step])
-        gate_up = lax.dynamic_update_index_in_dim(gate_up, block, (replica - step) % replicas, 0)
-    gate_up_other = lax.ppermute(gate_up, "shard", swap)
-    partials, outs, _, _, _, down_part, gate_part, up_part, _, _, _ = feed_forward(
-        normed_two, cot_all, gate_up, gate_up_other, down_weight, down_other
+    cot_rows = cotangent.reshape(rows, width)
+    _, partials, outs, _, _, _, down_part, gate_part, up_part, _, _, _ = feed_forward(
+        normed_two, cot_rows, shares, down_weight, down_other
     )
     grad_two = jnp.sum(partials.astype(f32), 0)
     grad_hidden = cot_rows.astype(f32) + norm_back(grad_two, unit_two, scale_two, gain_two)

time: 1090 us -> 1020 us (0.936)
  Pallas kernels: 659 us -> 876 us
  waiting for transfers between devices: 94.7 us -> 0.01 us
  blocking collectives: 93.7 us -> 10.2 us
  local copies, waits for them, and re-layouts: 80.5 us -> 43 us
  starting transfers between devices: 26.8 us -> 0.52 us
  other arithmetic: 70.6 us -> 54 us
  between operations: 14.9 us -> 1.57 us
    pallas_call x2, Pallas kernels: 267 us -> 484 us  [the longest x1 282 us: feed_forward(): pl.pallas_call(feed_kernel, in_specs=[hbm] * 5, out_specs=(hbm,) * len(ou...]
    all_gather x2 -> x1, blocking collectives: 93.7 us -> 10.2 us  [body(): small = lax.all_gather(small, 'shard')]
    ppermute x7 -> x0, waiting for transfers between devices: 40.3 us -> none  [the longest x3 40.3 us: line_step(): lax.ppermute(left, 'replica', down_pairs)]
    all_gather x3 -> x0, waiting for transfers between devices: 31.7 us -> none  [the longest x2 31.7 us: gather(): return lax.all_gather(block, 'shard', axis=0, tiled=True)]
    all_to_all x3 -> x0, waiting for transfers between devices: 22 us -> none  [the longest x2 22 us: exchange(): return lax.all_to_all(blocks, 'shard', 0, 0, tiled=True)]
    dot_general x1 -> x0, local copies, waits for them, and re-layouts: 16.6 us -> none  [dot_nn(): lax.dot_general(left, right, (((1,), (0,)), ((), ())), preferred_element_...]
    all_to_all x3 -> x0, starting transfers between devices: 14.8 us -> none  [the longest x2 9.48 us: exchange(): return lax.all_to_all(blocks, 'shard', 0, 0, tiled=True)]
    ppermute x7 -> x0, starting transfers between devices: 11.4 us -> none  [the longest x3 7.54 us: line_step(): lax.ppermute(right, 'replica', up_pairs)]
  transfers between devices with their start and end apart: 14 -> 1, of which waited for: 3 -> 0; matrix products, arithmetic and copies ran while one was open for 8% -> 3% of each run, Pallas kernels for 4% -> 20%
where the time goes in v4:
time: 1020 us; the launch traced here: 1010 us
  Pallas kernels  876 us (86%)
  other arithmetic  54 us (5%)
  local copies, waits for them, and re-layouts  43 us (4%)
  matrix products  29.4 us (3%)
    pallas_call x1, Pallas kernels, tail(): pl.pallas_call(functools.partial(tail_kernel, heads), in_specs=[hbm] * 9...  392 us
    pallas_call x1, Pallas kernels, feed_forward(): pl.pallas_call(feed_kernel, in_specs=[hbm] * 5, out_specs=(hbm,) * len(ou...  282 us
    pallas_call x1, Pallas kernels, head(): pl.pallas_call(functools.partial(head_kernel, heads), in_specs=[hbm] * 4...  202 us
    dot_general x2, matrix products, dot_nt(): lax.dot_general(left, right, (((1,), (1,)), ((), ())), preferred_element_...  21.7 us
    unnamed x83, local copies, waits for them, and re-layouts  20.5 us
  transfers between devices with their start and end apart: 1, of which 0 were waited for; matrix products, arithmetic and copies ran while one was open for 3% of the time, Pallas kernels for 20%

profile of v4, /device:TPU:0, one launch (start us, length us, event | category | flops | bytes accessed | tf_op | source)
XLA Modules:
  0.0 1014.7 jit_solution(1606981863706311794)
XLA Ops:
  3.2 10.2 %all-gather.1 = f32[8,1,1536]{2,1,0:T(1,128)S(1)} all-gather(f32[1,1,1536]{2,1,0:T(1,128)S(1)} %reshape.157), channel_id=2, replica_groups=mesh['replica'=4,'shard'=8] {'shard'}, dimensions={0}, use_global_device_ids=true | all-gather | bytes 55296 | tf_op jit(solution)/shard_map/all_gather | solution.py:1331
  13.4 1.7 fusion.11
  16.6 2.0 copy.72.seg_col_ref
  20.2 1.5 copy.87
  22.8 1.6 concatenate.14.cos_ref
  24.4 1.6 concatenate.15.sin_ref
  26.6 1.9 fusion.5.normed_ref
  28.4 201.8 %shard_map.212 = (bf16[2,4,4,2,64,2048]{5,4,3,2,1,0:T(8,128)(2,1)}, bf16[8,256,3072]{2,1,0:T(8,128)(2,1)}, bf16[8,256,2048]{2,1,0:T(8,128)(2,1)}, bf16[8,4,128,3...) custom-call(bf16[4,2,64,2048]{3,2,1,0:T(8,128)(2,1)} %bitcast.109, ...), custom_call_target="tpu_custom_call" | custom-call | flops 4294967296 | bytes 268435456 | tf_op jit(solution)/shard_map/pallas_call | solution.py:448
  230.3 7.8 multiply_reduce_fusion.1
  238.1 3.2 multiply_sine_fusion
  241.3 1.7 multiply_convert_fusion.normed_ref
  243.0 281.8 %shard_map.213 = (bf16[4,512,2048]{2,1,0:T(8,128)(2,1)}, bf16[4,512,2048]{2,1,0:T(8,128)(2,1)}, bf16[4,512,2048]{2,1,0:T(8,128)(2,1)}, bf16[2048,2048]{1,0:T(8,1...) custom-call(bf16[512,2048]{1,0:T(8,128)(2,1)} %multiply_convert_fusi, ...), custom_call_target="tpu_custom_call" | custom-call | flops 154618822656 | bytes 134217728 | tf_op jit(solution)/shard_map/pallas_call | solution.py:829
  524.9 5.8 convert_reduce_fusion
  536.4 9.1 convolution_convert_fusion
  545.5 2.9 copy.73
  548.3 2.8 copy.74
  551.1 392.3 %shard_map.214 = (bf16[2,8,256,1024]{3,2,1,0:T(8,128)(2,1)}, bf16[8,512,256]{2,1,0:T(8,128)(2,1)}, bf16[8,512,384]{2,1,0:T(8,128)(2,1)}, bf16[29,256,1024]{2,1,0...) custom-call(bf16[1024,2048]{1,0:T(8,128)(2,1)} %get-tuple-element.32, ...), custom_call_target="tpu_custom_call" | custom-call | flops 10737418240 | bytes 536870912 | tf_op jit(solution)/shard_map/pallas_call | solution.py:1249
  943.4 4.9 convert_element_type.93
  949.2 1.5 slice.54
  952.0 1.6 slice.57
  953.6 1.8 copy-done.8
  956.6 7.6 add_reduce_fusion
  964.8 4.8 copy.76
  969.6 12.6 %fusion.6 = (f32[512]{0:T(512)S(1)}, f32[512,2048]{1,0:T(8,128)}) fusion(bf16[4,128,2048]{2,1,0:T(8,128)(2,1)S(1)} %copy-done.7, f32[2048]{0:T(1024)S(1)} %bitcast.124, f32[512]{0:T(512)S(1)} %copy-done.28, bf16[512,3072]{0,1:T(8,128)(2,1)} %bitcast.106, bf16[2048,3072]{1,0:T(8,128)(2,1)} %bitcast.130), kind=kOutput, calls=%fused_computation.15 | convolution fusion | flops 6447693312 | bytes 22032384 | tf_op jit(solution)/shard_map/dot_general | solution.py:33
  982.2 3.3 convert_reduce_fusion.1
  985.5 2.5 multiply_reduce_fusion.2
  988.6 2.2 copy.92
  990.8 2.3 copy.82
  993.1 2.0 copy.79
  996.3 2.0 copy.80
  998.4 7.7 convert_element_type.98
  1007.3 6.9 fusion.9
  (104 shorter events, 19.8 us)
Async XLA Ops:
  0.6 242.4 %collective-permute-start = (bf16[1024,2048]{1,0:T(8,128)(2,1)}, bf16[1024,2048]{1,0:T(8,128)(2,1)}, u32[]{:S(2)}, u32[]{:S(2)}) collective-permute-start(bf16[1024,2048]{1,0:T(8,128)(2,1)} %down_own_ref.1), channel_id=1, source_target_pairs={{0,1},{1,0},{2,3},{3,2},{4,5},{5,4},{6,7},{7,6},{8,9},{9,8},{10,11... | collective-permute-start | bytes 12582920 | tf_op jit(solution)/shard_map/ppermute | solution.py:1345
  13.4 13.2 %copy-start.22 = (f32[1,2,8,128]{3,1,2,0:T(2,128)}, f32[1,2,8,128]{3,1,2,0:T(2,128)S(1)}, u32[]{:S(2)}) copy-start(f32[1,2,8,128]{3,1,2,0:T(2,128)S(1)} %copy.88) | copy-start | bytes 24580
  15.1 3.5 copy-start.17
  15.1 3.8 copy-start.18
  15.1 4.2 copy-start.19
  16.6 3.6 copy-start.24
  21.7 219.6 %copy-start.20 = (f32[1,2,8,128]{3,1,2,0:T(2,128)}, f32[1,2,8,128]{3,1,2,0:T(2,128)S(1)}, u32[]{:S(2)}) copy-start(f32[1,2,8,128]{3,1,2,0:T(2,128)S(1)} %copy.89) | copy-start | bytes 24580
  21.7 4.3 copy-start.6
  26.6 203.7 %copy-start.27 = (f32[512]{0:T(512)}, f32[512]{0:T(512)S(1)}, u32[]{:S(2)}) copy-start(f32[512]{0:T(512)S(1)} %rsqrt_bitcast_fusion) | copy-start | bytes 6148
  238.1 3.2 copy-start.2
  238.1 286.7 %copy-start.25 = (f32[512]{0:T(512)}, f32[512]{0:T(512)S(1)}, u32[]{:S(2)}) copy-start(f32[512]{0:T(512)S(1)} %add_rsqrt_fusion) | copy-start | bytes 6148
  524.8 5.9 copy-start.3
  524.9 5.9 copy-start.21
  524.9 5.9 copy-start.26
  530.8 3.1 copy-start.12
  943.4 4.9 copy-start.5
  948.6 4.9 copy-start.15
  949.2 4.4 copy-start.14
  950.7 4.7 copy-start.8
  950.7 5.9 copy-start.9
  956.6 7.6 copy-start.29
  964.2 5.4 copy-start.7
  964.2 5.4 copy-start.23
  964.2 5.4 copy-start.28
  969.6 12.6 %slice-start = ((s8[8388608]{0:T(1024)(128)(4,1)}), s8[4194304]{0:T(1024)(128)(4,1)S(1)}, s32[]{:S(2)}) async-start(s8[8388608]{0:T(1024)(128)(4,1)} %bitcast.101), calls=%async_computation | async-start | bytes 8388608
  969.6 12.6 %slice-start.1 = ((s8[8388608]{0:T(1024)(128)(4,1)}), s8[4194304]{0:T(1024)(128)(4,1)S(1)}, s32[]{:S(2)}) async-start(s8[8388608]{0:T(1024)(128)(4,1)} %bitcast.101), calls=%async_computation.1 | async-start | bytes 8388608
  982.2 3.3 copy-start.13
  985.5 2.5 copy-start.30
  985.5 3.1 copy-start.11
  998.4 7.7 copy-start.1
  998.4 7.7 copy-start.4
  998.4 8.9 copy-start.10
  (2 other events, 3.5 us)

commit v5 on v4

v5 whole, which is shorter than its diff:
```python
import functools
import math

import jax
import jax.numpy as jnp
from jax import lax
from jax.experimental import pallas as pl
from jax.experimental.pallas import tpu as pltpu
from jax.sharding import PartitionSpec as P

HEADS = 32
KV_HEADS = 8
HEAD_DIM = 64

epsilon = 1e-05
rope_base = 500000.0
masked_score = -1e30
f32 = jnp.float32
bf16 = jnp.bfloat16


def angles(doc_positions):
    freq_index = jnp.arange(HEAD_DIM // 2, dtype=f32)
    inverse_freq = jnp.exp(freq_index * (-2.0 * math.log(rope_base) / HEAD_DIM))
    return doc_positions.astype(f32)[..., None] * inverse_freq


def outer_sum(left, right):
    return lax.dot_general(left, right, (((0,), (0,)), ((), ())), preferred_element_type=f32)


def dot_nt(left, right):
    return lax.dot_general(left, right, (((1,), (1,)), ((), ())), preferred_element_type=f32)


def dot_nn(left, right):
    return lax.dot_general(left, right, (((1,), (0,)), ((), ())), preferred_element_type=f32)


def score_bias(seg_col, seg_row, first, rows):
    last = first + rows
    key_at = lax.broadcasted_iota(jnp.int32, (last, rows), 0)
    query_at = lax.broadcasted_iota(jnp.int32, (last, rows), 1) + first
    allowed = (seg_col[:last] == seg_row[:, first:last]) & (key_at <= query_at)
    return jnp.where(allowed, 0.0, masked_score)


def attention_fore(heads, rows, qkv_ref, seg_col, seg_row, out_ref, norm_ref):
    shards, span, _ = qkv_ref.shape
    length = shards * span
    wide = heads * HEAD_DIM
    keys = qkv_ref[:, :, wide : wide + HEAD_DIM].reshape(length, HEAD_DIM)
    values = qkv_ref[:, :, wide + HEAD_DIM :].reshape(length, HEAD_DIM)
    values_t = values.astype(f32).T.astype(bf16)
    for first in range(0, length, rows):
        last = first + rows
        at = slice(first // span, last // span)
        bias = score_bias(seg_col, seg_row, first, rows)
        queries = qkv_ref[at, :, :wide].reshape(rows, wide) * HEAD_DIM ** (-0.5)
        parts = []
        for head in range(heads):
            one = queries[:, head * HEAD_DIM : (head + 1) * HEAD_DIM]
            scores = dot_nt(keys[:last], one) + bias
            top = jnp.max(scores, 0, keepdims=True)
            lifted = jnp.exp(scores - top)
            total = jnp.sum(lifted, 0, keepdims=True)
            probs = (lifted * (1.0 / total)).astype(bf16)
            parts.append(dot_nn(values_t[:, :last], probs))
            norm_ref[head : head + 1, first:last] = top + jnp.log(total)
        out = jnp.concatenate(parts, 0).T.astype(bf16)
        out_ref[at] = out.reshape(rows // span, span, wide)


def turn_back(part, cosine, sine):
    half = HEAD_DIM // 2
    lower, upper = part[:half], part[half:]
    return [lower * cosine + upper * sine, upper * cosine - lower * sine]


def attention_back(
    heads, rows, qkv_ref, grad_ref, norm, seg_col, seg_row, cos, sin, out_ref, sums, between
):
    shards, span, _ = qkv_ref.shape
    length = shards * span
    wide = heads * HEAD_DIM
    keys = qkv_ref[:, :, wide : wide + HEAD_DIM].reshape(length, HEAD_DIM)
    values = qkv_ref[:, :, wide + HEAD_DIM :].reshape(length, HEAD_DIM)
    keys_t = keys.astype(f32).T.astype(bf16)
    sums[...] = jnp.zeros_like(sums)
    key_sum, value_sum = sums.at[0], sums.at[1]
    for first in range(0, length, rows):
        last = first + rows
        at = slice(first // span, last // span)
        bias = score_bias(seg_col, seg_row, first, rows)
        queries = qkv_ref[at, :, :wide].reshape(rows, wide) * HEAD_DIM ** (-0.5)
        grads = grad_ref[at].reshape(rows, wide)
        cosine, sine = cos[:, first:last], sin[:, first:last]
        parts = []
        for head in range(heads):
            lanes = slice(head * HEAD_DIM, (head + 1) * HEAD_DIM)
            one, grad = queries[:, lanes], grads[:, lanes]
            scores = dot_nt(keys[:last], one) + bias
            probs = jnp.exp(scores - norm[head : head + 1, first:last])
            grad_probs = dot_nt(values[:last], grad)
            level = jnp.sum(probs * grad_probs, 0, keepdims=True)
            grad_scores = (probs * (grad_probs - level)).astype(bf16)
            value_sum[:last] += dot_nn(probs.astype(bf16), grad)
            key_sum[:last] += dot_nn(grad_scores, one)
            turned = dot_nn(keys_t[:, :last], grad_scores) * HEAD_DIM ** (-0.5)
            parts.extend(turn_back(turned, cosine, sine))
        out = jnp.concatenate(parts, 0).T.astype(bf16)
        out_ref[at, :, :wide] = out.reshape(rows // span, span, wide)
        if last * 4 == length * 3:
            between()
    key_parts = turn_back(key_sum[...].T, cos[...], sin[...])
    both = jnp.concatenate([jnp.concatenate(key_parts, 0).T, value_sum[...]], -1)
    out_ref[:, :, wide:] = both.astype(bf16).reshape(shards, span, 2 * HEAD_DIM)


def chip_at(chip, distance):
    result, bit = chip, 1
    while bit <= distance:
        if distance & bit:
            result = result + bit * (1 - 2 * ((chip // bit) % 2))
        bit *= 2
    return result


def head_kernel(
    heads,
    share_ref, weight_ref, output_ref, normed_ref, cos_ref, sin_ref, seg_col_ref, seg_row_ref,
    share_land, weight_out, output_land, qkv_land, attn_land, norm_ref,
    weights, normed, made, qkv, attended,
    share_send, share_recv, line_send, line_recv, swap_send, swap_recv,
    weight_send, weight_recv, near_send, near_recv, output_send, output_recv, close_send, close_recv,
    qkv_send, qkv_recv, attn_send, attn_recv, self_sem, load_sem,
):
    shards, owned, columns = weights.shape
    chips = shards // 2
    rows, width = normed_ref.shape
    _, seqs, span, part = qkv_land.shape
    wide = heads * HEAD_DIM
    replicas = lax.axis_size("replica")
    me, replica = lax.axis_index("shard"), lax.axis_index("replica")
    chip, core = me // 2, me % 2
    partner = [
        chip_at(chip, d // 2) * 2 + (core if d % 2 == 0 else 1 - core) for d in range(shards)
    ]
    relay = chips == 4
    half_owned = owned // 2

    def remote(source, target, send, recv, shard, to=None):
        return pltpu.make_async_remote_copy(
            src_ref=source, dst_ref=target, send_sem=send, recv_sem=recv,
            device_id=(replica if to is None else to, shard),
            device_id_type=pl.DeviceIdType.MESH,
        )

    barrier = pltpu.get_barrier_semaphore()

    def greet(to, shard):
        pl.semaphore_signal(
            barrier, inc=1, device_id=(to, shard), device_id_type=pl.DeviceIdType.MESH
        )

    for d in range(1, shards):
        greet(replica, partner[d])
    has_left, has_right = replica > 0, replica < replicas - 1

    @pl.when(has_left)
    def _():
        greet(replica - 1, me)

    @pl.when(has_right)
    def _():
        greet(replica + 1, me)

    @pl.when(has_left & has_right)
    def _():
        pl.semaphore_wait(barrier, shards + 1)

    @pl.when(jnp.logical_not(has_left & has_right))
    def _():
        pl.semaphore_wait(barrier, shards)

    def share_copy(d):
        return remote(
            share_ref.at[chip_at(chip, d)], share_land.at[core, replica, chip],
            share_send.at[d], share_recv.at[d], partner[2 * d],
        )

    own_share = pltpu.make_async_copy(
        share_ref.at[chip], share_land.at[core, replica, chip], self_sem.at[0]
    )
    own_share.start()
    for d in range(1, chips):
        share_copy(d).start()

    def rows_copies(ref, land, far_send, far_recv, side_send, side_recv):
        def half(index):
            return pl.ds(index * half_owned, half_owned)

        def far(d, index):
            if relay and d == 3:
                origin, way = (1, 2) if index == 0 else (2, 1)
                at = partner[2 * origin]
                return remote(
                    land.at[at, half(index)], land.at[at, half(index)],
                    far_send.at[d, index], far_recv.at[d, index], partner[2 * way],
                )
            return remote(
                ref.at[half(index)], land.at[me, half(index)],
                far_send.at[d, index], far_recv.at[d, index], partner[2 * d],
            )

        def near(d, index):
            at = partner[2 * d]
            source = ref.at[half(index)] if d == 0 else land.at[at, half(index)]
            return remote(
                source, land.at[at, half(index)],
                side_send.at[d, index], side_recv.at[d, index], partner[1],
            )

        return far, near

    def start_rows(far, near):
        for index in range(2):
            for d in range(1, chips):
                if not (relay and d == 3):
                    far(d, index).start()
        for index in range(2):
            near(0, index).start()

    def pass_rows(far, near, between=None):
        if relay:
            for index in range(2):
                for d in (1, 2):
                    far(d, index).wait_recv()
                far(3, index).start()
                for d in (1, 2):
                    near(d, index).start()
                if between is not None:
                    between(index)
            for index in range(2):
                far(3, index).wait_recv()
                near(3, index).start()
        else:
            for d in range(1, chips):
                for index in range(2):
                    far(d, index).wait_recv()
                    near(d, index).start()

    def end_rows(far, near):
        for d in range(chips):
            for index in range(2):
                near(d, index).wait_recv()

    def sent_rows(far, near):
        for d in range(chips):
            for index in range(2):
                near(d, index).wait_send()
                if d > 0:
                    far(d, index).wait_send()

    weight_rows = rows_copies(
        weight_ref, weights, weight_send, weight_recv, near_send, near_recv
    )
    output_rows = rows_copies(
        output_ref, output_land, output_send, output_recv, close_send, close_recv
    )
    own_weight = pltpu.make_async_copy(weight_ref, weights.at[me], self_sem.at[1])
    own_weight.start()
    own_output = pltpu.make_async_copy(output_ref, output_land.at[me], self_sem.at[2])
    own_output.start()
    take_normed = pltpu.make_async_copy(normed_ref, normed, load_sem.at[0])
    take_normed.start()

    def share_at(way, distance, index):
        far = replica - distance if way == 0 else replica + distance
        return share_land.at[core, far, pl.ds(index * (chips // 2), chips // 2)]

    def line_copy(way, step, index):
        at = share_at(way, step, index)
        return remote(
            at, at, line_send.at[way, step, index], line_recv.at[way, step, index], me,
            replica + 1 if way == 0 else replica - 1,
        )

    def came(way, step, index):
        at = share_at(way, step + 1, index)
        return remote(
            at, at, line_send.at[way, step, index], line_recv.at[way, step, index], me
        )

    def swap_copy(way, step, index):
        at = share_at(way, step, index)
        return remote(
            at, at, swap_send.at[way, step, index], swap_recv.at[way, step, index], partner[1]
        )

    def line_step(step, index):
        if step == 0 and index == 0:
            own_share.wait()
            for d in range(1, chips):
                share_copy(d).wait_recv()
        if step == 0:
            swap_copy(0, 0, index).start()
        for way in range(2):
            room = replica - step >= 0 if way == 0 else replica + step < replicas
            onward = has_right if way == 0 else has_left
            if step > 0:

                @pl.when(room)
                def _():
                    came(way, step - 1, index).wait_recv()
                    swap_copy(way, step, index).start()

            if step < replicas - 1:

                @pl.when(room & onward)
                def _():
                    line_copy(way, step, index).start()

    line_step(0, 0)
    line_step(0, 1)
    start_rows(*weight_rows)
    if relay and replicas > 2:
        pass_rows(*weight_rows, between=lambda index: line_step(1, index))
    else:
        pass_rows(*weight_rows)
        if replicas > 2:
            line_step(1, 0)
            line_step(1, 1)
    own_weight.wait()
    take_normed.wait()
    end_rows(*weight_rows)
    keep_weight = pltpu.make_async_copy(weights, weight_out, self_sem.at[1])
    keep_weight.start()

    lane = lax.broadcasted_iota(jnp.int32, (rows, part), 1)
    lower = lane % HEAD_DIM < HEAD_DIM // 2

    def project(owner):
        at = pl.ds(pl.multiple_of(owner * part, part), part)
        value = dot_nn(normed[...], weights[:, :, at].reshape(width, part))
        swapped = jnp.where(
            lower,
            pltpu.roll(value, part - HEAD_DIM // 2, 1),
            pltpu.roll(value, HEAD_DIM // 2, 1),
        )
        turned = value * cos_ref[...] + swapped * sin_ref[...]
        made[owner] = turned.astype(bf16)

    @pl.loop(0, shards)
    def _(k):
        project(k)

    def at_seq(s):
        return pl.ds(pl.multiple_of(s * span, span), span)

    def qkv_copy(d, s):
        return remote(
            made.at[partner[d], at_seq(s)], qkv_land.at[me, s],
            qkv_send.at[d, s], qkv_recv.at[d, s], partner[d],
        )

    def own_qkv(s):
        return pltpu.make_async_copy(made.at[me, at_seq(s)], qkv_land.at[me, s], load_sem.at[1 + s])

    for s in range(seqs):
        own_qkv(s).start()
        for d in range(shards - 1, 0, -1):
            qkv_copy(d, s).start()
    start_rows(*output_rows)
    if replicas > 3:
        line_step(2, 0)

    def attn_copy(d, s):
        return remote(
            attended.at[s, partner[d]],
            attn_land.at[at_seq(s), pl.ds(pl.multiple_of(me * wide, wide), wide)],
            attn_send.at[d, s], attn_recv.at[d, s], partner[d],
        )

    def own_attn(s):
        return pltpu.make_async_copy(
            attended.at[s, me],
            attn_land.at[at_seq(s), pl.ds(pl.multiple_of(me * wide, wide), wide)],
            load_sem.at[1 + s],
        )

    @pl.loop(0, seqs)
    def _(s):
        own_qkv(s).wait()
        for d in range(1, shards):
            qkv_copy(d, s).wait_recv()
        take = pltpu.make_async_copy(qkv_land.at[:, s], qkv, load_sem.at[0])
        take.start()
        take.wait()
        attention_fore(
            heads, 256, qkv, seg_col_ref[s], seg_row_ref[s], attended.at[s], norm_ref.at[s]
        )
        own_attn(s).start()
        for d in range(1, shards):
            attn_copy(d, s).start()
        if replicas > 3:

            @pl.when(s == 0)
            def _():
                line_step(2, 1)

    for step in range(2, replicas):
        for index in range(2):
            if (step, index) not in ((2, 0), (2, 1)) and step < replicas - 1:
                line_step(step, index)
    pass_rows(*output_rows)
    for s in range(seqs):
        own_attn(s).wait()
        for d in range(1, shards):
            attn_copy(d, s).wait_recv()
    line_step(replicas - 1, 0)
    line_step(replicas - 1, 1)

    end_rows(*output_rows)
    own_output.wait()
    keep_weight.wait()
    sent_rows(*weight_rows)
    sent_rows(*output_rows)
    for d in range(1, chips):
        share_copy(d).wait_send()
    for s in range(seqs):
        for d in range(1, shards):
            qkv_copy(d, s).wait_send()
            attn_copy(d, s).wait_send()
    for index in range(2):
        swap_copy(0, 0, index).wait_send()
        swap_copy(0, 0, index).wait_recv()
        for way in range(2):
            for step in range(replicas):
                room = replica - step >= 0 if way == 0 else replica + step < replicas
                onward = has_right if way == 0 else has_left
                if step > 0:

                    @pl.when(room)
                    def _():
                        swap_copy(way, step, index).wait_send()
                        swap_copy(way, step, index).wait_recv()

                if step < replicas - 1:

                    @pl.when(room & onward)
                    def _():
                        line_copy(way, step, index).wait_send()


def head(heads, seqs, share, weight, output, normed, cosine, sine, seg_col, seg_row):
    chips = share.shape[0]
    shards = 2 * chips
    rows, width = normed.shape
    span = rows // seqs
    owned, columns = weight.shape
    part = columns // shards
    wide = heads * HEAD_DIM
    length = shards * span
    replicas = lax.axis_size("replica")
    hbm = pl.BlockSpec(memory_space=pl.ANY)
    vmem = pl.BlockSpec(memory_space=pltpu.VMEM)
    dma = pltpu.SemaphoreType.DMA

    def low(*shape):
        return jax.ShapeDtypeStruct(shape, bf16)

    out_shape = (
        low(2, replicas, *share.shape), low(shards, owned, columns), low(shards, owned, width),
        low(shards, seqs, span, part), low(rows, shards * wide),
        jax.ShapeDtypeStruct((seqs, heads, length), f32),
    )
    return pl.pallas_call(
        functools.partial(head_kernel, heads),
        in_specs=[hbm] * 4 + [vmem] * 4,
        out_specs=(hbm,) * 5 + (vmem,),
        out_shape=out_shape,
        scratch_shapes=[
            pltpu.VMEM((shards, owned, columns), bf16),
            pltpu.VMEM((rows, width), bf16),
            pltpu.VMEM((shards, rows, part), bf16),
            pltpu.VMEM((shards, span, part), bf16),
            pltpu.VMEM((seqs, shards, span, wide), bf16),
            dma((chips,)), dma((chips,)), dma((2, replicas, 2)), dma((2, replicas, 2)),
            dma((2, replicas, 2)), dma((2, replicas, 2)),
            dma((chips, 2)), dma((chips, 2)), dma((chips, 2)), dma((chips, 2)),
            dma((chips, 2)), dma((chips, 2)), dma((chips, 2)), dma((chips, 2)),
            dma((shards, seqs)), dma((shards, seqs)), dma((shards, seqs)), dma((shards, seqs)),
            dma((3,)), dma((1 + seqs,)),
        ],
        compiler_params=pltpu.CompilerParams(
            collective_id=2, has_side_effects=True, vmem_limit_bytes=56 * 2**20
        ),
        cost_estimate=pl.CostEstimate(
            flops=4 * seqs * heads * length * length * HEAD_DIM,
            bytes_accessed=2**28,
            transcendentals=seqs * heads * length * length,
        ),
    )(share, weight, output, normed, cosine, sine, seg_col, seg_row)


def pieces_of(chips):
    if chips == 4:
        return [[(0, 0), (0, 1)], [(1, 0), (2, 0)], [(1, 1), (2, 1)], [(3, 0), (3, 1)]]
    return [[(d, 0), (d, 1)] for d in range(chips)]


def feed_kernel(
    normed_ref, cot_own_ref, share_ref, down_own_ref, down_other_ref,
    normed_out, cot_ref, partial_ref, late_ref, out_ref, mixed_ref, gate_ref, up_ref,
    weights, normed, cot, inner, sent, out_stage,
    weight_sem, normed_send, normed_recv, far_send, far_recv, cot_sem, inner_sem,
    sum_send, sum_recv, own_sem, late_sem, out_sem, keep_sem,
):
    chips, rows, width = normed.shape
    units = mixed_ref.shape[1]
    half_rows, half_units = rows // 2, units // 2
    _, replicas, _, _, share, _ = share_ref.shape
    me = lax.axis_index("shard")
    replica = lax.axis_index("replica")
    chip, core = me // 2, me % 2
    partner = [chip_at(chip, d) * 2 + core for d in range(chips)]
    steps = pieces_of(chips)
    spot = {piece: (i, at) for i, step in enumerate(steps) for at, piece in enumerate(step)}
    relay = chips == 4

    def remote(source, target, send, recv, shard):
        return pltpu.make_async_remote_copy(
            src_ref=source, dst_ref=target, send_sem=send, recv_sem=recv,
            device_id=(replica, shard), device_id_type=pl.DeviceIdType.MESH,
        )

    barrier = pltpu.get_barrier_semaphore()
    for shard in partner[1:]:
        pl.semaphore_signal(
            barrier, inc=1, device_id=(replica, shard), device_id_type=pl.DeviceIdType.MESH
        )
    pl.semaphore_wait(barrier, chips - 1)

    def half(index):
        return pl.ds(index * half_rows, half_rows)

    def block_copy(which, d, part):
        own, land = ((normed_ref, normed), (cot_own_ref, cot_ref))[which]
        send, recv = ((normed_send, normed_recv), (far_send, far_recv))[which]
        index, at = spot[d, part]
        if relay and d == 3:
            origin, way = (1, 2) if part == 0 else (2, 1)
            from_index, from_at = spot[origin, part]
            source, to = land.at[from_index, half(from_at)], partner[way]
        else:
            source, to = own.at[half(part)], partner[d]
        return remote(source, land.at[index, half(at)], send.at[d, part], recv.at[d, part], to)

    for part in range(2):
        for which in range(2):
            for d in range(1, 3 if relay else chips):
                block_copy(which, d, part).start()
    own_copy = pltpu.make_async_copy(normed_ref, normed.at[0], own_sem.at[0])
    own_copy.start()
    own_cot = pltpu.make_async_copy(cot_own_ref, cot_ref.at[0], own_sem.at[1])
    own_cot.start()

    def cot_copy(index):
        source = cot_own_ref if index == 0 else cot_ref.at[index]
        return pltpu.make_async_copy(source, cot.at[index % 2], cot_sem.at[index % 2])

    cot_copy(0).start()
    owned = share * replicas
    for which in range(2):
        for k in range(chips):
            for z in range(replicas):
                for c in range(2):
                    pltpu.make_async_copy(
                        share_ref.at[c, z, k, which],
                        weights.at[which, pl.ds((2 * k + c) * owned + z * share, share), pl.ds(0, units)],
                        weight_sem.at[which],
                    ).start()
    down_own = pltpu.make_async_copy(
        down_own_ref, weights.at[2, pl.ds(core * half_units, half_units)], weight_sem.at[2]
    )
    down_other = pltpu.make_async_copy(
        down_other_ref, weights.at[2, pl.ds((1 - core) * half_units, half_units)], weight_sem.at[3]
    )
    down_own.start()
    down_other.start()
    own_copy.wait()
    for which in range(2):
        whole = weights.at[which, pl.ds(0, width), pl.ds(0, units)]
        pltpu.make_async_copy(whole, whole, weight_sem.at[which]).wait()
    down_own.wait()
    down_other.wait()

    def inner_copies(index):
        return [
            pltpu.make_async_copy(
                inner.at[which], ref.at[pl.ds(index * rows, rows)], inner_sem.at[which]
            )
            for which, ref in enumerate((mixed_ref, gate_ref, up_ref))
        ]

    def out_copies(index):
        return [
            pltpu.make_async_copy(
                out_stage.at[half(at)], out_ref.at[chip_at(chip, d), half(part)], out_sem.at[at]
            )
            for at, (d, part) in enumerate(steps[index])
        ]

    def sum_copy(index, at):
        d, part = steps[index][at]
        return remote(
            sent.at[index % 2, half(at)], partial_ref.at[d, half(part)],
            sum_send.at[d, part], sum_recv.at[d, part], partner[d],
        )

    own_sum = pltpu.make_async_copy(sent.at[0], partial_ref.at[0], own_sem.at[2])
    late_sum = pltpu.make_async_copy(sent.at[(chips - 1) % 2], late_ref, late_sem)
    keep_normed = pltpu.make_async_copy(normed, normed_out, keep_sem)
    tile = min(512, units)
    for index in range(chips):
        for d, part in steps[index]:
            if d > 0:
                block_copy(0, d, part).wait_recv()
                block_copy(1, d, part).wait_recv()
        if relay and index in (1, 2):
            for which in range(2):
                block_copy(which, 3, index - 1).start()
        if index > 0:
            cot_copy(index).start()
        if index == chips - 1:
            keep_normed.start()
        if index > 0:
            for copy in inner_copies(index - 1):
                copy.wait()
        cot_copy(index).wait()

        @pl.loop(0, units // tile)
        def _(j):
            columns = pl.ds(pl.multiple_of(j * tile, tile), tile)
            block = normed[index]
            gate = dot_nn(block, weights[0, :width, columns])
            up = dot_nn(block, weights[1, :width, columns])
            grad = dot_nt(cot[index % 2], weights[2, columns, :])
            sigmoid = jax.nn.sigmoid(gate)
            swish = gate * sigmoid
            inner[0, :, columns] = (swish * up).astype(bf16)
            inner[1, :, columns] = (grad * up * (sigmoid + swish * (1.0 - sigmoid))).astype(bf16)
            inner[2, :, columns] = (grad * swish).astype(bf16)

        for copy in inner_copies(index):
            copy.start()
        if index > 0:
            for copy in out_copies(index - 1):
                copy.wait()
        if index == 2:
            own_sum.wait()
        if index >= 3:
            for at in range(2):
                sum_copy(index - 2, at).wait_send()

        @pl.loop(0, width // 512)
        def _(j):
            columns = pl.ds(pl.multiple_of(j * 512, 512), 512)
            sent[index % 2, :, columns] = (
                dot_nt(inner[1], weights[0, columns, :units])
                + dot_nt(inner[2], weights[1, columns, :units])
            ).astype(bf16)

        if index == 0:
            own_sum.start()
        elif index == chips - 1:
            late_sum.start()
        else:
            for at in range(2):
                sum_copy(index, at).start()

        @pl.loop(0, width // 512)
        def _(j):
            columns = pl.ds(pl.multiple_of(j * 512, 512), 512)
            out_stage[:, columns] = dot_nn(inner[0], weights[2, :units, columns]).astype(bf16)

        for copy in out_copies(index):
            copy.start()

    for copy in inner_copies(chips - 1):
        copy.wait()
    for copy in out_copies(chips - 1):
        copy.wait()
    late_sum.wait()
    keep_normed.wait()
    own_cot.wait()
    for at in range(2):
        sum_copy(chips - 2, at).wait_send()
    for index in range(1, chips - 1):
        for at in range(2):
            sum_copy(index, at).wait_recv()
    for d in range(1, chips):
        for part in range(2):
            for which in range(2):
                block_copy(which, d, part).wait_send()


def feed_forward(normed, cot, share, down_own, down_other):
    chips = share.shape[2]
    rows, width = normed.shape
    units = down_own.shape[0] * 2
    tokens = chips * rows
    hbm = pl.BlockSpec(memory_space=pl.ANY)
    dma = pltpu.SemaphoreType.DMA

    def low(*shape):
        return jax.ShapeDtypeStruct(shape, bf16)

    out_shape = (
        low(chips, rows, width), low(chips, rows, width), low(chips - 1, rows, width),
        low(rows, width), low(chips, rows, width),
        low(tokens, units), low(tokens, units), low(tokens, units),
    )
    return pl.pallas_call(
        feed_kernel,
        in_specs=[hbm] * 5,
        out_specs=(hbm,) * len(out_shape),
        out_shape=out_shape,
        scratch_shapes=[
            pltpu.VMEM((3, width, width), bf16),
            pltpu.VMEM((chips, rows, width), bf16),
            pltpu.VMEM((2, rows, width), bf16),
            pltpu.VMEM((3, rows, units), bf16),
            pltpu.VMEM((2, rows, width), bf16),
            pltpu.VMEM((rows, width), bf16),
            dma((4,)), dma((chips, 2)), dma((chips, 2)), dma((chips, 2)), dma((chips, 2)),
            dma((2,)), dma((3,)), dma((chips, 2)), dma((chips, 2)), dma((3,)), dma(()), dma((2,)),
            dma(()),
        ],
        compiler_params=pltpu.CompilerParams(
            collective_id=0, has_side_effects=True, vmem_limit_bytes=60 * 2**20
        ),
        cost_estimate=pl.CostEstimate(
            flops=12 * tokens * units * width, bytes_accessed=2**27, transcendentals=tokens * units
        ),
    )(normed, cot, share, down_own, down_other)


def tail_kernel(
    heads,
    normed_all, cot_all, mixed_ref, gate_ref, up_ref, partial_ref, late_ref, outs_ref,
    hidden_ref, cot_ref, output_ref, weight_ref, qkv_ref, normed_ref, attn_ref,
    scale_ref, gain_ref, norm_ref, seg_col_ref, seg_row_ref, cos_ref, sin_ref,
    down_sum, inner_sum, down_got, inner_got, late_land, hidden_out,
    inner_land, grad_land, turn_land, end_land, mid_land, sum_out, sum_qkv, pass_land, out_land, total,
    one_out, down_result, gate_result, up_result, rest_result,
    branch, grad_made, core_out, core_qkv, relay_out, relay_qkv, mine, theirs, half, whole,
    pair_send, pair_recv, late_send, late_recv,
    inner_send, inner_recv, grad_send, grad_recv, turn_send, turn_recv, core_send, core_recv,
    sum_send, sum_recv, part_send, part_recv, end_send, end_recv, mid_send, mid_recv, out_send,
    out_recv, relay_send, relay_recv, pass_send, pass_recv,
    big_sem, tile_sem, got_sem, self_sem, load_sem, seq_sem, tick_sem, whole_sem, total_sem,
    one_sem,
):
    shards, seqs, span, part = qkv_ref.shape
    rows, width = normed_ref.shape
    _, owned, units = inner_land.shape[1:]
    chips = shards // 2
    tokens = chips * rows
    wide = heads * HEAD_DIM
    chunks = end_land.shape[0]
    qkv_width = shards * part
    full = qkv_width + width
    across = total.shape[0]
    line = lax.axis_size("replica") == 4
    relay = chips == 4
    me, replica = lax.axis_index("shard"), lax.axis_index("replica")
    chip, core = me // 2, me % 2
    partner = [
        chip_at(chip, d // 2) * 2 + (core if d % 2 == 0 else 1 - core) for d in range(shards)
    ]
    is_inner = (replica == 1) | (replica == 2)
    inward = jnp.where(replica < 2, 1, 2)
    outward = jnp.where(replica < 2, 0, 3)

    def partner_at(d):
        if isinstance(d, int):
            return partner[d]
        result, bit = 0, 1
        while bit < shards:
            result = result + bit * (((me // bit) % 2 + (d // bit) % 2) % 2)
            bit *= 2
        return result

    def remote(source, target, send, recv, shard, to=None):
        return pltpu.make_async_remote_copy(
            src_ref=source, dst_ref=target, send_sem=send, recv_sem=recv,
            device_id=(replica if to is None else to, shard),
            device_id_type=pl.DeviceIdType.MESH,
        )

    barrier = pltpu.get_barrier_semaphore()

    def greet(to, shard):
        pl.semaphore_signal(
            barrier, inc=1, device_id=(to, shard), device_id_type=pl.DeviceIdType.MESH
        )

    for d in range(1, shards):
        greet(replica, partner[d])
    if line:

        @pl.when(is_inner)
        def _():
            greet(outward, me)
            greet(3 - replica, me)
            pl.semaphore_wait(barrier, shards + 1)

        @pl.when(jnp.logical_not(is_inner))
        def _():
            greet(inward, me)
            pl.semaphore_wait(barrier, shards)

    else:
        pl.semaphore_wait(barrier, shards - 1)

    half_rows = rows // 2

    def late_copy(index):
        at = pl.ds(index * half_rows, half_rows)
        return remote(
            late_ref.at[at], late_land.at[at], late_send.at[index], late_recv.at[index],
            partner[2 * (chips - 1)],
        )

    late_copy(0).start()
    late_copy(1).start()

    down_across = width // units
    down_chunks = down_sum.shape[0] // owned * down_across
    last_inner = down_chunks + 2 * shards
    up_first = down_chunks + shards
    out_chunks = width // units

    def block(ref, row, column):
        return ref.at[
            pl.ds(pl.multiple_of(row * owned, owned), owned),
            pl.ds(pl.multiple_of(column * units, units), units),
        ]

    def inner_of(c):
        return (c - down_chunks) // shards, (c - down_chunks) % shards

    def source_of(c):
        if isinstance(c, int):
            if c < down_chunks:
                return block(down_sum, c // down_across, c % down_across)
            if c >= last_inner:
                return total.at[c - last_inner]
        which, d = inner_of(c)
        return inner_land.at[which, partner_at(d)]

    def place_of(c):
        if isinstance(c, int):
            if c < down_chunks:
                return block(down_result, c // down_across, c % down_across)
            if c >= last_inner + out_chunks:
                return block(rest_result, 0, c - last_inner - out_chunks)
            if c >= last_inner:
                return block(rest_result, 0, qkv_width // units + c - last_inner)
            which, d = inner_of(c)
            return block((gate_result, up_result)[which], 0, partner[d])
        return block(gate_result, 0, partner_at(inner_of(c)[1]))

    def end_copy(c):
        return remote(source_of(c), end_land.at[c], end_send.at[c], end_recv.at[c], me, inward)

    def mid_copy(c):
        return remote(
            half.at[c % 4], mid_land.at[c], mid_send.at[c], mid_recv.at[c], me, 3 - replica
        )

    def out_copy(c):
        return remote(whole.at[c % 2], place_of(c), out_send.at[c], out_recv.at[c], me, outward)

    def keep_copy(c):
        return pltpu.make_async_copy(whole.at[c % 2], place_of(c), whole_sem.at[c % 2])

    def from_end(c):
        if line:

            @pl.when(jnp.logical_not(is_inner))
            def _():
                end_copy(c).start()

    def take_mine(c):
        return pltpu.make_async_copy(source_of(c), mine, tick_sem.at[0])

    def take_other(c):
        return pltpu.make_async_copy(mid_land.at[c], theirs.at[1], tick_sem.at[2])

    def send_out(c):
        mid_copy(c).wait_recv()
        take_other(c).start()
        if not isinstance(c, int) or c >= 2:
            out_copy(c - 2).wait_send()
            keep_copy(c - 2).wait()
        take_other(c).wait()
        whole[c % 2] = (half[c % 4].astype(f32) + theirs[1].astype(f32)).astype(bf16)
        if isinstance(c, int):
            out_copy(c).start()
            keep_copy(c).start()
            return

        @pl.when(c >= down_chunks)
        def _():
            out_copy(c).start()
            keep_copy(c).start()

        for old in (down_chunks - 2, down_chunks - 1):

            @pl.when(c == old)
            def _():
                out_copy(old).start()
                keep_copy(old).start()

    def middle(c):
        if not line:
            return
        static = isinstance(c, int)

        @pl.when(is_inner)
        def _():
            if static and (c == 0 or c == up_first or c >= last_inner):
                take_mine(c).start()
            end_copy(c).wait_recv()
            two = pltpu.make_async_copy(end_land.at[c], theirs.at[0], tick_sem.at[1])
            two.start()
            if not static or c >= 4:
                mid_copy(c - 4).wait_send()
            take_mine(c).wait()
            two.wait()
            half[c % 4] = (mine[...].astype(f32) + theirs[0].astype(f32)).astype(bf16)
            mid_copy(c).start()
            if not static:

                @pl.when(c + 1 < up_first)
                def _():
                    take_mine(c + 1).start()

            elif c + 1 < last_inner and c + 1 != up_first:
                take_mine(c + 1).start()
            if not static or c >= 2:
                send_out(c - 2)

    lead = 3
    position = [0]

    settled = [down_chunks]

    def ticks(count):
        for _ in range(count):
            c = position[0]
            if c >= last_inner:
                return
            position[0] += 1
            ahead = c + lead
            if c >= up_first:
                ahead = min(ahead, up_first + 2 * (c - up_first) + 1)
            while settled[0] <= min(ahead, last_inner - 1):
                settle(settled[0])
                from_end(settled[0])
                settled[0] += 1
            middle(c)

    def later_tick(c):
        @pl.when(c + lead < up_first)
        def _():
            settle(c + lead)
            from_end(c + lead)

        middle(c)

    def inner_copy(which, d):
        at = partner_at(d)
        return remote(
            inner_sum.at[which, pl.ds(pl.multiple_of(at * owned, owned), owned)],
            inner_land.at[which, me],
            inner_send.at[which, d], inner_recv.at[which, d], at,
        )

    def own_inner(which):
        return pltpu.make_async_copy(
            inner_sum.at[which, pl.ds(pl.multiple_of(me * owned, owned), owned)],
            inner_land.at[which, me], self_sem.at[which],
        )

    def start_inner(which):
        own_inner(which).start()
        for d in range(1, shards):
            inner_copy(which, d).start()

    def settle(c):
        which, d = inner_of(c)
        if isinstance(c, int):
            if d == 0:
                own_inner(which).wait()
            else:
                inner_copy(which, d).wait_recv()
            return

        @pl.when(d == 0)
        def _():
            own_inner(which).wait()

        @pl.when(d > 0)
        def _():
            inner_copy(which, d).wait_recv()

    half_units = units
    tiles = width // rows
    per_slot = width // half_units

    def weight_gradients(big, sent_stage, kept_stage):
        got = branch
        def load(ref, slot, columns):
            return pltpu.make_async_copy(
                ref, big.at[slot, pl.ds(0, tokens), pl.ds(0, columns)], big_sem.at[slot]
            )

        def load_blocks(ref, slot):
            return [
                pltpu.make_async_copy(
                    ref.at[k], big.at[slot, pl.ds(k * rows, rows)], big_sem.at[3 + slot * chips + k]
                )
                for k in range(chips)
            ]

        first_loads = load_blocks(cot_all, 1) + [load(mixed_ref, 0, 2 * half_units)]
        normed_loads = load_blocks(normed_all, 2)
        for copy in first_loads + normed_loads:
            copy.start()
        for copy in first_loads:
            copy.wait()

        sums = (down_sum, inner_sum.at[0], inner_sum.at[1])
        gots = (down_got, inner_got.at[0], inner_got.at[1])

        def tile_copies(which, owner, stage):
            result = []
            for t in range(half_units // rows if which == 0 else tiles):
                if which == 0:
                    source = stage.at[t]
                else:
                    source = stage.at[
                        t // per_slot, :, pl.ds((t % per_slot) * half_units, half_units)
                    ]
                place = pl.ds(t * rows, rows)
                if owner == 0:
                    copy = remote(
                        source, gots[which].at[place], pair_send.at[which, t],
                        pair_recv.at[which, t], partner[1],
                    )
                else:
                    copy = pltpu.make_async_copy(
                        source, sums[which].at[place], tile_sem.at[which, t]
                    )
                result.append(copy)
            return result

        pair, made = {}, [0]
        for which in range(3):
            if which == 1:
                later = load(gate_ref, 0, 2 * half_units)
                later.start()
                following = load(up_ref, 1, 2 * half_units)
                following.start()
                for copy in normed_loads:
                    copy.wait()
                later.wait()
            if which == 2:
                following.wait()
            for owner in range(2):
                stage = (sent_stage, kept_stage)[owner]
                first = ((1 - core) if owner == 0 else core) * half_units
                copies = tile_copies(which, owner, stage)
                pair[which, owner] = copies
                if which > 0 and owner == 0:
                    for copy in pair[which - 1, 0]:
                        copy.wait_send()
                for t, copy in enumerate(copies):
                    columns = width if which == 0 else half_units
                    if owner == 1:
                        pair[which, 0][t].wait_recv()
                        take = pltpu.make_async_copy(
                            gots[which].at[pl.ds(t * rows, rows)], got.at[:, pl.ds(0, columns)],
                            got_sem,
                        )
                        take.start()
                    if which == 0:
                        at = pl.ds(pl.multiple_of(first + t * rows, rows), rows)
                        left, right, slot, begin = big[0, :tokens, at], 1, t, 0
                    else:
                        left = big[2, :tokens, t * rows : (t + 1) * rows]
                        right = which - 1
                        slot, begin = t // per_slot, (t % per_slot) * half_units
                    step = min(1024, columns)
                    for j in range(columns // step):
                        if which == 0:
                            at = pl.ds(j * step, step)
                        else:
                            at = pl.ds(pl.multiple_of(first, half_units), half_units)
                        product = outer_sum(left, big[right, :tokens, at])
                        if owner == 1:
                            if j == 0:
                                take.wait()
                            product = product + got[:, j * step : (j + 1) * step].astype(f32)
                        stage[slot, :, begin + j * step : begin + (j + 1) * step] = product.astype(
                            bf16
                        )
                    copy.start()
                    if which == 0 and owner == 1:
                        copy.wait()
                        per_tile = rows // owned * down_across
                        for c in range(t * per_tile, (t + 1) * per_tile):
                            from_end(c)
                    if which > 0:
                        made[0] += 1
                        if made[0] % 3 == 0 and position[0] < down_chunks - lead:
                            ticks(1)
                if owner == 1 and which > 0:
                    for copy in copies:
                        copy.wait()
                    if which == 1:
                        start_inner(0)
        for copy in pair[2, 0]:
            copy.wait_send()

    pl.run_scoped(
        weight_gradients,
        pltpu.VMEM((3, tokens, width), bf16),
        pltpu.VMEM((2, rows, width), bf16),
        pltpu.VMEM((2, rows, width), bf16),
    )

    def grad_copy(d, s):
        at = pl.ds(pl.multiple_of(s * span, span), span)
        return remote(
            grad_made.at[partner[d], at], grad_land.at[me, at],
            grad_send.at[d, s], grad_recv.at[d, s], partner[d],
        )

    own_grad = pltpu.make_async_copy(grad_made.at[me], grad_land.at[me], self_sem.at[2])

    def norm_backward(partials, hidden, cot, output):
        loads = [
            pltpu.make_async_copy(partial_ref, partials.at[pl.ds(0, chips - 1)], load_sem.at[0]),
            pltpu.make_async_copy(hidden_ref, hidden, load_sem.at[1]),
            pltpu.make_async_copy(cot_ref, cot, load_sem.at[2]),
            pltpu.make_async_copy(output_ref, output, load_sem.at[3]),
        ]
        for copy in loads:
            copy.start()
        late_copy(0).wait_recv()
        late_copy(1).wait_recv()
        last = pltpu.make_async_copy(late_land, partials.at[chips - 1], load_sem.at[4])
        last.start()
        ticks(1)
        for copy in loads[:3] + [last]:
            copy.wait()

        @pl.loop(0, rows // 32)
        def _(i):
            at = pl.ds(pl.multiple_of(i * 32, 32), 32)
            grad = partials[0, at].astype(f32)
            for d in range(1, chips):
                grad = grad + partials[d, at].astype(f32)
            scale = scale_ref[at]
            unit = hidden[at] * scale
            scaled = grad * gain_ref[...]
            level = jnp.mean(scaled * unit, -1, keepdims=True)
            result = cot[at].astype(f32) + scale * (scaled - unit * level)
            hidden[at] = result
            branch[at] = result.astype(bf16)

        keep = pltpu.make_async_copy(hidden, hidden_out, load_sem.at[1])
        keep.start()
        ticks(1)
        loads[3].wait()

        @pl.loop(0, shards)
        def _(k):
            grad_made[k] = dot_nt(branch[...], output[k]).astype(bf16)

        own_grad.start()
        for s in range(seqs):
            for d in range(1, shards):
                grad_copy(d, s).start()
        keep.wait()

    pl.run_scoped(
        norm_backward,
        pltpu.VMEM((chips, rows, width), bf16),
        pltpu.VMEM((rows, width), f32),
        pltpu.VMEM((rows, width), bf16),
        pltpu.VMEM((shards, owned, width), bf16),
    )

    def turn_copy(turned, d, s):
        at = pl.ds(pl.multiple_of(s * span, span), span)
        return remote(
            turned.at[s, partner[d]], turn_land.at[me, at],
            turn_send.at[d, s], turn_recv.at[d, s], partner[d],
        )

    def attention(qkv, grads, turned, sums, turned_all, normed, attn, sent, weight, one):
        loads = [
            pltpu.make_async_copy(normed_ref, normed, load_sem.at[0]),
            pltpu.make_async_copy(attn_ref, attn, load_sem.at[1]),
        ]
        for copy in loads:
            copy.start()
        own_grad.wait()
        half_owned = owned // 2

        def part_of(index):
            return pl.ds(index * half_owned, half_owned)

        def scatter_steps(which, product, core_land, relay_land, sum_land):
            wide_of = core_land.shape[2]

            def core_copy(d):
                return remote(
                    sent.at[d, :, pl.ds(0, wide_of)], core_land.at[d],
                    core_send.at[which, d], core_recv.at[which, d], partner[1],
                )

            def sum_copy(d, index):
                return remote(
                    core_land.at[d, part_of(index)], sum_land.at[d, part_of(index)],
                    sum_send.at[which, d, index], sum_recv.at[which, d, index], partner[2 * d],
                )

            def relay_copy(index):
                return remote(
                    core_land.at[3, part_of(index)], relay_land.at[index],
                    relay_send.at[which, index], relay_recv.at[which, index],
                    partner[2 * (index + 1)],
                )

            order = list(range(chips - 1, -1, -1))

            def near():
                for d in order:
                    for place, value in product(chip_at(chip, d) * 2 + 1 - core):
                        sent[d, :, place] = value.astype(bf16)
                    core_copy(d).start()

            def far():
                for d in order:
                    core_copy(d).wait_recv()
                    for place, value in product(chip_at(chip, d) * 2 + core):
                        core_land[d, :, place] = (
                            core_land[d, :, place].astype(f32) + value
                        ).astype(bf16)
                    if relay and d == 3:
                        relay_copy(0).start()
                        relay_copy(1).start()
                    elif d > 0:
                        for index in range(2):
                            if not relay or index != 2 - d:
                                sum_copy(d, index).start()
                for d in range(chips):
                    core_copy(d).wait_send()

            def onward():
                for index in range(2 if relay else 0):
                    relay_copy(index).wait_recv()
                    at = part_of(index)
                    core_land[2 - index, at] = (
                        core_land[2 - index, at].astype(f32) + relay_land[index].astype(f32)
                    ).astype(bf16)
                    sum_copy(2 - index, index).start()

            def arrive(first):
                direct = range(1, 3 if relay else chips)
                for d in direct:
                    for index in range(2):
                        sum_copy(d, index).wait_recv()
                gets = [
                    pltpu.make_async_copy(
                        sum_land.at[d], sent.at[d, :, pl.ds(0, wide_of)], load_sem.at[2 + d]
                    )
                    for d in direct
                ]
                for copy in gets:
                    copy.start()
                for copy in gets:
                    copy.wait()
                count = wide_of // units
                for k in range(count):
                    columns = slice(k * units, (k + 1) * units)
                    value = core_land[0, :, columns].astype(f32)
                    for d in direct:
                        value = value + sent[d, :, columns].astype(f32)
                    sent[0, :, columns] = value.astype(bf16)
                puts = [
                    pltpu.make_async_copy(
                        sent.at[0, :, pl.ds(k * units, units)], total.at[first + k],
                        total_sem.at[first + k],
                    )
                    for k in range(count)
                ]
                for put in puts:
                    put.start()
                for k, put in enumerate(puts):
                    put.wait()
                    from_end(last_inner + first + k)

            def leave():
                for index in range(2 if relay else 0):
                    relay_copy(index).wait_send()
                for d in range(1, 3 if relay else chips):
                    for index in range(2):
                        sum_copy(d, index).wait_send()

            return near, far, onward, arrive, leave

        def rows_for(owner):
            return pl.ds(pl.multiple_of(owner * owned, owned), owned)

        def out_product(owner):
            left = attn[:, rows_for(owner)]
            for k in range(out_chunks):
                at = slice(k * units, (k + 1) * units)
                yield at, outer_sum(left, branch[:, at])

        def qkv_product(owner):
            left = normed[:, rows_for(owner)]
            for k in range(shards):
                value = outer_sum(left, turned_all[k])
                key_at = shards * wide + k * HEAD_DIM
                value_at = key_at + shards * HEAD_DIM
                yield slice(k * wide, (k + 1) * wide), value[:, :wide]
                yield slice(key_at, key_at + HEAD_DIM), value[:, wide : wide + HEAD_DIM]
                yield slice(value_at, value_at + HEAD_DIM), value[:, wide + HEAD_DIM :]

        out_scatter = scatter_steps(0, out_product, core_out, relay_out, sum_out)
        qkv_scatter = scatter_steps(1, qkv_product, core_qkv, relay_qkv, sum_qkv)
        loads[1].wait()
        out_scatter[0]()
        ticks(1)
        out_scatter[1]()
        ticks(down_chunks - position[0])

        def own_turn(s):
            at = pl.ds(pl.multiple_of(s * span, span), span)
            return pltpu.make_async_copy(turned.at[s, me], turn_land.at[me, at], seq_sem.at[2 + s])

        @pl.loop(0, seqs)
        def _(s):
            for d in range(1, shards):
                grad_copy(d, s).wait_recv()
            at = pl.ds(pl.multiple_of(s * span, span), span)
            takes = [
                pltpu.make_async_copy(qkv_ref.at[:, s], qkv, seq_sem.at[0]),
                pltpu.make_async_copy(grad_land.at[:, at], grads, seq_sem.at[1]),
            ]
            for copy in takes:
                copy.start()
            for copy in takes:
                copy.wait()
            attention_back(
                heads, 256, qkv, grads, norm_ref.at[s], seg_col_ref[s], seg_row_ref[s],
                cos_ref.at[s], sin_ref.at[s], turned.at[s], sums,
                between=lambda: later_tick(down_chunks + 2 * s) if line else None,
            )
            own_turn(s).start()
            for d in range(1, shards):
                turn_copy(turned, d, s).start()
            if line:
                later_tick(down_chunks + 1 + 2 * s)

        if line:
            position[0] = down_chunks + 2 * seqs
            settled[0] = up_first
        start_inner(1)
        ticks(1)
        for s in range(seqs):
            own_turn(s).wait()
            for d in range(1, shards):
                turn_copy(turned, d, s).wait_recv()
        take = pltpu.make_async_copy(turn_land, turned_all, load_sem.at[2])
        take.start()
        weight_load(weight, 0).start()
        ticks(1)
        loads[0].wait()
        take.wait()

        qkv_scatter[0]()
        ticks(1)
        qkv_scatter[1]()
        ticks(1)
        out_scatter[2]()
        qkv_scatter[2]()

        def rows_of(index):
            return pl.ds(index * half_rows, half_rows)

        def part_copy(d, index):
            return remote(
                outs_ref.at[chip_at(chip, d), rows_of(index)], out_land.at[d, rows_of(index)],
                part_send.at[d, index], part_recv.at[d, index], partner[2 * d],
            )

        def pass_copy(index):
            return remote(
                outs_ref.at[chip_at(chip, 3), rows_of(index)], pass_land.at[index],
                pass_send.at[index], pass_recv.at[index], partner[2 * (index + 1)],
            )

        if relay:
            pass_copy(0).start()
            pass_copy(1).start()
            part_copy(1, 0).start()
            part_copy(2, 1).start()
        else:
            for d in range(1, chips):
                for index in range(2):
                    part_copy(d, index).start()

        def one_copy(k):
            at = pl.ds(k * owned, owned)
            return pltpu.make_async_copy(one.at[k % 2], one_out.at[:, at], one_sem.at[2 + k % 2])

        for k in range(shards):
            weight_load(weight, k).wait()
            if k + 1 < shards:
                weight_load(weight, k + 1).start()
            if k >= 2:
                one_copy(k - 2).wait()
            value = dot_nt(turned_all[0], weight[k % 2, :, :part])
            for j in range(1, shards):
                value = value + dot_nt(
                    turned_all[j], weight[k % 2, :, j * part : (j + 1) * part]
                )
            one[k % 2] = value
            one_copy(k).start()
            if k % 2 == 1:
                ticks(1)
            if k == 3:
                out_scatter[3](0)
        one_copy(shards - 2).wait()
        one_copy(shards - 1).wait()

        if relay:
            for index in range(2):
                pass_copy(index).wait_recv()
                at = rows_of(index)
                gets = [
                    pltpu.make_async_copy(
                        outs_ref.at[chip_at(chip, 2 - index), at], normed.at[rows_of(0)],
                        load_sem.at[0],
                    ),
                    pltpu.make_async_copy(
                        pass_land.at[index], normed.at[rows_of(1)], load_sem.at[1]
                    ),
                ]
                for copy in gets:
                    copy.start()
                for copy in gets:
                    copy.wait()
                attn[at] = (
                    normed[rows_of(0)].astype(f32) + normed[rows_of(1)].astype(f32)
                ).astype(bf16)
                remote(
                    attn.at[at], out_land.at[2 - index, at],
                    part_send.at[2 - index, index], part_recv.at[2 - index, index],
                    partner[2 * (2 - index)],
                ).start()
                ticks(1)
        ticks(last_inner - 4 - position[0])
        qkv_scatter[3](out_chunks)
        ticks(last_inner)
        for k in range(across):
            middle(last_inner + k)
        if line:

            @pl.when(is_inner)
            def _():
                send_out(chunks - 2)
                send_out(chunks - 1)

        for s in range(seqs):
            for d in range(1, shards):
                turn_copy(turned, d, s).wait_send()
        out_scatter[4]()
        qkv_scatter[4]()
        if relay:
            for index in range(2):
                pass_copy(index).wait_send()
        for d in range(1, 3 if relay else chips):
            for index in range(2):
                part_copy(d, index).wait_send()
                part_copy(d, index).wait_recv()

    def weight_load(weight, k):
        return pltpu.make_async_copy(weight_ref.at[k], weight.at[k % 2], one_sem.at[k % 2])

    pl.run_scoped(
        attention,
        pltpu.VMEM((shards, span, part), bf16),
        pltpu.VMEM((shards, span, wide), bf16),
        pltpu.VMEM((seqs, shards, span, part), bf16),
        pltpu.VMEM((2, shards * span, HEAD_DIM), f32),
        pltpu.VMEM((shards, rows, part), bf16),
        pltpu.VMEM((rows, width), bf16),
        pltpu.VMEM((rows, width), bf16),
        pltpu.VMEM((chips, owned, qkv_width), bf16),
        pltpu.VMEM((2, owned, qkv_width), bf16),
        pltpu.VMEM((2, rows, owned), f32),
    )

    late_copy(0).wait_send()
    late_copy(1).wait_send()
    for s in range(seqs):
        for d in range(1, shards):
            grad_copy(d, s).wait_send()
    for which in range(2):
        for d in range(1, shards):
            inner_copy(which, d).wait_send()
    if line:

        @pl.when(is_inner)
        def _():
            for c in range(chunks - 4, chunks):
                mid_copy(c).wait_send()
            for c in (chunks - 2, chunks - 1):
                out_copy(c).wait_send()
                keep_copy(c).wait()

        @pl.when(jnp.logical_not(is_inner))
        def _():
            for c in range(chunks):
                end_copy(c).wait_send()
                out_copy(c).wait_recv()


def tail(
    heads, normed_all, cot_all, mixed, gate, up, partials, late, outs,
    hidden, cot, output, weight, qkv, normed, attn, *tables,
):
    shards, seqs, span, part = qkv.shape
    rows, width = normed.shape
    chips = shards // 2
    units = mixed.shape[1] // 2
    owned = width // shards
    wide = heads * HEAD_DIM
    full = shards * part + width
    across = full // units
    chunks = (units // owned) * (width // units) + 2 * shards + across
    tiles = width // rows
    hbm = pl.BlockSpec(memory_space=pl.ANY)
    vmem = pl.BlockSpec(memory_space=pltpu.VMEM)
    dma = pltpu.SemaphoreType.DMA

    def low(*shape):
        return jax.ShapeDtypeStruct(shape, bf16)

    def high(*shape):
        return jax.ShapeDtypeStruct(shape, f32)

    pieces = low(chunks, owned, units)
    out_shape = (
        low(units, width), low(2, width, units), low(units, width), low(2, width, units),
        low(rows, width), high(rows, width),
        low(2, shards, owned, units), low(shards, rows, wide), low(shards, rows, part),
        pieces, pieces, low(chips, owned, width), low(chips, owned, shards * part),
        low(2, rows // 2, width), low(*outs.shape),
        low(across, owned, units), high(rows, width),
        low(units, width), low(owned, shards * units), low(owned, shards * units), low(owned, full),
    )
    length = shards * span
    return pl.pallas_call(
        functools.partial(tail_kernel, heads),
        in_specs=[hbm] * 15 + [vmem] * 7,
        out_specs=(hbm,) * len(out_shape),
        out_shape=out_shape,
        scratch_shapes=[
            pltpu.VMEM((rows, width), bf16),
            pltpu.VMEM((shards, rows, wide), bf16),
            pltpu.VMEM((chips, owned, width), bf16),
            pltpu.VMEM((chips, owned, shards * part), bf16),
            pltpu.VMEM((2, owned // 2, width), bf16),
            pltpu.VMEM((2, owned // 2, shards * part), bf16),
            pltpu.VMEM((owned, units), bf16),
            pltpu.VMEM((2, owned, units), bf16),
            pltpu.VMEM((4, owned, units), bf16),
            pltpu.VMEM((2, owned, units), bf16),
            dma((3, tiles)), dma((3, tiles)), dma((2,)), dma((2,)),
            dma((2, shards)), dma((2, shards)), dma((shards, seqs)), dma((shards, seqs)),
            dma((shards, seqs)), dma((shards, seqs)), dma((2, chips)), dma((2, chips)),
            dma((2, chips, 2)), dma((2, chips, 2)), dma((chips, 2)), dma((chips, 2)),
            dma((chunks,)), dma((chunks,)), dma((chunks,)), dma((chunks,)), dma((chunks,)),
            dma((chunks,)), dma((2, 2)), dma((2, 2)), dma((2,)), dma((2,)),
            dma((3 + 3 * chips,)), dma((3, tiles)), dma(()), dma((3,)), dma((5 + chips,)),
            dma((2 + seqs,)), dma((3,)), dma((2,)), dma((across,)), dma((4,)),
        ],
        compiler_params=pltpu.CompilerParams(
            collective_id=1, has_side_effects=True, vmem_limit_bytes=63 * 2**20
        ),
        cost_estimate=pl.CostEstimate(
            flops=10 * seqs * heads * length * length * HEAD_DIM + 6 * chips * rows * width * width,
            bytes_accessed=2**29,
            transcendentals=seqs * heads * length * length,
        ),
    )(
        normed_all, cot_all, mixed, gate, up, partials, late, outs,
        hidden, cot, output, weight, qkv, normed, attn, *tables,
    )


def norm_back(grad_normed, unit_rows, scale_rows, gain_rows):
    scaled_grad = grad_normed * gain_rows
    return scale_rows * (
        scaled_grad - unit_rows * jnp.mean(scaled_grad * unit_rows, -1, keepdims=True)
    )


def body(
    tokens,
    segments,
    positions,
    cotangent,
    attention_gain,
    query_weight,
    key_weight,
    value_weight,
    output_weight,
    mlp_gain,
    gate_weight,
    up_weight,
    down_weight,
):
    seqs, span, width = tokens.shape
    shards = lax.axis_size("shard")
    me = lax.axis_index("shard")
    rows = seqs * span
    length = shards * span
    owned = query_weight.shape[0]
    heads = HEADS // shards
    copies = max(1, shards // KV_HEADS)
    wide = heads * HEAD_DIM
    part = wide + 2 * HEAD_DIM
    hidden_share = down_weight.shape[0]

    chips = shards // 2
    replicas = lax.axis_size("replica")
    swap = [(i, i + 1 - 2 * (i % 2)) for i in range(shards)]

    small = jnp.concatenate(
        [
            attention_gain.astype(f32), mlp_gain.astype(f32),
            segments.astype(f32).reshape(rows), positions.astype(f32).reshape(rows),
        ]
    )
    small = lax.all_gather(small, "shard")
    gain_one, gain_two = small[:, :owned].reshape(width), small[:, owned : 2 * owned].reshape(width)
    places = jnp.swapaxes(small[:, 2 * owned :].reshape(shards, 2, seqs, span), 0, 1)
    places = jnp.swapaxes(places, 1, 2).reshape(2, seqs, length)
    seg_row, seg_col = places[0][:, None, :], places[0][:, :, None]
    angle_all = jnp.swapaxes(angles(places[1]), 1, 2)
    cos_all, sin_all = jnp.cos(angle_all), jnp.sin(angle_all)

    share = owned // replicas
    units = 2 * hidden_share
    share_own = lax.dynamic_slice_in_dim(
        jnp.stack([gate_weight, up_weight]), lax.axis_index("replica") * share, share, 1
    )
    share_own = jnp.transpose(share_own.reshape(2, share, chips, units), (2, 0, 1, 3))
    down_other = lax.ppermute(down_weight, "shard", swap)

    def per_head(weight):
        return jnp.repeat(weight.reshape(owned, KV_HEADS, HEAD_DIM), copies, axis=1)

    qkv_owned = jnp.concatenate(
        [query_weight.reshape(owned, shards, wide), per_head(key_weight), per_head(value_weight)],
        -1,
    ).reshape(owned, shards * part)

    x = tokens.reshape(rows, width).astype(f32)
    scale_one = lax.rsqrt(jnp.mean(x * x, -1, keepdims=True) + epsilon)
    unit_one = x * scale_one
    normed_one = (unit_one * gain_one).astype(bf16)
    angle = angles(positions).reshape(rows, HEAD_DIM // 2)
    cosine, sine = jnp.cos(angle), jnp.sin(angle)
    still = jnp.ones((rows, HEAD_DIM), f32)
    cos_lanes = jnp.concatenate([cosine] * (2 * heads + 2) + [still], 1)
    sin_lanes = jnp.concatenate([-sine, sine] * (heads + 1) + [still * 0.0], 1)
    shares, qkv_full, output_full, qkv, attn, norms = head(
        heads, seqs, share_own, qkv_owned, output_weight, normed_one, cos_lanes, sin_lanes,
        seg_col, seg_row,
    )
    hidden = x + dot_nn(attn, output_full.reshape(width, width))
    scale_two = lax.rsqrt(jnp.mean(hidden * hidden, -1, keepdims=True) + epsilon)
    normed_two = (hidden * scale_two * gain_two).astype(bf16)

    cot_rows = cotangent.reshape(rows, width)
    normed_all, cot_all, partials, late, outs, mixed, gate, up = feed_forward(
        normed_two, cot_rows, shares, down_weight, down_other
    )
    results = tail(
        heads, normed_all, cot_all, mixed, gate, up, partials, late, outs, hidden, cot_rows,
        output_full, qkv_full, qkv, normed_one, attn, scale_two, gain_two[None], norms, seg_col,
        seg_row, cos_all, sin_all,
    )
    down_part, grad_hidden, inner_blocks = results[0], results[5], results[6]
    out_land, total, grad_one, summed = results[14], results[15], results[16], results[17:]
    out_sum = lax.dynamic_index_in_dim(outs, me // 2, 0, keepdims=False).astype(f32)
    arrived = 3 if chips == 4 else chips
    out_sum = out_sum + jnp.sum(out_land[1:arrived].astype(f32), 0)
    block_out = (hidden + out_sum).astype(bf16)

    if replicas != 4:

        def side_by_side(some):
            return jnp.swapaxes(some, 0, 1).reshape(owned, some.shape[0] * hidden_share)

        out_blocks = width // hidden_share
        rest_blocks = jnp.concatenate([total[out_blocks:], total[:out_blocks]])
        summed = lax.psum(
            (
                down_part, side_by_side(inner_blocks[0]), side_by_side(inner_blocks[1]),
                side_by_side(rest_blocks),
            ),
            "replica",
        )
    down_grad, gate_grad, up_grad, rest = [some.astype(f32) for some in summed]
    key_at, value_at = shards * wide, shards * (wide + HEAD_DIM)
    output_grad = rest[:, shards * part :]

    def kv_grad(columns):
        return jnp.sum(columns.reshape(owned, KV_HEADS, copies, HEAD_DIM), 2).reshape(
            owned, KV_HEADS * HEAD_DIM
        )

    query_grad = rest[:, :key_at]
    key_grad = kv_grad(rest[:, key_at:value_at])
    value_grad = kv_grad(rest[:, value_at : shards * part])

    own_one, own_two = attention_gain.astype(f32), mlp_gain.astype(f32)
    gain_one_grad = (
        jnp.sum(query_weight.astype(f32) * query_grad, 1)
        + jnp.sum(key_weight.astype(f32) * key_grad + value_weight.astype(f32) * value_grad, 1)
    ) / own_one
    gain_two_grad = (
        jnp.sum(gate_weight.astype(f32) * gate_grad + up_weight.astype(f32) * up_grad, 1) / own_two
    )
    token_grad = grad_hidden + norm_back(grad_one, unit_one, scale_one, gain_one)
    return (
        block_out.reshape(seqs, span, width),
        token_grad.reshape(seqs, span, width),
        gain_one_grad,
        query_grad,
        key_grad,
        value_grad,
        output_grad,
        gain_two_grad,
        gate_grad,
        up_grad,
        down_grad,
    )


def solution(mesh):
    rows = P("shard", None)
    blocks = P("replica", "shard", None)
    in_specs = (
        blocks, P("replica", "shard"), P("replica", "shard"), blocks, P("shard"),
        rows, rows, rows, rows, P("shard"), rows, rows, rows,
    )
    out_specs = (
        blocks, blocks, P("shard"), rows, rows, rows, rows, P("shard"), rows, rows, rows,
    )
    return jax.shard_map(body, mesh=mesh, in_specs=in_specs, out_specs=out_specs, check_vma=False)
```

time: 1020 us -> 927 us (0.909)
  Pallas kernels: 876 us -> 831 us
  local copies, waits for them, and re-layouts: 43 us -> 19 us
  matrix products: 29.4 us -> 10.6 us
    pallas_call x1, Pallas kernels: 282 us -> 196 us  [feed_forward(): pl.pallas_call(feed_kernel, in_specs=[hbm] * 5, out_specs=(hbm,) * len(ou...]
    pallas_call x1, Pallas kernels: 392 us -> 438 us  [tail(): pl.pallas_call(functools.partial(tail_kernel, heads), in_specs=[hbm] * 15...]
    dot_general x2 -> x0, matrix products: 21.7 us -> none  [dot_nt(): lax.dot_general(left, right, (((1,), (1,)), ((), ())), preferred_element_...]
    unnamed x83 -> x52, local copies, waits for them, and re-layouts: 20.5 us -> 10.7 us
  transfers between devices with their start and end apart: 1 -> 1, of which waited for: 0 -> 0; matrix products, arithmetic and copies ran while one was open for 3% -> 4% of each run, Pallas kernels for 20% -> 21%
where the time goes in v5:
time: 927 us; the launch traced here: 919 us
  Pallas kernels  831 us (90%)
  other arithmetic  45.8 us (5%)
  local copies, waits for them, and re-layouts  19 us (2%)
  matrix products  10.6 us (1%)
  blocking collectives  10.2 us (1%)
    pallas_call x1, Pallas kernels, tail(): pl.pallas_call(functools.partial(tail_kernel, heads), in_specs=[hbm] * 15...  438 us
    pallas_call x1, Pallas kernels, head(): pl.pallas_call(functools.partial(head_kernel, heads), in_specs=[hbm] * 4...  197 us
    pallas_call x1, Pallas kernels, feed_forward(): pl.pallas_call(feed_kernel, in_specs=[hbm] * 5, out_specs=(hbm,) * len(ou...  196 us
  transfers between devices with their start and end apart: 1, of which 0 were waited for; matrix products, arithmetic and copies ran while one was open for 4% of the time, Pallas kernels for 21%

profile of v5, /device:TPU:0, one launch (start us, length us, event | category | flops | bytes accessed | tf_op | source)
XLA Modules:
  0.0 918.7 jit_solution(3592677897560616962)
XLA Ops:
  1.2 0.7 convert_element_type.72
  2.5 0.7 convert_bitcast_fusion
  3.2 10.2 %all-gather.1 = f32[8,1,1536]{2,1,0:T(1,128)S(1)} all-gather(f32[1,1,1536]{2,1,0:T(1,128)S(1)} %reshape.140), channel_id=2, replica_groups=mesh['replica'=4,'shard'=8] {'shard'}, dimensions={0}, use_global_device_ids=true | all-gather | bytes 55296 | tf_op jit(solution)/shard_map/all_gather | solution.py:1668
  14.1 1.1 copy.49
  15.5 1.1 copy.50
  16.9 1.5 copy.60
  18.4 1.7 fusion.11
  20.5 1.4 copy.61
  21.9 1.5 copy.69
  23.4 2.0 copy.54.seg_col_ref
  25.4 1.0 multiply_sine_fusion.1
  26.4 1.6 concatenate.14.cos_ref
  28.1 1.6 concatenate.15.sin_ref
  30.2 1.9 fusion.5.normed_ref
  32.1 196.9 %shard_map.212 = (bf16[2,4,4,2,64,2048]{5,4,3,2,1,0:T(8,128)(2,1)}, bf16[8,256,3072]{2,1,0:T(8,128)(2,1)}, bf16[8,256,2048]{2,1,0:T(8,128)(2,1)}, bf16[8,4,128,3...) custom-call(bf16[4,2,64,2048]{3,2,1,0:T(8,128)(2,1)} %bitcast.82, ...), custom_call_target="tpu_custom_call" | custom-call | flops 4294967296 | bytes 268435456 | tf_op jit(solution)/shard_map/pallas_call | solution.py:478
  229.0 10.6 %multiply_reduce_fusion = (f32[512]{0:T(512)S(1)}, f32[512,2048]{1,0:T(8,128)}) fusion(bf16[512,2048]{1,0:T(8,128)(2,1)} %get-tuple-element.32.attn_ref, bf16[2048,2048]{1,0:T(8,128)(2,1)} %bitcast.101, bf16[4,128,2048]{2,1,0:T(8,128)(2,1)S(1)} %copy-done), kind=kOutput, calls=%fused_computation.20 | convolution fusion | flops 4299161088 | bytes 16779264 | tf_op jit(solution)/shard_map/dot_general | solution.py:37
  239.6 0.9 copy.55.scale_ref
  240.5 2.8 multiply_sine_fusion
  243.2 3.9 multiply_convert_fusion.normed_ref
  247.2 196.1 %shard_map.213 = (bf16[4,512,2048]{2,1,0:T(8,128)(2,1)}, bf16[4,512,2048]{2,1,0:T(8,128)(2,1)}, bf16[3,512,2048]{2,1,0:T(8,128)(2,1)}, bf16[512,2048]{1,0:T(8,12...) custom-call(bf16[512,2048]{1,0:T(8,128)(2,1)} %multiply_convert_fusi, ...), custom_call_target="tpu_custom_call" | custom-call | flops 103079215104 | bytes 134217728 | tf_op jit(solution)/shard_map/pallas_call | solution.py:725
  443.3 438.3 %shard_map.214 = (bf16[1024,2048]{1,0:T(8,128)(2,1)}, bf16[2,2048,1024]{2,1,0:T(8,128)(2,1)}, bf16[1024,2048]{1,0:T(8,128)(2,1)}, bf16[2,2048,1024]{2,1,0:T(8,12...) custom-call(bf16[4,512,2048]{2,1,0:T(8,128)(2,1)} %get-tuple-element, ...), custom_call_target="tpu_custom_call" | custom-call | flops 62277025792 | bytes 536870912 | tf_op jit(solution)/shard_map/pallas_call | solution.py:1585
  881.6 2.3 add_reduce_fusion.1
  883.9 3.9 multiply_reduce_fusion.1
  887.8 1.3 copy-done.10
  889.1 1.0 convert_reduce_fusion
  890.7 1.2 copy-done.5
  891.9 0.9 fusion.6
  893.4 5.3 convert_element_type.90
  898.7 1.2 copy-done.3
  899.9 9.6 %add_reduce_fusion = (f32[256]{0:T(256)S(1)}, f32[256,8192]{1,0:T(8,128)}, f32[256,8192]{1,0:T(8,128)}) fusion(bf16[256,8192]{1,0:T(8,128)(2,1)S(1)} %copy-done.3, bf16[256,8192]{1,0:T(8,128)(2,1)S(1)} %copy-done.2, bf16[256,8192]{1,0:T(8,128)(2,1)} %get-tuple-element.50, bf16[256,8192]{1,0:T(8,128)(2,1)} %get-tuple-element.51), kind=kLoop, calls=%fused_computation.2 | loop fusion | flops 16776960 | bytes 33555456 | tf_op jit(solution)/shard_map/reduce_sum | solution.py:1758
  910.0 4.4 fusion.1
  914.4 3.3 fusion.9
  (62 shorter events, 5.7 us)
Async XLA Ops:
  0.6 246.5 %collective-permute-start = (bf16[1024,2048]{1,0:T(8,128)(2,1)}, bf16[1024,2048]{1,0:T(8,128)(2,1)}, u32[]{:S(2)}, u32[]{:S(2)}) collective-permute-start(bf16[1024,2048]{1,0:T(8,128)(2,1)} %down_own_ref.1), channel_id=1, source_target_pairs={{0,1},{1,0},{2,3},{3,2},{4,5},{5,4},{6,7},{7,6},{8,9},{9,8},{10,11... | collective-permute-start | bytes 12582920 | tf_op jit(solution)/shard_map/ppermute | solution.py:1682
  14.0 9.3 %copy-start.15 = (f32[1,4,8,128]{3,2,1,0:T(8,128)}, f32[1,4,8,128]{3,2,1,0:T(8,128)S(1)}, u32[]{:S(2)}) copy-start(f32[1,4,8,128]{3,2,1,0:T(8,128)S(1)} %get-tuple-element.66) | copy-start | bytes 49156
  14.1 16.1 %copy-start.13 = (f32[1,2,8,128]{3,1,2,0:T(2,128)}, f32[1,2,8,128]{3,1,2,0:T(2,128)S(1)}, u32[]{:S(2)}) copy-start(f32[1,2,8,128]{3,1,2,0:T(2,128)S(1)} %copy.62) | copy-start | bytes 24580
  25.4 4.3 copy-start
  30.2 198.8 %copy-start.16 = (f32[512]{0:T(512)}, f32[512]{0:T(512)S(1)}, u32[]{:S(2)}) copy-start(f32[512]{0:T(512)S(1)} %rsqrt_bitcast_fusion) | copy-start | bytes 6148
  443.3 438.3 %copy-start.11 = (bf16[256,512]{1,0:T(8,128)(2,1)S(1)}, bf16[256,512]{1,0:T(8,128)(2,1)}, u32[]{:S(2)}) copy-start(bf16[256,512]{1,0:T(8,128)(2,1)} %param.20) | copy-start | bytes 786436
  443.3 438.3 %copy-start.12 = (bf16[256,512]{1,0:T(8,128)(2,1)S(1)}, bf16[256,512]{1,0:T(8,128)(2,1)}, u32[]{:S(2)}) copy-start(bf16[256,512]{1,0:T(8,128)(2,1)} %param.19) | copy-start | bytes 786436
  881.6 2.3 copy-start.7
  883.9 5.2 copy-start.10
  889.1 1.6 copy-start.1
  889.1 2.8 copy-start.5
  889.1 2.8 copy-start.14
  889.1 2.8 copy-start.17
  890.1 3.3 copy-start.8
  893.4 5.3 copy-start.2
  893.4 6.5 copy-start.3
  899.9 9.6 %copy-start.18 = (bf16[256]{0:T(256)(128)(2,1)S(1)}, bf16[256]{0:T(256)(128)(2,1)}, u32[]{:S(2)}) copy-start(bf16[256]{0:T(256)(128)(2,1)} %param.22) | copy-start | bytes 1540
  899.9 10.2 %copy-start.4 = (f32[512,2048]{1,0:T(8,128)S(1)}, f32[512,2048]{1,0:T(8,128)}, u32[]{:S(2)}) copy-start(f32[512,2048]{1,0:T(8,128)} %get-tuple-element.73.hidden_ref) | copy-start | bytes 12582916
  910.0 4.4 copy-start.6
  910.0 4.4 copy-start.9
  914.4 3.3 copy-start.19

commit v6 on v5

--- a/solution.py
+++ b/solution.py
@@ -128,16 +128,18 @@
 
 def head_kernel(
     heads,
-    share_ref, weight_ref, output_ref, normed_ref, cos_ref, sin_ref, seg_col_ref, seg_row_ref,
-    share_land, weight_out, output_land, qkv_land, attn_land, norm_ref,
-    weights, normed, made, qkv, attended,
+    share_ref, weight_ref, output_ref, token_ref, gain_ref, place_ref, cos_ref, sin_ref,
+    share_land, weight_out, output_land, qkv_land, attn_land, normed_out, hidden_out, second_out,
+    norm_ref, scale_ref, gain_out, place_out, seg_col_ref, seg_row_ref,
+    weights, tokens, normed, made, qkv, attended, hidden, gains, places,
+    small_send, small_recv,
     share_send, share_recv, line_send, line_recv, swap_send, swap_recv,
     weight_send, weight_recv, near_send, near_recv, output_send, output_recv, close_send, close_recv,
     qkv_send, qkv_recv, attn_send, attn_recv, self_sem, load_sem,
 ):
     shards, owned, columns = weights.shape
     chips = shards // 2
-    rows, width = normed_ref.shape
+    rows, width = token_ref.shape
     _, seqs, span, part = qkv_land.shape
     wide = heads * HEAD_DIM
     replicas = lax.axis_size("replica")
@@ -182,6 +184,20 @@
     @pl.when(jnp.logical_not(has_left & has_right))
     def _():
         pl.semaphore_wait(barrier, shards)
+
+    def small_copy(which, d):
+        source, land = ((gain_ref, gains), (place_ref, places))[which]
+        return remote(
+            source, land.at[me], small_send.at[which, d], small_recv.at[which, d], partner[d]
+        )
+
+    for which in range(2):
+        for d in range(1, shards):
+            small_copy(which, d).start()
+    take_tokens = pltpu.make_async_copy(token_ref, tokens, load_sem.at[0])
+    take_tokens.start()
+    gains[me] = gain_ref[...]
+    places[me] = place_ref[...]
 
     def share_copy(d):
         return remote(
@@ -223,12 +239,12 @@
 
         return far, near
 
-    def start_rows(far, near):
-        for index in range(2):
+    def start_rows(far, near, halves=range(2)):
+        for index in halves:
             for d in range(1, chips):
                 if not (relay and d == 3):
                     far(d, index).start()
-        for index in range(2):
+        for index in halves:
             near(0, index).start()
 
     def pass_rows(far, near, between=None):
@@ -272,8 +288,6 @@
     own_weight.start()
     own_output = pltpu.make_async_copy(output_ref, output_land.at[me], self_sem.at[2])
     own_output.start()
-    take_normed = pltpu.make_async_copy(normed_ref, normed, load_sem.at[0])
-    take_normed.start()
 
     def share_at(way, distance, index):
         far = replica - distance if way == 0 else replica + distance
@@ -324,6 +338,32 @@
     line_step(0, 0)
     line_step(0, 1)
     start_rows(*weight_rows)
+
+    for which in range(2):
+        for d in range(1, shards):
+            small_copy(which, d).wait_recv()
+    gain_out[...] = gains[...]
+    place_out[...] = places[...]
+    for s in range(seqs):
+        seg_row_ref[s] = jnp.concatenate([places[k, 0, s : s + 1] for k in range(shards)], 1)
+        turned = jnp.concatenate([places[k, 0, s : s + 1] for k in range(shards)], 0).T
+        seg_col_ref[s] = jnp.concatenate([turned[:, k : k + 1] for k in range(shards)], 0)
+
+    def gain_row(which):
+        return jnp.concatenate([gains[k, which : which + 1] for k in range(shards)], 1)
+
+    take_tokens.wait()
+    gain_one = gain_row(0)
+
+    @pl.loop(0, rows // 32)
+    def _(i):
+        at = pl.ds(pl.multiple_of(i * 32, 32), 32)
+        x = tokens[at].astype(f32)
+        unit = x * lax.rsqrt(jnp.mean(x * x, -1, keepdims=True) + epsilon)
+        normed[at] = (unit * gain_one).astype(bf16)
+
+    keep_normed = pltpu.make_async_copy(normed, normed_out, load_sem.at[0])
+    keep_normed.start()
     if relay and replicas > 2:
         pass_rows(*weight_rows, between=lambda index: line_step(1, index))
     else:
@@ -332,7 +372,8 @@
             line_step(1, 0)
             line_step(1, 1)
     own_weight.wait()
-    take_normed.wait()
+    keep_normed.wait()
+    start_rows(*output_rows, halves=range(1))
     end_rows(*weight_rows)
     keep_weight = pltpu.make_async_copy(weights, weight_out, self_sem.at[1])
     keep_weight.start()
@@ -371,7 +412,6 @@
         own_qkv(s).start()
         for d in range(shards - 1, 0, -1):
             qkv_copy(d, s).start()
-    start_rows(*output_rows)
     if replicas > 3:
         line_step(2, 0)
 
@@ -403,10 +443,11 @@
         own_attn(s).start()
         for d in range(1, shards):
             attn_copy(d, s).start()
-        if replicas > 3:
-
-            @pl.when(s == 0)
-            def _():
+
+        @pl.when(s == 0)
+        def _():
+            start_rows(*output_rows, halves=range(1, 2))
+            if replicas > 3:
                 line_step(2, 1)
 
     for step in range(2, replicas):
@@ -418,13 +459,48 @@
         own_attn(s).wait()
         for d in range(1, shards):
             attn_copy(d, s).wait_recv()
-    line_step(replicas - 1, 0)
-    line_step(replicas - 1, 1)
-
     end_rows(*output_rows)
     own_output.wait()
     keep_weight.wait()
     sent_rows(*weight_rows)
+    take_output = pltpu.make_async_copy(
+        output_land, weights.at[:, :, pl.ds(0, width)], self_sem.at[1]
+    )
+    take_attn = pltpu.make_async_copy(attn_land, normed, load_sem.at[0])
+    take_output.start()
+    take_attn.start()
+    line_step(replicas - 1, 0)
+    take_output.wait()
+    take_attn.wait()
+
+    @pl.loop(0, width // 512)
+    def _(j):
+        at = pl.ds(pl.multiple_of(j * 512, 512), 512)
+        hidden[:, at] = tokens[:, at].astype(f32) + dot_nn(
+            normed[...], weights[:, :, at].reshape(width, 512)
+        )
+
+    keep_hidden = pltpu.make_async_copy(hidden, hidden_out, self_sem.at[1])
+    keep_hidden.start()
+    gain_two = gain_row(1)
+
+    @pl.loop(0, rows // 32)
+    def _(i):
+        at = pl.ds(pl.multiple_of(i * 32, 32), 32)
+        x = hidden[at]
+        scale = lax.rsqrt(jnp.mean(x * x, -1, keepdims=True) + epsilon)
+        scale_ref[at] = scale
+        normed[at] = (x * scale * gain_two).astype(bf16)
+
+    keep_second = pltpu.make_async_copy(normed, second_out, load_sem.at[0])
+    keep_second.start()
+    line_step(replicas - 1, 1)
+    keep_hidden.wait()
+    keep_second.wait()
+
+    for which in range(2):
+        for d in range(1, shards):
+            small_copy(which, d).wait_send()
     sent_rows(*output_rows)
     for d in range(1, chips):
         share_copy(d).wait_send()
@@ -453,11 +529,11 @@
                         line_copy(way, step, index).wait_send()
 
 
-def head(heads, seqs, share, weight, output, normed, cosine, sine, seg_col, seg_row):
+def head(heads, share, weight, output, tokens, gains, places, cosine, sine):
     chips = share.shape[0]
     shards = 2 * chips
-    rows, width = normed.shape
-    span = rows // seqs
+    rows, width = tokens.shape
+    _, seqs, span = places.shape
     owned, columns = weight.shape
     part = columns // shards
     wide = heads * HEAD_DIM
@@ -470,22 +546,32 @@
     def low(*shape):
         return jax.ShapeDtypeStruct(shape, bf16)
 
+    def high(*shape):
+        return jax.ShapeDtypeStruct(shape, f32)
+
     out_shape = (
         low(2, replicas, *share.shape), low(shards, owned, columns), low(shards, owned, width),
         low(shards, seqs, span, part), low(rows, shards * wide),
-        jax.ShapeDtypeStruct((seqs, heads, length), f32),
+        low(rows, width), high(rows, width), low(rows, width),
+        high(seqs, heads, length), high(rows, 1), high(shards, *gains.shape),
+        high(shards, *places.shape), high(seqs, length, 1), high(seqs, 1, length),
     )
     return pl.pallas_call(
         functools.partial(head_kernel, heads),
         in_specs=[hbm] * 4 + [vmem] * 4,
-        out_specs=(hbm,) * 5 + (vmem,),
+        out_specs=(hbm,) * 8 + (vmem,) * 6,
         out_shape=out_shape,
         scratch_shapes=[
             pltpu.VMEM((shards, owned, columns), bf16),
             pltpu.VMEM((rows, width), bf16),
+            pltpu.VMEM((rows, width), bf16),
             pltpu.VMEM((shards, rows, part), bf16),
             pltpu.VMEM((shards, span, part), bf16),
             pltpu.VMEM((seqs, shards, span, wide), bf16),
+            pltpu.VMEM((rows, width), f32),
+            pltpu.VMEM((shards, *gains.shape), f32),
+            pltpu.VMEM((shards, *places.shape), f32),
+            dma((2, shards)), dma((2, shards)),
             dma((chips,)), dma((chips,)), dma((2, replicas, 2)), dma((2, replicas, 2)),
             dma((2, replicas, 2)), dma((2, replicas, 2)),
             dma((chips, 2)), dma((chips, 2)), dma((chips, 2)), dma((chips, 2)),
@@ -501,7 +587,7 @@
             bytes_accessed=2**28,
             transcendentals=seqs * heads * length * length,
         ),
-    )(share, weight, output, normed, cosine, sine, seg_col, seg_row)
+    )(share, weight, output, tokens, gains, places, cosine, sine)
 
 
 def pieces_of(chips):
@@ -513,7 +599,7 @@
 def feed_kernel(
     normed_ref, cot_own_ref, share_ref, down_own_ref, down_other_ref,
     normed_out, cot_ref, partial_ref, late_ref, out_ref, mixed_ref, gate_ref, up_ref,
-    weights, normed, cot, inner, sent, out_stage,
+    weights, normed, cot, inner, sent, out_stage, kept,
     weight_sem, normed_send, normed_recv, far_send, far_recv, cot_sem, inner_sem,
     sum_send, sum_recv, own_sem, late_sem, out_sem, keep_sem,
 ):
@@ -624,38 +710,71 @@
     keep_normed = pltpu.make_async_copy(normed, normed_out, keep_sem)
     tile = min(512, units)
     for index in range(chips):
+        split = index == chips - 1
         for d, part in steps[index]:
             if d > 0:
                 block_copy(0, d, part).wait_recv()
-                block_copy(1, d, part).wait_recv()
+                if not split:
+                    block_copy(1, d, part).wait_recv()
         if relay and index in (1, 2):
             for which in range(2):
                 block_copy(which, 3, index - 1).start()
-        if index > 0:
+        if index > 0 and not split:
             cot_copy(index).start()
         if index == chips - 1:
             keep_normed.start()
         if index > 0:
             for copy in inner_copies(index - 1):
                 copy.wait()
-        cot_copy(index).wait()
+        if not split:
+            cot_copy(index).wait()
+
+        def project_out():
+            @pl.loop(0, width // 512)
+            def _(j):
+                columns = pl.ds(pl.multiple_of(j * 512, 512), 512)
+                out_stage[:, columns] = dot_nn(inner[0], weights[2, :units, columns]).astype(bf16)
+
+            for copy in out_copies(index):
+                copy.start()
+
+        if split:
+            @pl.loop(0, units // tile)
+            def _(j):
+                columns = pl.ds(pl.multiple_of(j * tile, tile), tile)
+                gate = dot_nn(normed[index], weights[0, :width, columns])
+                up = dot_nn(normed[index], weights[1, :width, columns])
+                kept[0, :, columns] = gate
+                kept[1, :, columns] = up
+                inner[0, :, columns] = (gate * jax.nn.sigmoid(gate) * up).astype(bf16)
+
+            for copy in out_copies(index - 1):
+                copy.wait()
+            project_out()
+            for d, part in steps[index]:
+                block_copy(1, d, part).wait_recv()
+            cot_copy(index).start()
+            cot_copy(index).wait()
 
         @pl.loop(0, units // tile)
         def _(j):
             columns = pl.ds(pl.multiple_of(j * tile, tile), tile)
-            block = normed[index]
-            gate = dot_nn(block, weights[0, :width, columns])
-            up = dot_nn(block, weights[1, :width, columns])
+            if split:
+                gate, up = kept[0, :, columns], kept[1, :, columns]
+            else:
+                gate = dot_nn(normed[index], weights[0, :width, columns])
+                up = dot_nn(normed[index], weights[1, :width, columns])
             grad = dot_nt(cot[index % 2], weights[2, columns, :])
             sigmoid = jax.nn.sigmoid(gate)
             swish = gate * sigmoid
-            inner[0, :, columns] = (swish * up).astype(bf16)
+            if not split:
+                inner[0, :, columns] = (swish * up).astype(bf16)
             inner[1, :, columns] = (grad * up * (sigmoid + swish * (1.0 - sigmoid))).astype(bf16)
             inner[2, :, columns] = (grad * swish).astype(bf16)
 
         for copy in inner_copies(index):
             copy.start()
-        if index > 0:
+        if index > 0 and not split:
             for copy in out_copies(index - 1):
                 copy.wait()
         if index == 2:
@@ -680,13 +799,8 @@
             for at in range(2):
                 sum_copy(index, at).start()
 
-        @pl.loop(0, width // 512)
-        def _(j):
-            columns = pl.ds(pl.multiple_of(j * 512, 512), 512)
-            out_stage[:, columns] = dot_nn(inner[0], weights[2, :units, columns]).astype(bf16)
-
-        for copy in out_copies(index):
-            copy.start()
+        if not split:
+            project_out()
 
     for copy in inner_copies(chips - 1):
         copy.wait()
@@ -734,12 +848,13 @@
             pltpu.VMEM((3, rows, units), bf16),
             pltpu.VMEM((2, rows, width), bf16),
             pltpu.VMEM((rows, width), bf16),
+            pltpu.VMEM((2, rows, units), f32),
             dma((4,)), dma((chips, 2)), dma((chips, 2)), dma((chips, 2)), dma((chips, 2)),
             dma((2,)), dma((3,)), dma((chips, 2)), dma((chips, 2)), dma((3,)), dma(()), dma((2,)),
             dma(()),
         ],
         compiler_params=pltpu.CompilerParams(
-            collective_id=0, has_side_effects=True, vmem_limit_bytes=60 * 2**20
+            collective_id=0, has_side_effects=True, vmem_limit_bytes=63 * 2**20
         ),
         cost_estimate=pl.CostEstimate(
             flops=12 * tokens * units * width, bytes_accessed=2**27, transcendentals=tokens * units
@@ -1659,20 +1774,6 @@
     replicas = lax.axis_size("replica")
     swap = [(i, i + 1 - 2 * (i % 2)) for i in range(shards)]
 
-    small = jnp.concatenate(
-        [
-            attention_gain.astype(f32), mlp_gain.astype(f32),
-            segments.astype(f32).reshape(rows), positions.astype(f32).reshape(rows),
-        ]
-    )
-    small = lax.all_gather(small, "shard")
-    gain_one, gain_two = small[:, :owned].reshape(width), small[:, owned : 2 * owned].reshape(width)
-    places = jnp.swapaxes(small[:, 2 * owned :].reshape(shards, 2, seqs, span), 0, 1)
-    places = jnp.swapaxes(places, 1, 2).reshape(2, seqs, length)
-    seg_row, seg_col = places[0][:, None, :], places[0][:, :, None]
-    angle_all = jnp.swapaxes(angles(places[1]), 1, 2)
-    cos_all, sin_all = jnp.cos(angle_all), jnp.sin(angle_all)
-
     share = owned // replicas
     units = 2 * hidden_share
     share_own = lax.dynamic_slice_in_dim(
@@ -1689,22 +1790,28 @@
         -1,
     ).reshape(owned, shards * part)
 
-    x = tokens.reshape(rows, width).astype(f32)
-    scale_one = lax.rsqrt(jnp.mean(x * x, -1, keepdims=True) + epsilon)
-    unit_one = x * scale_one
-    normed_one = (unit_one * gain_one).astype(bf16)
     angle = angles(positions).reshape(rows, HEAD_DIM // 2)
     cosine, sine = jnp.cos(angle), jnp.sin(angle)
     still = jnp.ones((rows, HEAD_DIM), f32)
     cos_lanes = jnp.concatenate([cosine] * (2 * heads + 2) + [still], 1)
     sin_lanes = jnp.concatenate([-sine, sine] * (heads + 1) + [still * 0.0], 1)
-    shares, qkv_full, output_full, qkv, attn, norms = head(
-        heads, seqs, share_own, qkv_owned, output_weight, normed_one, cos_lanes, sin_lanes,
-        seg_col, seg_row,
-    )
-    hidden = x + dot_nn(attn, output_full.reshape(width, width))
-    scale_two = lax.rsqrt(jnp.mean(hidden * hidden, -1, keepdims=True) + epsilon)
-    normed_two = (hidden * scale_two * gain_two).astype(bf16)
+    small_gains = jnp.stack([attention_gain, mlp_gain]).astype(f32)
+    small_places = jnp.stack([segments, positions]).astype(f32)
+    (
+        shares, qkv_full, output_full, qkv, attn, normed_one, hidden, normed_two,
+        norms, scale_two, gains, places, seg_col, seg_row,
+    ) = head(
+        heads, share_own, qkv_owned, output_weight, tokens.reshape(rows, width), small_gains,
+        small_places, cos_lanes, sin_lanes,
+    )
+    gain_one, gain_two = gains[:, 0].reshape(width), gains[:, 1].reshape(width)
+    spots = jnp.swapaxes(places[:, 1], 0, 1).reshape(seqs, length)
+    angle_all = jnp.swapaxes(angles(spots), 1, 2)
+    cos_all, sin_all = jnp.cos(angle_all), jnp.sin(angle_all)
+
+    x = tokens.reshape(rows, width).astype(f32)
+    scale_one = lax.rsqrt(jnp.mean(x * x, -1, keepdims=True) + epsilon)
+    unit_one = x * scale_one
 
     cot_rows = cotangent.reshape(rows, width)
     normed_all, cot_all, partials, late, outs, mixed, gate, up = feed_forward(

time: 927 us -> 886 us (0.956)
  matrix products: 10.6 us -> 0 us
  blocking collectives: 10.2 us -> 0 us
    pallas_call x1, Pallas kernels: 196 us -> 183 us  [feed_forward(): pl.pallas_call(feed_kernel, in_specs=[hbm] * 5, out_specs=(hbm,) * len(ou...]
    dot_general x1 -> x0, matrix products: 10.6 us -> none  [dot_nn(): lax.dot_general(left, right, (((1,), (0,)), ((), ())), preferred_element_...]
    all_gather x1 -> x0, blocking collectives: 10.2 us -> none  [body(): small = lax.all_gather(small, 'shard')]
  transfers between devices with their start and end apart: 1 -> 1, of which waited for: 0 -> 0; matrix products, arithmetic and copies ran while one was open for 4% -> 2% of each run, Pallas kernels for 21% -> 23%
where the time goes in v6:
time: 886 us; the launch traced here: 879 us
  Pallas kernels  822 us (93%)
  other arithmetic  43.7 us (5%)
  local copies, waits for them, and re-layouts  10.6 us (1%)
    pallas_call x1, Pallas kernels, tail(): pl.pallas_call(functools.partial(tail_kernel, heads), in_specs=[hbm] * 15...  438 us
    pallas_call x1, Pallas kernels, head(): pl.pallas_call(functools.partial(head_kernel, heads), in_specs=[hbm] * 4...  201 us
    pallas_call x1, Pallas kernels, feed_forward(): pl.pallas_call(feed_kernel, in_specs=[hbm] * 5, out_specs=(hbm,) * len(ou...  183 us
  transfers between devices with their start and end apart: 1, of which 0 were waited for; matrix products, arithmetic and copies ran while one was open for 2% of the time, Pallas kernels for 23%

profile of v6, /device:TPU:0, one launch (start us, length us, event | category | flops | bytes accessed | tf_op | source)
XLA Modules:
  0.0 878.6 jit_solution(9570945954669694847)
XLA Ops:
  0.6 0.5 collective-permute-start
  1.2 1.7 fusion.2
  2.9 1.5 copy.39
  4.4 0.3 copy.36
  4.7 0.1 copy.30
  4.9 0.3 copy.32
  5.4 0.3 copy.33
  5.7 0.3 pad_maximum_fusion
  6.0 1.4 copy.37
  7.6 1.0 multiply_sine_fusion.1
  8.6 1.6 concatenate.10.cos_ref
  10.3 1.6 concatenate.11.sin_ref
  11.9 0.6 maximum_convert_fusion.gain_ref
  12.5 0.6 add_convert_fusion.place_ref
  13.1 0.5 multiply_reduce_fusion.1
  13.6 0.6 rsqrt_bitcast_fusion
  14.2 200.6 %shard_map.212 = (bf16[2,4,4,2,64,2048]{5,4,3,2,1,0:T(8,128)(2,1)}, bf16[8,256,3072]{2,1,0:T(8,128)(2,1)}, bf16[8,256,2048]{2,1,0:T(8,128)(2,1)}, bf16[8,4,128,3...) custom-call(bf16[4,2,64,2048]{3,2,1,0:T(8,128)(2,1)} %bitcast.47, ...), custom_call_target="tpu_custom_call" | custom-call | flops 4294967296 | bytes 268435456 | tf_op jit(solution)/shard_map/pallas_call | solution.py:559
  214.8 0.7 slice_bitcast_fusion
  215.5 1.4 fusion.4
  216.9 2.8 multiply_sine_fusion
  219.7 183.4 %shard_map.213 = (bf16[4,512,2048]{2,1,0:T(8,128)(2,1)}, bf16[4,512,2048]{2,1,0:T(8,128)(2,1)}, bf16[3,512,2048]{2,1,0:T(8,128)(2,1)}, bf16[512,2048]{1,0:T(8,12...) custom-call(bf16[512,2048]{1,0:T(8,128)(2,1)} %get-tuple-element.41., ...), custom_call_target="tpu_custom_call" | custom-call | flops 103079215104 | bytes 134217728 | tf_op jit(solution)/shard_map/pallas_call | solution.py:839
  403.2 438.4 %shard_map.214 = (bf16[1024,2048]{1,0:T(8,128)(2,1)}, bf16[2,2048,1024]{2,1,0:T(8,128)(2,1)}, bf16[1024,2048]{1,0:T(8,128)(2,1)}, bf16[2,2048,1024]{2,1,0:T(8,12...) custom-call(bf16[4,512,2048]{2,1,0:T(8,128)(2,1)} %get-tuple-element, ...), custom_call_target="tpu_custom_call" | custom-call | flops 62277025792 | bytes 536870912 | tf_op jit(solution)/shard_map/pallas_call | solution.py:1700
  841.6 4.4 multiply_reduce_fusion.2
  846.0 2.3 add_reduce_fusion.1
  848.3 0.9 multiply_reduce_fusion
  849.3 4.4 convert_element_type.79
  853.7 3.9 convert_reduce_fusion
  857.6 0.8 copy-done.3
  858.4 9.4 %add_reduce_fusion = (f32[256]{0:T(256)S(1)}, f32[256,8192]{1,0:T(8,128)}, f32[256,8192]{1,0:T(8,128)}) fusion(bf16[256,8192]{1,0:T(8,128)(2,1)S(1)} %copy-done.3, bf16[256,8192]{1,0:T(8,128)(2,1)S(1)} %copy-done.2, bf16[256,8192]{1,0:T(8,128)(2,1)} %get-tuple-element.66, bf16[256,8192]{1,0:T(8,128)(2,1)} %get-tuple-element.67), kind=kLoop, calls=%fused_computation.2 | loop fusion | flops 16776960 | bytes 33555456 | tf_op jit(solution)/shard_map/reduce_sum | solution.py:1865
  867.9 5.5 multiply_add_fusion
  873.4 4.2 fusion.1
  877.6 0.6 convert_divide_fusion
  (48 shorter events, 0.4 us)
Async XLA Ops:
  0.6 219.1 %collective-permute-start = (bf16[1024,2048]{1,0:T(8,128)(2,1)}, bf16[1024,2048]{1,0:T(8,128)(2,1)}, u32[]{:S(2)}, u32[]{:S(2)}) collective-permute-start(bf16[1024,2048]{1,0:T(8,128)(2,1)} %down_own_ref.1), channel_id=1, source_target_pairs={{0,1},{1,0},{2,3},{3,2},{4,5},{5,4},{6,7},{7,6},{8,9},{9,8},{10,11... | collective-permute-start | bytes 12582920 | tf_op jit(solution)/shard_map/ppermute | solution.py:1783
  2.8 1.6 copy-start.6
  2.9 1.9 copy-start.10
  2.9 2.3 copy-start.8
  5.2 2.3 copy-start.18
  5.2 2.3 copy-start.16
  5.2 2.3 copy-start.14
  7.6 4.9 copy-start.15
  7.6 5.5 copy-start
  841.5 4.5 copy-start.9
  841.5 4.5 copy-start.11
  841.6 6.8 copy-start.1
  841.6 6.7 copy-start.4
  841.6 6.7 copy-start.12
  841.6 6.7 copy-start.13
  846.0 3.2 copy-start.5
  853.7 3.9 copy-start.2
  853.7 4.7 copy-start.3
  867.9 5.5 copy-start.7
  873.4 4.2 copy-start.17
  873.4 4.2 copy-start.19

commit v7 on v6

--- a/solution.py
+++ b/solution.py
@@ -1066,8 +1066,12 @@
 
             elif c + 1 < last_inner and c + 1 != up_first:
                 take_mine(c + 1).start()
-            if not static or c >= 2:
+            if static and c > last_inner:
+                send_out(c - 1)
+            elif not static or c >= 2:
                 send_out(c - 2)
+            if static and c == last_inner:
+                send_out(c - 1)
 
     lead = 3
     position = [0]
@@ -1604,7 +1608,6 @@
 
             @pl.when(is_inner)
             def _():
-                send_out(chunks - 2)
                 send_out(chunks - 1)
 
         for s in range(seqs):

time: 886 us -> 886 us (level)
  no operation moved by 1% of the time
where the time goes in v7:
time: 886 us; the launch traced here: 879 us
  Pallas kernels  822 us (93%)
  other arithmetic  43.7 us (5%)
  local copies, waits for them, and re-layouts  10.6 us (1%)
    pallas_call x1, Pallas kernels, tail(): pl.pallas_call(functools.partial(tail_kernel, heads), in_specs=[hbm] * 15...  438 us
    pallas_call x1, Pallas kernels, head(): pl.pallas_call(functools.partial(head_kernel, heads), in_specs=[hbm] * 4...  201 us
    pallas_call x1, Pallas kernels, feed_forward(): pl.pallas_call(feed_kernel, in_specs=[hbm] * 5, out_specs=(hbm,) * len(ou...  183 us
  transfers between devices with their start and end apart: 1, of which 0 were waited for; matrix products, arithmetic and copies ran while one was open for 2% of the time, Pallas kernels for 23%

profile of v7, /device:TPU:0, one launch (start us, length us, event | category | flops | bytes accessed | tf_op | source)
XLA Modules:
  0.0 878.6 jit_solution(17097539117331595322)
XLA Ops:
  0.6 0.5 collective-permute-start
  1.2 1.7 fusion.2
  2.9 1.5 copy.39
  4.4 0.3 copy.36
  4.7 0.1 copy.30
  4.9 0.3 copy.32
  5.4 0.3 copy.33
  5.7 0.3 pad_maximum_fusion
  6.0 1.4 copy.37
  7.6 1.0 multiply_sine_fusion.1
  8.6 1.6 concatenate.10.cos_ref
  10.3 1.6 concatenate.11.sin_ref
  11.9 0.6 maximum_convert_fusion.gain_ref
  12.5 0.6 add_convert_fusion.place_ref
  13.1 0.5 multiply_reduce_fusion.1
  13.6 0.6 rsqrt_bitcast_fusion
  14.2 200.6 %shard_map.212 = (bf16[2,4,4,2,64,2048]{5,4,3,2,1,0:T(8,128)(2,1)}, bf16[8,256,3072]{2,1,0:T(8,128)(2,1)}, bf16[8,256,2048]{2,1,0:T(8,128)(2,1)}, bf16[8,4,128,3...) custom-call(bf16[4,2,64,2048]{3,2,1,0:T(8,128)(2,1)} %bitcast.47, ...), custom_call_target="tpu_custom_call" | custom-call | flops 4294967296 | bytes 268435456 | tf_op jit(solution)/shard_map/pallas_call | solution.py:559
  214.8 0.7 slice_bitcast_fusion
  215.5 1.4 fusion.4
  216.9 2.8 multiply_sine_fusion
  219.7 183.4 %shard_map.213 = (bf16[4,512,2048]{2,1,0:T(8,128)(2,1)}, bf16[4,512,2048]{2,1,0:T(8,128)(2,1)}, bf16[3,512,2048]{2,1,0:T(8,128)(2,1)}, bf16[512,2048]{1,0:T(8,12...) custom-call(bf16[512,2048]{1,0:T(8,128)(2,1)} %get-tuple-element.41., ...), custom_call_target="tpu_custom_call" | custom-call | flops 103079215104 | bytes 134217728 | tf_op jit(solution)/shard_map/pallas_call | solution.py:839
  403.2 438.4 %shard_map.214 = (bf16[1024,2048]{1,0:T(8,128)(2,1)}, bf16[2,2048,1024]{2,1,0:T(8,128)(2,1)}, bf16[1024,2048]{1,0:T(8,128)(2,1)}, bf16[2,2048,1024]{2,1,0:T(8,12...) custom-call(bf16[4,512,2048]{2,1,0:T(8,128)(2,1)} %get-tuple-element, ...), custom_call_target="tpu_custom_call" | custom-call | flops 62277025792 | bytes 536870912 | tf_op jit(solution)/shard_map/pallas_call | solution.py:1703
  841.6 4.4 multiply_reduce_fusion.2
  846.0 2.3 add_reduce_fusion.1
  848.3 0.9 multiply_reduce_fusion
  849.3 4.4 convert_element_type.79
  853.7 3.9 convert_reduce_fusion
  857.6 0.8 copy-done.3
  858.4 9.4 %add_reduce_fusion = (f32[256]{0:T(256)S(1)}, f32[256,8192]{1,0:T(8,128)}, f32[256,8192]{1,0:T(8,128)}) fusion(bf16[256,8192]{1,0:T(8,128)(2,1)S(1)} %copy-done.3, bf16[256,8192]{1,0:T(8,128)(2,1)S(1)} %copy-done.2, bf16[256,8192]{1,0:T(8,128)(2,1)} %get-tuple-element.66, bf16[256,8192]{1,0:T(8,128)(2,1)} %get-tuple-element.67), kind=kLoop, calls=%fused_computation.2 | loop fusion | flops 16776960 | bytes 33555456 | tf_op jit(solution)/shard_map/reduce_sum | solution.py:1868
  867.9 5.5 multiply_add_fusion
  873.4 4.2 fusion.1
  877.6 0.6 convert_divide_fusion
  (48 shorter events, 0.4 us)
Async XLA Ops:
  0.6 219.1 %collective-permute-start = (bf16[1024,2048]{1,0:T(8,128)(2,1)}, bf16[1024,2048]{1,0:T(8,128)(2,1)}, u32[]{:S(2)}, u32[]{:S(2)}) collective-permute-start(bf16[1024,2048]{1,0:T(8,128)(2,1)} %down_own_ref.1), channel_id=1, source_target_pairs={{0,1},{1,0},{2,3},{3,2},{4,5},{5,4},{6,7},{7,6},{8,9},{9,8},{10,11... | collective-permute-start | bytes 12582920 | tf_op jit(solution)/shard_map/ppermute | solution.py:1786
  2.8 1.6 copy-start.6
  2.9 1.9 copy-start.10
  2.9 2.3 copy-start.8
  5.2 2.3 copy-start.18
  5.2 2.3 copy-start.16
  5.2 2.3 copy-start.14
  7.6 4.9 copy-start.15
  7.6 5.5 copy-start
  841.5 4.5 copy-start.9
  841.5 4.5 copy-start.11
  841.6 6.8 copy-start.1
  841.6 6.7 copy-start.4
  841.6 6.7 copy-start.12
  841.6 6.7 copy-start.13
  846.0 3.2 copy-start.5
  853.7 3.9 copy-start.2
  853.7 4.7 copy-start.3
  867.9 5.5 copy-start.7
  873.4 4.2 copy-start.17
  873.4 4.2 copy-start.19
